TPU v7x, 32 devices: a whole 2x2x4 slice. The times are simulated.
32 devices in a mesh: pairs: 8 (over z, y), orb: 4 (over x, core).
Axes of the slice: x: 2, y: 2, z: 4, core: 2. Of those that a mesh axis runs over, the one named last changes fastest.
Arguments:
- amplitudes: float32 [128, 128, 128], P(('pairs', 'orb')), may hold values from -4 to 4
- integrals: bfloat16 [128, 128, 128], P(('pairs', 'orb')), may hold values from -6 to 6
- energies: float32 [128, 128], P(('pairs', 'orb')), may hold values from 0.5 to 4
- intersections: bfloat16 [128, 16, 128, 128], P(('pairs', 'orb')), may hold values from -0.5 to 0.5
- couplings: float32 [128, 16], P(('pairs', 'orb')), may hold values from -2 to 2
- projector: float32 [128, 128], P(('pairs', 'orb')), may hold values from -0.5 to 0.5
- pair_orbitals: int32 [128, 2], P(('pairs', 'orb')), may hold values from 0 to 3
- coupled: int32 [128, 16], replicated, may hold values from 0 to 127, as said below
- pair_slot: int32 [128], replicated, may hold values from 0 to 127, as said below
Outputs:
- final_amplitudes: float32 [128, 128, 128], P(('pairs', 'orb'))
- residual: float32 [128, 128, 128], P(('pairs', 'orb'))
Inputs may be any that keep to these rules, and one draw needn't show every extreme that they name: `coupled`: each row holds 16 different pair ids, never the id of the pair held in that row's slot. The rows of one device name at most 3 different pairs held by the devices of any one pairs index, and exactly 3 held by the devices of the next pairs index. `pair_slot`: A permutation of the pair ids.
All inputs are finite; a program needn't handle non-finite values.
Results may differ from a plain program's by a relative error of at most 0.00037.
Values may be sent and summed in bfloat16 or wider, within the bound.
No kernel may reach another device: no remote copies, remote signals or barrier semaphores. Data moves between devices by JAX's collectives and lax.ppermute only.
A program may use at most 64 MiB of HBM per device.

v0:
```python
import jax
import jax.numpy as jnp
from jax import lax
from jax.sharding import PartitionSpec as P

PAIRS_ORB = 32
ITERS = 2


def body(
    amplitudes,
    integrals,
    energies,
    intersections,
    couplings,
    projector,
    pair_orbitals,
    coupled,
    pair_slot,
):
    highest = lax.Precision.HIGHEST
    pair_count = lax.axis_size("pairs")
    orb_count = lax.axis_size("orb")
    devices = pair_count * orb_count
    per_device = amplitudes.shape[0]
    width = amplitudes.shape[1]
    total = coupled.shape[0]
    capacity = 1 + coupled.shape[1] // pair_count
    group = orb_count * per_device
    orbitals = total // PAIRS_ORB
    pair_idx = lax.axis_index("pairs")
    orb_idx = lax.axis_index("orb")
    device_id = pair_idx * orb_count + orb_idx
    targets = pair_slot[coupled]
    row_owner = jnp.broadcast_to(
        (jnp.arange(total, dtype=jnp.int32) // per_device)[:, None], targets.shape
    )
    needed = jnp.zeros((devices, total), jnp.int32).at[row_owner, targets].set(1)
    mine = lax.dynamic_slice_in_dim(needed, device_id, 1, 0)[0].reshape(pair_count, group)
    ranks = (jnp.cumsum(mine, axis=1) - 1).reshape(total)
    own_targets = lax.dynamic_slice_in_dim(targets, device_id * per_device, per_device, 0)
    slot_ids = jnp.arange(capacity, dtype=jnp.int32)
    group_cols = lax.dynamic_slice_in_dim(needed, pair_idx * group, group, 1)
    group_rank = jnp.cumsum(group_cols, axis=1) - 1
    entry_pos = own_targets // group * capacity + ranks[own_targets]
    dest_cols = group_cols.reshape(pair_count, orb_count, group)
    dest_cols = lax.dynamic_slice_in_dim(dest_cols, orb_idx, 1, 1)[:, 0]
    dest_rank = group_rank.reshape(pair_count, orb_count, group)
    dest_rank = lax.dynamic_slice_in_dim(dest_rank, orb_idx, 1, 1)[:, 0]
    select = (
        (dest_cols == 1)[:, None, :] & (dest_rank[:, None, :] == slot_ids[None, :, None])
    ).astype(jnp.bfloat16)
    orbital_ids = jnp.arange(orbitals, dtype=jnp.int32)
    first_hot = (pair_orbitals[:, 0:1] == orbital_ids[None, :]).astype(jnp.float32)
    second_hot = (pair_orbitals[:, 1:2] == orbital_ids[None, :]).astype(jnp.float32)
    denom = energies[:, :, None] + energies[:, None, :]
    state = amplitudes
    residual = amplitudes
    for step in range(ITERS):
        blocks = state.astype(jnp.bfloat16)
        group_blocks = lax.all_gather(blocks, "orb", axis=0, tiled=True)
        outgoing = jnp.einsum(
            "pcj,jxy->pcxy", select, group_blocks, preferred_element_type=jnp.float32
        )
        outgoing = outgoing.astype(jnp.bfloat16)
        arrived = lax.all_to_all(outgoing, "pairs", split_axis=0, concat_axis=0, tiled=True)
        arrived = arrived.reshape(pair_count * capacity, width, width)
        fetched = arrived[entry_pos]
        lifted = jnp.einsum(
            "pkab,pkbc->pkac", intersections, fetched, preferred_element_type=jnp.float32
        )
        scaled = (couplings[:, :, None, None] * lifted).astype(jnp.bfloat16)
        coupling = jnp.einsum(
            "pkac,pkdc->pad", scaled, intersections, preferred_element_type=jnp.float32
        )
        projected = jnp.einsum("pab,pb->pa", state, projector, precision=highest)
        partial_sum = jnp.dot(first_hot.T, projected, precision=highest) + jnp.dot(
            second_hot.T, projected, precision=highest
        )
        summed = lax.psum(partial_sum, ("pairs", "orb"))
        left = jnp.dot(first_hot, summed, precision=highest)
        right = jnp.dot(second_hot, summed, precision=highest)
        residual = (
            integrals.astype(jnp.float32)
            + energies[:, :, None] * state
            + state * energies[:, None, :]
            - coupling
            + left[:, :, None] * projector[:, None, :]
            + projector[:, :, None] * right[:, None, :]
        )
        state = state - residual / denom
    return (state, residual)


def solution(mesh):
    return jax.shard_map(
        body,
        mesh=mesh,
        in_specs=(
            P(("pairs", "orb"), None, None),
            P(("pairs", "orb"), None, None),
            P(("pairs", "orb"), None),
            P(("pairs", "orb"), None, None, None),
            P(("pairs", "orb"), None),
            P(("pairs", "orb"), None),
            P(("pairs", "orb"), None),
            P(),
            P(),
        ),
        out_specs=(P(("pairs", "orb"), None, None), P(("pairs", "orb"), None, None)),
        check_vma=False,
    )
```

profile of v0, /device:TPU:0, one launch (start us, length us, event | category | flops | bytes accessed | tf_op | source)
XLA Modules:
  0.0 154.1 jit_solution(16488326164033136478)
XLA Ops:
  0.7 0.8 compare_select_fusion.1
  1.8 12.6 %gather_fusion = s32[2048]{0:T(1024)S(1)} fusion(s32[128]{0:T(128)S(1)} %copy-done.1, s32[2048]{0:T(1024)S(1)} %broadcast_clamp_fusion), kind=kCustom, calls=%fused_computation | custom fusion | bytes 24576 | tf_op jit(solution)/shard_map/gather | solution.py:34
  14.9 8.1 %scatter_custom_fusion = s32[4096]{0:T(1024)S(1)} fusion(s32[2048]{0:T(1024)S(1)} %reshape.158, s32[2048]{0:T(1024)S(1)} %broadcast.186, s32[]{:T(128)} %constant.52.clone.1), kind=kCustom, calls=%fused_computation.43 | custom fusion | bytes 16388
  23.1 0.7 reduce_window_sum.22
  23.8 8.6 %all_gather.6 = bf16[16,128,128]{2,1,0:T(8,128)(2,1)S(1)} all-gather(bf16[4,128,128]{2,1,0:T(8,128)(2,1)S(1)} %convert_element_type.32), channel_id=1, replica_groups=mesh['pairs'=8,'orb'=4] {'orb'}, dimensions={0}, use_global_device_ids=true | all-gather | bytes 655360 | tf_op jit(solution)/shard_map/all_gather | solution.py:61
  32.5 0.4 convolution_convert_fusion.1
  32.9 1.1 copy.45
  33.9 6.0 %all-to-all-start = ((bf16[8,3,128,128]{3,2,1,0:T(8,128)(2,1)}), bf16[8,3,128,128]{3,2,1,0:T(8,128)(2,1)S(1)}, u32[]{:S(2)}, u32[]{:S(2)}) async-start(bf16[8,3,128,128]{3,2,1,0:T(8,128)(2,1)} %copy.45), calls=%async_computation | async-start | bytes 1572864 | tf_op jit(solution)/shard_map/all_to_all | solution.py:66
  40.5 0.8 gather_fusion.1
  41.5 0.5 fusion.72
  42.0 0.3 fusion.60
  42.2 0.3 convolution_add_fusion.1
  42.5 42.0 %psum.14 = f32[4,128]{1,0:T(4,128)S(1)} all-reduce(f32[4,128]{1,0:T(4,128)S(1)} %convolution_add_fusion.1), channel_id=1, replica_groups=mesh['pairs'=8,'orb'=4] {'pairs','orb'}, use_global_device_ids=true, to_apply=%region_3.4 | all-reduce | flops 512 | bytes 4096 | tf_op jit(solution)/shard_map/psum | solution.py:80
  84.9 2.2 %gather_fusion.2 = bf16[64,128,128]{2,1,0:T(8,128)(2,1)} fusion(bf16[24,128,128]{2,1,0:T(8,128)(2,1)S(1)} %bitcast.104, s32[1024]{0:T(1024)S(1)} %pad_clamp_fusion), kind=kCustom, calls=%fused_computation.2 | custom fusion | bytes 4194560 | tf_op jit(solution)/shard_map/gather | solution.py:68
  87.1 3.8 %fusion.71 = (bf16[4,128,128]{2,1,0:T(8,128)(2,1)S(1)}, f32[4,128,128]{2,1,0:T(8,128)S(1)}) fusion(f32[4,128,128]{2,1,0:T(8,128)S(1)} %copy-done.2, f32[4,128]{1,0:T(4,128)S(1)} %fusion.56, f32[4,128]{1,0:T(4,128)S(1)} %copy-done.3, f32[4,128]{1,0:T(4,128)S(1)} %fusion.59, bf16[4,16,128,128]{3,2,1,0:T(8,128)(2,1)S(1)} %copy-done, ...), kind=kOutput, calls=%fused_computation.97 | convolution fusion | flops 539885568 | bytes 4989184 | tf_op jit(solution)/shard_map/pkac,pkdc->pad/dot_general | solution.py:73
  90.9 8.0 %all_gather.7 = bf16[16,128,128]{2,1,0:T(8,128)(2,1)S(1)} all-gather(bf16[4,128,128]{2,1,0:T(8,128)(2,1)S(1)} %get-tuple-element.4), channel_id=1, replica_groups=mesh['pairs'=8,'orb'=4] {'orb'}, dimensions={0}, use_global_device_ids=true | all-gather | bytes 655360 | tf_op jit(solution)/shard_map/all_gather | solution.py:61
  98.8 0.4 convolution_convert_fusion
  99.3 1.1 copy.49
  100.3 3.5 %all-to-all-start.1 = ((bf16[8,3,128,128]{3,2,1,0:T(8,128)(2,1)}), bf16[8,3,128,128]{3,2,1,0:T(8,128)(2,1)S(1)}, u32[]{:S(2)}, u32[]{:S(2)}) async-start(bf16[8,3,128,128]{3,2,1,0:T(8,128)(2,1)} %copy.49), calls=%async_computation.1 | async-start | bytes 1572864 | tf_op jit(solution)/shard_map/all_to_all | solution.py:66
  103.9 0.5 fusion.73
  104.6 0.3 convolution_add_fusion
  104.9 42.0 %psum.15 = f32[4,128]{1,0:T(4,128)S(1)} all-reduce(f32[4,128]{1,0:T(4,128)S(1)} %convolution_add_fusion), channel_id=1, replica_groups=mesh['pairs'=8,'orb'=4] {'pairs','orb'}, use_global_device_ids=true, to_apply=%region_4.5 | all-reduce | flops 512 | bytes 4096 | tf_op jit(solution)/shard_map/psum | solution.py:80
  147.3 2.2 %gather_fusion.3 = bf16[64,128,128]{2,1,0:T(8,128)(2,1)} fusion(bf16[24,128,128]{2,1,0:T(8,128)(2,1)S(1)} %bitcast.105, s32[1024]{0:T(1024)S(1)} %pad_clamp_fusion), kind=kCustom, calls=%fused_computation.3 | custom fusion | bytes 4194560 | tf_op jit(solution)/shard_map/gather | solution.py:68
  149.5 4.6 %fusion.40 = (f32[4,128,128]{2,1,0:T(8,128)}, f32[4,128,128]{2,1,0:T(8,128)}) fusion(f32[4,128,128]{2,1,0:T(8,128)S(1)} %get-tuple-element.5, f32[4,128]{1,0:T(4,128)S(1)} %copy-done.9, f32[4,128]{1,0:T(4,128)S(1)} %fusion.55, f32[4,128]{1,0:T(4,128)S(1)} %copy-done.3, f32[4,128]{1,0:T(4,128)S(1)} %fusion.57, bf16[4,16,128,128]{3,2,1,0:T(8,128)(2,1)S(1)} %copy-done, ...), kind=kOutput, calls=%fused_computation.34 | convolution fusion | flops 539820032 | bytes 5120256 | tf_op jit(solution)/shard_map/pkac,pkdc->pad/dot_general | solution.py:73
  (62 shorter events, 2.6 us)
Async XLA Ops:
  0.6 86.4 %copy-start = (bf16[4,16,128,128]{3,2,1,0:T(8,128)(2,1)S(1)}, bf16[4,16,128,128]{3,2,1,0:T(8,128)(2,1)}, u32[]{:S(2)}) copy-start(bf16[4,16,128,128]{3,2,1,0:T(8,128)(2,1)} %param.12) | copy-start | bytes 6291460
  0.6 1.1 copy-start.1
  1.7 12.8 %copy-start.6 = (s32[2]{0:T(128)S(1)}, s32[2]{0:T(128)}, u32[]{:S(2)}) copy-start(s32[2]{0:T(128)} %constant.73) | copy-start | bytes 28
  1.7 12.9 %copy-start.5 = (s32[2]{0:T(128)S(1)}, s32[2]{0:T(128)}, u32[]{:S(2)}) copy-start(s32[2]{0:T(128)} %constant.76) | copy-start | bytes 28
  1.8 22.0 %copy-start.2 = (f32[4,128,128]{2,1,0:T(8,128)S(1)}, f32[4,128,128]{2,1,0:T(8,128)}, u32[]{:S(2)}) copy-start(f32[4,128,128]{2,1,0:T(8,128)} %param.9) | copy-start | bytes 786436
  33.9 7.5 %copy-start.4 = (s32[4,2]{0,1:T(2,128)S(1)}, s32[4,2]{0,1:T(2,128)}, u32[]{:S(2)}) copy-start(s32[4,2]{0,1:T(2,128)} %param.15) | copy-start | bytes 100
  33.9 7.5 %copy-start.3 = (f32[4,128]{1,0:T(4,128)S(1)}, f32[4,128]{1,0:T(4,128)}, u32[]{:S(2)}) copy-start(f32[4,128]{1,0:T(4,128)} %param.14) | copy-start | bytes 6148
  33.9 50.9 %all-to-all-start = ((bf16[8,3,128,128]{3,2,1,0:T(8,128)(2,1)}), bf16[8,3,128,128]{3,2,1,0:T(8,128)(2,1)S(1)}, u32[]{:S(2)}, u32[]{:S(2)}) async-start(bf16[8,3,128,128]{3,2,1,0:T(8,128)(2,1)} %copy.45), calls=%async_computation | async-start | bytes 1572864 | tf_op jit(solution)/shard_map/all_to_all | solution.py:66
  84.9 2.2 %copy-start.8 = (f32[4,16]{1,0:T(4,128)S(1)}, f32[4,16]{1,0:T(4,128)}, u32[]{:S(2)}) copy-start(f32[4,16]{1,0:T(4,128)} %param.13) | copy-start | bytes 772
  84.9 2.2 %copy-start.9 = (f32[4,128]{1,0:T(4,128)S(1)}, f32[4,128]{1,0:T(4,128)}, u32[]{:S(2)}) copy-start(f32[4,128]{1,0:T(4,128)} %param.11) | copy-start | bytes 6148
  100.3 47.0 %all-to-all-start.1 = ((bf16[8,3,128,128]{3,2,1,0:T(8,128)(2,1)}), bf16[8,3,128,128]{3,2,1,0:T(8,128)(2,1)S(1)}, u32[]{:S(2)}, u32[]{:S(2)}) async-start(bf16[8,3,128,128]{3,2,1,0:T(8,128)(2,1)} %copy.49), calls=%async_computation.1 | async-start | bytes 1572864 | tf_op jit(solution)/shard_map/all_to_all | solution.py:66
  147.3 2.2 %copy-start.7 = (bf16[4,128,128]{2,1,0:T(8,128)(2,1)S(1)}, bf16[4,128,128]{2,1,0:T(8,128)(2,1)}, u32[]{:S(2)}) copy-start(bf16[4,128,128]{2,1,0:T(8,128)(2,1)} %param.10) | copy-start | bytes 393220
where the time goes:
time: 155 us; the launch traced here: 154 us
  blocking collectives  101 us (65%)
  local copies, waits for them, and re-layouts  29.1 us (19%)
  matrix products  12 us (8%)
  starting transfers between devices  9.51 us (6%)
  other arithmetic  1.98 us (1%)
    psum x2, blocking collectives, body(): summed = lax.psum(partial_sum, ('pairs', 'orb'))  84 us
    all_gather x2, blocking collectives, body(): group_blocks = lax.all_gather(blocks, 'orb', axis=0, tiled=True)  16.6 us
    gather x3, local copies, waits for them, and re-layouts, body(): targets = pair_slot[coupled]  12.8 us
    all_to_all x2, starting transfers between devices, body(): lax.all_to_all(outgoing, 'pairs', split_axis=0, concat_axis=0, tiled=True)  9.51 us
    dot_general x2, matrix products, body(): jnp.einsum('pkac,pkdc->pad', scaled, intersections, preferred_element_typ...  8.4 us
    unnamed x25, local copies, waits for them, and re-layouts  8.32 us
    gather x2, local copies, waits for them, and re-layouts, body(): fetched = arrived[entry_pos]  4.35 us
  transfers between devices with their start and end apart: 2, of which 0 were waited for; matrix products, arithmetic and copies ran while one was open for 3% of the time, Pallas kernels for 0%

commit v1 on v0

v1 whole, which is shorter than its diff:
```python
import functools

import jax
import jax.numpy as jnp
from jax import lax
from jax.experimental import pallas as pl
from jax.experimental.pallas import tpu as pltpu
from jax.sharding import PartitionSpec as P

PAIRS_ORB = 32
ITERS = 2
ROWS = 16
PARTS = 3

F32 = jnp.float32
BF16 = jnp.bfloat16
VMEM = pl.BlockSpec(memory_space=pltpu.VMEM)
SMEM = pl.BlockSpec(memory_space=pltpu.SMEM)
ANY = pl.BlockSpec(memory_space=pl.ANY)
LIMIT = 40 * 1024 * 1024


def eye_mask(width):
    rows = lax.broadcasted_iota(jnp.int32, (width, width), 0)
    cols = lax.broadcasted_iota(jnp.int32, (width, width), 1)
    return rows == cols


def to_row(column, eye):
    return jnp.sum(jnp.where(eye, column, 0.0), axis=0, keepdims=True)


def to_column(row, eye):
    return jnp.sum(jnp.where(eye, row, 0.0), axis=1, keepdims=True)


def split_parts(value):
    parts = []
    for _ in range(PARTS):
        part = value.astype(BF16)
        parts.append(part)
        value = value - part.astype(F32)
    return parts


def tail_rows(value, rows):
    parts = split_parts(value)
    missing = rows - sum(part.shape[0] for part in parts)
    if missing:
        parts.append(jnp.zeros((missing, value.shape[1]), BF16))
    return jnp.concatenate([part.astype(F32) for part in parts], axis=0).astype(BF16)


def join_parts(rows, orbitals):
    rows = rows.astype(F32)
    value = rows[:orbitals]
    for part in range(1, PARTS):
        value = value + rows[part * orbitals : (part + 1) * orbitals]
    return value


def singles_terms(state, projector_row, orbital_a, orbital_b, orbitals, eye):
    projected = to_row(jnp.sum(state * projector_row, axis=1, keepdims=True), eye)
    ids = lax.broadcasted_iota(jnp.int32, (orbitals, 1), 0)
    count = (ids == orbital_a).astype(F32) + (ids == orbital_b).astype(F32)
    return count * projected


def setup_kernel(
    capacity, group, stride, orbitals,
    position, ends, state, projector, dest_rows, own_row, slot_row, slot_col,
    payload, send_index, entry_row,
):
    per_device, width = state.shape[0], state.shape[1]
    eye = eye_mask(width)
    total = jnp.zeros((orbitals, width), F32)
    for s in range(per_device):
        block = state[s]
        payload[pl.ds(s * width, width), :] = block.astype(BF16)
        total += singles_terms(block, projector[pl.ds(s, 1), :], ends[s, 0], ends[s, 1], orbitals, eye)
    payload[pl.ds(per_device * width, payload.shape[0] - per_device * width), :] = tail_rows(
        total, payload.shape[0] - per_device * width
    )

    count = slot_row.shape[1]
    pair_idx = position[0]
    slots = slot_row[...]
    lanes = lax.broadcasted_iota(jnp.int32, (1, count), 1)
    wanted = dest_rows[...]
    run = jnp.zeros((wanted.shape[0], 1), jnp.int32)
    picked = [jnp.zeros((wanted.shape[0], 1), jnp.int32) for _ in range(capacity)]
    for g in range(group):
        pair = jnp.sum(jnp.where(slots == pair_idx * group + g, lanes, 0), axis=1, keepdims=True)
        hit = jnp.max((wanted == pair).astype(jnp.int32), axis=1, keepdims=True)
        for c in range(capacity):
            picked[c] = picked[c] + jnp.where((hit == 1) & (run == c), g, 0)
        run = run + hit
    column = lax.broadcasted_iota(jnp.int32, send_index.shape, 1)
    index = jnp.zeros(send_index.shape, jnp.int32)
    for c in range(capacity):
        index = jnp.where(column == c, picked[c], index)
    send_index[...] = index

    own = own_row[...]
    ids = lax.broadcasted_iota(jnp.int32, (count, own.shape[1]), 0)
    entry = (ids == own).astype(F32)
    mine = jnp.max(entry, axis=1, keepdims=True)
    slots_c = slot_col[...]
    before = (slots_c // group == slots // group) & (slots_c < slots)
    rank = jnp.sum(jnp.where(before, mine, 0.0), axis=0, keepdims=True)
    place = (slots // group).astype(F32) * (stride // ROWS) + rank * (width // ROWS)
    found = jnp.dot(place, entry, precision=lax.Precision.HIGHEST, preferred_element_type=F32)
    entry_row[...] = found.astype(jnp.int32) * ROWS


def select_kernel(capacity, per_device, orbitals, width, send_index, gathered, outgoing):
    blocks = per_device * width
    tail = gathered.shape[1] - blocks
    total = join_parts(gathered[0, pl.ds(blocks, tail), :], orbitals)
    for d in range(1, gathered.shape[0]):
        total += join_parts(gathered[d, pl.ds(blocks, tail), :], orbitals)
    rows = tail_rows(total, tail)
    for p in range(outgoing.shape[0]):
        for c in range(capacity):
            j = send_index[p, c]
            first = pl.multiple_of((j % per_device) * width, ROWS)
            outgoing[p, pl.ds(c * width, width), :] = gathered[j // per_device, pl.ds(first, width), :]
        outgoing[p, pl.ds(capacity * width, tail), :] = rows


def update_kernel(
    last, capacity, orbitals,
    entry_row, couplings, ends, arrived, intersections, state, integrals, energies, projector,
    out_a, out_b, held, sems,
):
    per_device, count, width = intersections.shape[0], intersections.shape[1], intersections.shape[2]
    stride = capacity * width + tail_size(orbitals)
    copies = [
        pltpu.make_async_copy(intersections.at[s], held.at[s], sems.at[s]) for s in range(per_device)
    ]
    for copy in copies:
        copy.start()
    eye = eye_mask(width)
    singles = None
    for p in range(arrived.shape[0] // stride):
        part = join_parts(
            arrived[pl.ds(p * stride + capacity * width, stride - capacity * width), :], orbitals
        )
        singles = part if singles is None else singles + part
    ids = lax.broadcasted_iota(jnp.int32, (orbitals, 1), 0)
    total = jnp.zeros((orbitals, width), F32)
    for s in range(per_device):
        copies[s].wait()
        coupling = jnp.zeros((width, width), F32)
        for k in range(0, count, 2):
            wide = jnp.concatenate([held[s, k], held[s, k + 1]], axis=1)
            scaled = []
            for m in (k, k + 1):
                first = pl.multiple_of(entry_row[0, s * count + m], ROWS)
                near = arrived[pl.ds(first, width), :]
                lifted = jnp.dot(held[s, m], near, preferred_element_type=F32)
                scaled.append((couplings[s, m] * lifted).astype(BF16))
            coupling += lax.dot_general(
                jnp.concatenate(scaled, axis=1), wide, (((1,), (1,)), ((), ())),
                preferred_element_type=F32,
            )
        old = state[s]
        energy = energies[pl.ds(s, 1), :]
        energy_c = to_column(energy, eye)
        proj = projector[pl.ds(s, 1), :]
        proj_c = to_column(proj, eye)
        left = jnp.sum(jnp.where(ids == ends[s, 0], singles, 0.0), axis=0, keepdims=True)
        right = jnp.sum(jnp.where(ids == ends[s, 1], singles, 0.0), axis=0, keepdims=True)
        residual = (
            integrals[s].astype(F32) + energy_c * old + old * energy - coupling
            + to_column(left, eye) * proj + proj_c * right
        )
        new = old - residual / (energy_c + energy)
        if last:
            out_a[s] = new
            out_b[s] = residual
        else:
            out_a[s] = new
            out_b[pl.ds(s * width, width), :] = new.astype(BF16)
            total += singles_terms(new, proj, ends[s, 0], ends[s, 1], orbitals, eye)
    if not last:
        tail = out_b.shape[0] - per_device * width
        out_b[pl.ds(per_device * width, tail), :] = tail_rows(total, tail)


def tail_size(orbitals):
    return -(-PARTS * orbitals // ROWS) * ROWS


def body(
    amplitudes, integrals, energies, intersections, couplings, projector, pair_orbitals, coupled, pair_slot,
):
    pair_count = lax.axis_size("pairs")
    orb_count = lax.axis_size("orb")
    per_device, width = amplitudes.shape[0], amplitudes.shape[1]
    total, near = coupled.shape
    capacity = 1 + near // pair_count
    group = orb_count * per_device
    orbitals = total // PAIRS_ORB
    tail = tail_size(orbitals)
    stride = capacity * width + tail
    pair_idx = lax.axis_index("pairs")
    orb_idx = lax.axis_index("orb")
    params = pltpu.CompilerParams(vmem_limit_bytes=LIMIT)

    by_device = coupled.reshape(pair_count, orb_count, per_device * near)
    dest_rows = lax.dynamic_index_in_dim(by_device, orb_idx, 1, keepdims=False)
    own_row = lax.dynamic_slice_in_dim(dest_rows, pair_idx, 1, 0)
    position = pair_idx.reshape(1).astype(jnp.int32)
    payload, send_index, entry_row = pl.pallas_call(
        functools.partial(setup_kernel, capacity, group, stride, orbitals),
        out_shape=(
            jax.ShapeDtypeStruct((per_device * width + tail, width), BF16),
            jax.ShapeDtypeStruct((pair_count, 128), jnp.int32),
            jax.ShapeDtypeStruct((1, per_device * near), jnp.int32),
        ),
        in_specs=[SMEM, SMEM, VMEM, VMEM, VMEM, VMEM, VMEM, VMEM],
        out_specs=(VMEM, VMEM, VMEM),
        compiler_params=params,
        name="setup",
    )(
        position, pair_orbitals, amplitudes, projector, dest_rows, own_row,
        pair_slot.reshape(1, total), pair_slot.reshape(total, 1),
    )
    state = amplitudes
    for step in range(ITERS):
        last = step == ITERS - 1
        gathered = lax.all_gather(payload, "orb", axis=0, tiled=False)
        outgoing = pl.pallas_call(
            functools.partial(select_kernel, capacity, per_device, orbitals, width),
            out_shape=jax.ShapeDtypeStruct((pair_count, stride, width), BF16),
            in_specs=[SMEM, VMEM],
            out_specs=VMEM,
            compiler_params=params,
            name="select",
        )(send_index, gathered)
        arrived = lax.all_to_all(outgoing, "pairs", split_axis=0, concat_axis=0, tiled=True)
        arrived = arrived.reshape(pair_count * stride, width)
        second = (
            jax.ShapeDtypeStruct(amplitudes.shape, F32)
            if last
            else jax.ShapeDtypeStruct((per_device * width + tail, width), BF16)
        )
        state, payload = pl.pallas_call(
            functools.partial(update_kernel, last, capacity, orbitals),
            out_shape=(jax.ShapeDtypeStruct(amplitudes.shape, F32), second),
            in_specs=[SMEM, SMEM, SMEM, VMEM, ANY, VMEM, VMEM, VMEM, VMEM],
            out_specs=(VMEM, VMEM),
            scratch_shapes=[
                pltpu.VMEM(intersections.shape, BF16),
                pltpu.SemaphoreType.DMA((per_device,)),
            ],
            compiler_params=params,
            name="update",
        )(entry_row, couplings, pair_orbitals, arrived, intersections, state, integrals, energies, projector)
    return state, payload


def solution(mesh):
    split = ("pairs", "orb")
    return jax.shard_map(
        body,
        mesh=mesh,
        in_specs=(
            P(split, None, None),
            P(split, None, None),
            P(split, None),
            P(split, None, None, None),
            P(split, None),
            P(split, None),
            P(split, None),
            P(),
            P(),
        ),
        out_specs=(P(split, None, None), P(split, None, None)),
        check_vma=False,
    )
```

time: 155 us -> 84.2 us (0.54)
  blocking collectives: 101 us -> 68.1 us
  local copies, waits for them, and re-layouts: 29.1 us -> 4.9 us
  matrix products: 12 us -> 0 us
  Pallas kernels: 0 us -> 10.1 us
  starting transfers between devices: 9.51 us -> 0 us
  other arithmetic: 1.98 us -> 0 us
    psum x2 -> x0, blocking collectives: 84 us -> none  [body(): summed = lax.psum(partial_sum, ('pairs', 'orb'))]
    all_to_all x0 -> x2, blocking collectives: none -> 52.5 us  [body(): lax.all_to_all(outgoing, 'pairs', split_axis=0, concat_axis=0, tiled=True)]
    gather x7 -> x0, local copies, waits for them, and re-layouts: 18 us -> none  [the longest x3 12.8 us: body(): targets = pair_slot[coupled]]
    dot_general x14 -> x0, matrix products: 12 us -> none  [the longest x2 8.4 us: body(): jnp.einsum('pkac,pkdc->pad', scaled, intersections, preferred_element_typ...]
    pallas_call x0 -> x5, Pallas kernels: none -> 10.1 us  [the longest x2 7.61 us: body(): pl.pallas_call(functools.partial(update_kernel, last, capacity, orbitals)...]
    all_to_all x2 -> x0, starting transfers between devices: 9.51 us -> none  [body(): lax.all_to_all(outgoing, 'pairs', split_axis=0, concat_axis=0, tiled=True)]
    unnamed x25 -> x20, local copies, waits for them, and re-layouts: 8.32 us -> 3.9 us
    convert_element_type x2 -> x0, local copies, waits for them, and re-layouts: 2.11 us -> none  [body(): outgoing = outgoing.astype(jnp.bfloat16)]
  transfers between devices with their start and end apart: 2 -> 0, of which waited for: 0 -> 0; matrix products, arithmetic and copies ran while one was open for 3% -> 0% of each run, Pallas kernels for 0% -> 0%
where the time goes in v1:
time: 84.2 us; the launch traced here: 83.9 us
  blocking collectives  68.1 us (81%)
  Pallas kernels  10.1 us (12%)
  local copies, waits for them, and re-layouts  4.9 us (6%)
    all_to_all x2, blocking collectives, body(): lax.all_to_all(outgoing, 'pairs', split_axis=0, concat_axis=0, tiled=True)  52.5 us
    all_gather x2, blocking collectives, body(): gathered = lax.all_gather(payload, 'orb', axis=0, tiled=False)  15.6 us
    pallas_call x2, Pallas kernels, body(): pl.pallas_call(functools.partial(update_kernel, last, capacity, orbitals)...  7.61 us
    unnamed x20, local copies, waits for them, and re-layouts  3.9 us

profile of v1, /device:TPU:0, one launch (start us, length us, event | category | flops | bytes accessed | tf_op | source)
XLA Modules:
  0.0 83.9 jit_solution(15556659087730888895)
XLA Ops:
  0.6 0.8 copy.16.ends
  1.4 0.0 copy-start.5
  1.4 0.8 copy.15
  2.3 0.1 reshape.24
  2.4 0.9 %copy.17.slot_col = s32[128,1]{1,0:T(8,128)S(1)} copy(s32[128,1]{0,1:T(1,128)} %bitcast.15) | data formatting | bytes 1024 | tf_op jit(solution)/shard_map/reshape | solution.py:228
  3.3 0.0 copy-start.1
  3.3 0.9 %copy-done.1 = f32[4,128,128]{2,1,0:T(8,128)S(1)} copy-done((f32[4,128,128]{2,1,0:T(8,128)S(1)}, f32[4,128,128]{2,1,0:T(8,128)}, u32[]{:S(2)}) %copy-start.1) | copy-done | bytes 262168
  4.2 0.7 copy-done.4
  4.9 0.7 copy-done.8
  5.6 1.0 %setup.1 = (bf16[528,128]{1,0:T(8,128)(2,1)S(1)}, s32[8,128]{1,0:T(8,128)S(1)}, s32[1,64]{1,0:T(1,128)S(1)}) custom-call(s32[1]{0:T(128)} %bitcast.position, s32[4,2]{1,0:T(4,128)S(1)} %copy.16.ends, f32[4,128,128]{2,1,0:T(8,128)S(1)} %copy-done.1, f32[4,128]{1,0:T(4,128)S(1)} %copy-done.4, s32[8,64]{1,0:T(8,128)S(1)} %bitcast.14, ...), custom_call_target="tpu_custom_call" | custom-call | tf_op jit(solution)/shard_map/setup/pallas_call | solution.py:215
  6.5 8.7 %all-gather = bf16[2112,128]{1,0:T(8,128)(2,1)S(1)} all-gather(bf16[528,128]{1,0:T(8,128)(2,1)S(1)} %get-tuple-element.9), channel_id=2, replica_groups=mesh['pairs'=8,'orb'=4] {'orb'}, dimensions={0}, use_global_device_ids=true | all-gather | bytes 675840 | tf_op jit(solution)/shard_map/all_gather | solution.py:233
  15.3 0.8 select.2
  16.0 27.7 %all_to_all.10 = bf16[8,400,128]{2,1,0:T(8,128)(2,1)S(1)} all-to-all(bf16[8,400,128]{2,1,0:T(8,128)(2,1)S(1)} %select.2), channel_id=1, replica_groups=mesh['pairs'=8,'orb'=4] {'pairs'}, dimensions={0} | all-to-all | bytes 1638400 | tf_op jit(solution)/shard_map/all_to_all | solution.py:242
  43.7 0.0 copy-done.5
  43.8 0.0 copy-done.6
  43.8 0.0 copy-done.7
  43.8 0.0 copy-done
  43.8 0.0 copy-done.2
  43.8 0.0 copy-done.3
  43.8 3.6 %update.2 = (f32[4,128,128]{2,1,0:T(8,128)S(1)}, bf16[528,128]{1,0:T(8,128)(2,1)S(1)}) custom-call(s32[1,64]{1,0:T(1,128)S(1)} %get-tuple-element.7.entry_row, f32[4,16]{1,0:T(4,128)S(1)} %copy-done.6, s32[4,2]{1,0:T(4,128)S(1)} %copy.16.ends, bf16[3200,128]{1,0:T(8,128)(2,1)S(1)} %bitcast.11, bf16[4,16,128,128]{3,2,1,0:T(8,128)(2,1)S(1)} %copy-done, ...), custom_call_target="tpu_custom_call" | custom-call | tf_op jit(solution)/shard_map/update/pallas_call | solution.py:249
  47.4 6.9 %all-gather.1 = bf16[2112,128]{1,0:T(8,128)(2,1)S(1)} all-gather(bf16[528,128]{1,0:T(8,128)(2,1)S(1)} %get-tuple-element.10), channel_id=3, replica_groups=mesh['pairs'=8,'orb'=4] {'orb'}, dimensions={0}, use_global_device_ids=true | all-gather | bytes 675840 | tf_op jit(solution)/shard_map/all_gather | solution.py:233
  54.3 0.8 select.3
  55.0 24.8 %all_to_all.11 = bf16[8,400,128]{2,1,0:T(8,128)(2,1)S(1)} all-to-all(bf16[8,400,128]{2,1,0:T(8,128)(2,1)S(1)} %select.3), channel_id=1, replica_groups=mesh['pairs'=8,'orb'=4] {'pairs'}, dimensions={0} | all-to-all | bytes 1638400 | tf_op jit(solution)/shard_map/all_to_all | solution.py:242
  79.9 4.0 %update.3 = (f32[4,128,128]{2,1,0:T(8,128)}, f32[4,128,128]{2,1,0:T(8,128)}) custom-call(s32[1,64]{1,0:T(1,128)S(1)} %get-tuple-element.7.entry_row, f32[4,16]{1,0:T(4,128)S(1)} %copy-done.6, s32[4,2]{1,0:T(4,128)S(1)} %copy.16.ends, bf16[3200,128]{1,0:T(8,128)(2,1)S(1)} %bitcast.10, bf16[4,16,128,128]{3,2,1,0:T(8,128)(2,1)S(1)} %copy-done, ...), custom_call_target="tpu_custom_call" | custom-call | tf_op jit(solution)/shard_map/update/pallas_call | solution.py:249
  (9 shorter events, 0.0 us)
Async XLA Ops:
  1.4 42.4 %copy-start.5 = (f32[4,128]{1,0:T(4,128)S(1)}, f32[4,128]{1,0:T(4,128)}, u32[]{:S(2)}) copy-start(f32[4,128]{1,0:T(4,128)} %projector.5) | copy-start | bytes 6148
  1.4 42.4 %copy-start.6 = (f32[4,16]{1,0:T(4,128)S(1)}, f32[4,16]{1,0:T(4,128)}, u32[]{:S(2)}) copy-start(f32[4,16]{1,0:T(4,128)} %couplings.3) | copy-start | bytes 772
  1.4 42.4 %copy-start.7 = (f32[4,128]{1,0:T(4,128)S(1)}, f32[4,128]{1,0:T(4,128)}, u32[]{:S(2)}) copy-start(f32[4,128]{1,0:T(4,128)} %energies.3) | copy-start | bytes 6148
  2.2 41.5 %copy-start = (bf16[4,16,128,128]{3,2,1,0:T(8,128)(2,1)S(1)}, bf16[4,16,128,128]{3,2,1,0:T(8,128)(2,1)}, u32[]{:S(2)}) copy-start(bf16[4,16,128,128]{3,2,1,0:T(8,128)(2,1)} %intersections.3) | copy-start | bytes 6291460
  3.3 1.0 %copy-start.1 = (f32[4,128,128]{2,1,0:T(8,128)S(1)}, f32[4,128,128]{2,1,0:T(8,128)}, u32[]{:S(2)}) copy-start(f32[4,128,128]{2,1,0:T(8,128)} %state.3) | copy-start | bytes 786436
  4.2 0.7 copy-start.4
  4.9 0.7 copy-start.8
  5.6 38.2 %copy-start.2 = (f32[4,128,128]{2,1,0:T(8,128)S(1)}, f32[4,128,128]{2,1,0:T(8,128)}, u32[]{:S(2)}) copy-start(f32[4,128,128]{2,1,0:T(8,128)} %state.3) | copy-start | bytes 786436
  5.6 38.2 %copy-start.3 = (bf16[4,128,128]{2,1,0:T(8,128)(2,1)S(1)}, bf16[4,128,128]{2,1,0:T(8,128)(2,1)}, u32[]{:S(2)}) copy-start(bf16[4,128,128]{2,1,0:T(8,128)(2,1)} %integrals.3) | copy-start | bytes 393220

commit v2 on v1

v2 whole, which is shorter than its diff:
```python
import functools

import jax
import jax.numpy as jnp
from jax import lax
from jax.experimental import pallas as pl
from jax.experimental.pallas import tpu as pltpu
from jax.sharding import PartitionSpec as P

PAIRS_ORB = 32
ITERS = 2
ROWS = 16
PARTS = 3

F32 = jnp.float32
BF16 = jnp.bfloat16
VMEM = pl.BlockSpec(memory_space=pltpu.VMEM)
SMEM = pl.BlockSpec(memory_space=pltpu.SMEM)
ANY = pl.BlockSpec(memory_space=pl.ANY)
HBM = pl.BlockSpec(memory_space=pltpu.HBM)
LIMIT = 40 * 1024 * 1024


def eye_mask(width):
    rows = lax.broadcasted_iota(jnp.int32, (width, width), 0)
    cols = lax.broadcasted_iota(jnp.int32, (width, width), 1)
    return rows == cols


def to_row(column, eye):
    return jnp.sum(jnp.where(eye, column, 0.0), axis=0, keepdims=True)


def to_column(row, eye):
    return jnp.sum(jnp.where(eye, row, 0.0), axis=1, keepdims=True)


def split_parts(value):
    parts = []
    for _ in range(PARTS):
        part = value.astype(BF16)
        parts.append(part)
        value = value - part.astype(F32)
    return parts


def tail_rows(value, rows):
    parts = split_parts(value)
    missing = rows - sum(part.shape[0] for part in parts)
    if missing:
        parts.append(jnp.zeros((missing, value.shape[1]), BF16))
    return jnp.concatenate([part.astype(F32) for part in parts], axis=0).astype(BF16)


def join_parts(rows, orbitals):
    rows = rows.astype(F32)
    value = rows[:orbitals]
    for part in range(1, PARTS):
        value = value + rows[part * orbitals : (part + 1) * orbitals]
    return value


def singles_terms(state, projector_row, orbital_a, orbital_b, orbitals, eye):
    projected = to_row(jnp.sum(state * projector_row, axis=1, keepdims=True), eye)
    ids = lax.broadcasted_iota(jnp.int32, (orbitals, 1), 0)
    count = (ids == orbital_a).astype(F32) + (ids == orbital_b).astype(F32)
    return count * projected


def setup_kernel(
    capacity, stride, orbitals, near,
    ends, state_hbm, projector_hbm, coupled_hbm, slot_hbm,
    payload, send_index, entry_index,
    state, projector, coupled, slot, sems,
):
    copies = [
        pltpu.make_async_copy(src, dst, sems.at[i])
        for i, (src, dst) in enumerate(
            ((coupled_hbm, coupled), (slot_hbm, slot), (projector_hbm, projector), (state_hbm, state))
        )
    ]
    for copy in copies:
        copy.start()
    per_device, width = state.shape[0], state.shape[1]
    count = slot.shape[1]
    pair_count, orb_count = lax.axis_size("pairs"), lax.axis_size("orb")
    pair_idx, orb_idx = lax.axis_index("pairs"), lax.axis_index("orb")
    group = orb_count * per_device
    copies[0].wait()
    copies[1].wait()
    slots = slot[...]
    wanted = coupled[...]
    lanes = lax.broadcasted_iota(jnp.int32, (1, count), 1)

    members = lax.broadcasted_iota(jnp.int32, (group, 1), 0)
    pairs = jnp.sum(jnp.where(slots == pair_idx * group + members, lanes, 0), axis=1, keepdims=True)
    hits = jnp.zeros((group, count), F32)
    for g in range(group):
        hit = jnp.max((wanted == pairs[g : g + 1, :]).astype(F32), axis=0, keepdims=True)
        hits = jnp.where(members == g, hit, hits)
    slot_ids = lax.broadcasted_iota(jnp.int32, (count, 128), 0)
    dest = lax.broadcasted_iota(jnp.int32, (count, 128), 1)
    owner = (slot_ids // per_device == dest * orb_count + orb_idx) & (dest < pair_count)
    needed = jnp.dot(hits, owner.astype(F32), preferred_element_type=F32) > 0.5
    run = jnp.zeros((1, 128), jnp.int32)
    picked = [jnp.zeros((1, 128), jnp.int32) for _ in range(capacity)]
    for g in range(group):
        hit = needed[g : g + 1, :].astype(jnp.int32)
        for c in range(capacity):
            picked[c] = picked[c] + jnp.where((hit == 1) & (run == c), g, 0)
        run = run + hit
    send_index[...] = jnp.concatenate(picked, axis=0)

    eye = eye_mask(count)
    slots_c = jnp.sum(jnp.where(eye, slots, 0), axis=1, keepdims=True)
    first = (pair_idx * orb_count + orb_idx) * per_device
    entries = []
    mine = jnp.zeros((1, count), F32)
    for i in range(per_device):
        own = jnp.sum(jnp.where(lanes == first + i, wanted, 0), axis=1, keepdims=True)
        entries.append((own == lanes).astype(F32))
        mine = jnp.maximum(mine, jnp.max(entries[i], axis=0, keepdims=True))
    mine_c = to_column(mine, eye)
    before = (slots_c // group == slots // group) & (slots_c < slots)
    rank = jnp.sum(jnp.where(before, mine_c, 0.0), axis=0, keepdims=True).astype(jnp.int32)
    place = ((slots // group) ^ (pair_idx & ~(near - 1))) * stride + rank * width
    place = place.astype(F32)
    column = lax.broadcasted_iota(jnp.int32, entry_index.shape, 1)
    index = jnp.zeros(entry_index.shape, F32)
    for i in range(per_device):
        found = jnp.sum(entries[i] * place, axis=1, keepdims=True)
        index = jnp.where(column == i, found, index)
    entry_index[...] = index.astype(jnp.int32)

    eye = eye_mask(width)
    copies[2].wait()
    copies[3].wait()
    total = jnp.zeros((orbitals, width), F32)
    for s in range(per_device):
        block = state[s]
        payload[pl.ds(s * width, width), :] = block.astype(BF16)
        total += singles_terms(block, projector[pl.ds(s, 1), :], ends[0, s], ends[1, s], orbitals, eye)
    tail = payload.shape[0] - per_device * width
    payload[pl.ds(per_device * width, tail), :] = tail_rows(total, tail)


def select_kernel(capacity, per_device, orbitals, width, near, send_index, gathered, out_near, *out_far):
    blocks = per_device * width
    tail = gathered.shape[1] - blocks
    base = lax.axis_index("pairs") & ~(near - 1)
    total = join_parts(gathered[0, pl.ds(blocks, tail), :], orbitals)
    for d in range(1, gathered.shape[0]):
        total += join_parts(gathered[d, pl.ds(blocks, tail), :], orbitals)
    rows = tail_rows(total, tail)
    outs = [(base + i, out_near.at[i]) for i in range(near)]
    outs += [(lax.axis_index("pairs") ^ (near + i), out) for i, out in enumerate(out_far)]
    for dest, out in outs:
        for c in range(capacity):
            j = send_index[c, dest]
            first = pl.multiple_of((j % per_device) * width, ROWS)
            out[pl.ds(c * width, width), :] = gathered[j // per_device, pl.ds(first, width), :]
        out[pl.ds(capacity * width, tail), :] = rows


def update_kernel(
    last, capacity, orbitals, sources,
    entry_index, couplings, ends, *refs,
):
    near, far = refs[0], refs[1:sources]
    intersections, state, integrals, energies, projector, out_a, out_b, held, arrived, sems = refs[sources:]
    per_device, count, width = intersections.shape[0], intersections.shape[1], intersections.shape[2]
    stride = capacity * width + tail_size(orbitals)
    copies = [
        pltpu.make_async_copy(intersections.at[s], held.at[s], sems.at[s]) for s in range(per_device)
    ]
    for copy in copies:
        copy.start()
    half = near.shape[0]
    for i in range(half):
        arrived[pl.ds(i * stride, stride), :] = near[i]
    for i in range(len(far)):
        place = (lax.axis_index("pairs") ^ (half + i)) ^ (lax.axis_index("pairs") & ~(half - 1))
        arrived[pl.ds(pl.multiple_of(place * stride, ROWS), stride), :] = far[i][...]
    eye = eye_mask(width)
    singles = None
    for p in range(arrived.shape[0] // stride):
        part = join_parts(
            arrived[pl.ds(p * stride + capacity * width, stride - capacity * width), :], orbitals
        )
        singles = part if singles is None else singles + part
    ids = lax.broadcasted_iota(jnp.int32, (orbitals, 1), 0)
    total = jnp.zeros((orbitals, width), F32)
    for s in range(per_device):
        copies[s].wait()
        coupling = jnp.zeros((width, width), F32)
        for k in range(0, count, 2):
            wide = jnp.concatenate([held[s, k], held[s, k + 1]], axis=1)
            scaled = []
            for m in (k, k + 1):
                first = pl.multiple_of(entry_index[m, s], ROWS)
                near = arrived[pl.ds(first, width), :]
                lifted = jnp.dot(held[s, m], near, preferred_element_type=F32)
                scaled.append((couplings[s, m] * lifted).astype(BF16))
            coupling += lax.dot_general(
                jnp.concatenate(scaled, axis=1), wide, (((1,), (1,)), ((), ())),
                preferred_element_type=F32,
            )
        old = state[s]
        energy = energies[pl.ds(s, 1), :]
        energy_c = to_column(energy, eye)
        proj = projector[pl.ds(s, 1), :]
        proj_c = to_column(proj, eye)
        left = jnp.sum(jnp.where(ids == ends[0, s], singles, 0.0), axis=0, keepdims=True)
        right = jnp.sum(jnp.where(ids == ends[1, s], singles, 0.0), axis=0, keepdims=True)
        residual = (
            integrals[s].astype(F32) + energy_c * old + old * energy - coupling
            + to_column(left, eye) * proj + proj_c * right
        )
        new = old - residual / (energy_c + energy)
        if last:
            out_a[s] = new
            out_b[s] = residual
        else:
            out_a[s] = new
            out_b[pl.ds(s * width, width), :] = new.astype(BF16)
            total += singles_terms(new, proj, ends[0, s], ends[1, s], orbitals, eye)
    if not last:
        tail = out_b.shape[0] - per_device * width
        out_b[pl.ds(per_device * width, tail), :] = tail_rows(total, tail)


def tail_size(orbitals):
    return -(-PARTS * orbitals // ROWS) * ROWS


def body(
    amplitudes, integrals, energies, intersections, couplings, projector, pair_orbitals, coupled, pair_slot,
):
    pair_count = lax.axis_size("pairs")
    per_device, width = amplitudes.shape[0], amplitudes.shape[1]
    total, neighbours = coupled.shape
    capacity = 1 + neighbours // pair_count
    orbitals = total // PAIRS_ORB
    tail = tail_size(orbitals)
    stride = capacity * width + tail
    params = pltpu.CompilerParams(vmem_limit_bytes=LIMIT)

    near = pair_count // 2 if pair_count <= 8 else pair_count
    ends = pair_orbitals.T
    payload, send_index, entry_index = pl.pallas_call(
        functools.partial(setup_kernel, capacity, stride, orbitals, near),
        out_shape=(
            jax.ShapeDtypeStruct((per_device * width + tail, width), BF16),
            jax.ShapeDtypeStruct((capacity, 128), jnp.int32),
            jax.ShapeDtypeStruct((neighbours, 128), jnp.int32),
        ),
        in_specs=[SMEM, HBM, HBM, HBM, HBM],
        out_specs=(VMEM, VMEM, VMEM),
        scratch_shapes=[
            pltpu.VMEM(amplitudes.shape, F32),
            pltpu.VMEM(projector.shape, F32),
            pltpu.VMEM((neighbours, total), jnp.int32),
            pltpu.VMEM((1, total), jnp.int32),
            pltpu.SemaphoreType.DMA((4,)),
        ],
        compiler_params=params,
        name="setup",
    )(ends, amplitudes, projector, coupled.T, pair_slot.reshape(1, total))
    entry_index = entry_index[:, :per_device]
    state = amplitudes
    sources = 1 + pair_count - near
    groups = [[i + j for j in range(near)] for i in range(0, pair_count, near)]
    for step in range(ITERS):
        last = step == ITERS - 1
        gathered = lax.all_gather(payload, "orb", axis=0, tiled=False)
        outgoing = pl.pallas_call(
            functools.partial(select_kernel, capacity, per_device, orbitals, width, near),
            out_shape=[jax.ShapeDtypeStruct((near, stride, width), BF16)]
            + [jax.ShapeDtypeStruct((stride, width), BF16)] * (sources - 1),
            in_specs=[SMEM, VMEM],
            out_specs=[VMEM] * sources,
            compiler_params=params,
            name="select",
        )(send_index, gathered)
        arrived = [
            lax.ppermute(outgoing[1 + i], "pairs", [(p, p ^ (near + i)) for p in range(pair_count)])
            for i in range(sources - 1)
        ]
        arrived = [
            lax.all_to_all(
                outgoing[0], "pairs", split_axis=0, concat_axis=0, axis_index_groups=groups, tiled=True
            )
        ] + arrived
        second = (
            jax.ShapeDtypeStruct(amplitudes.shape, F32)
            if last
            else jax.ShapeDtypeStruct((per_device * width + tail, width), BF16)
        )
        state, payload = pl.pallas_call(
            functools.partial(update_kernel, last, capacity, orbitals, sources),
            out_shape=(jax.ShapeDtypeStruct(amplitudes.shape, F32), second),
            in_specs=[SMEM, SMEM, SMEM] + [VMEM] * sources + [ANY, VMEM, VMEM, VMEM, VMEM],
            out_specs=(VMEM, VMEM),
            scratch_shapes=[
                pltpu.VMEM(intersections.shape, BF16),
                pltpu.VMEM((pair_count * stride, width), BF16),
                pltpu.SemaphoreType.DMA((per_device,)),
            ],
            compiler_params=params,
            name="update",
        )(
            entry_index, couplings, ends, *arrived, intersections, state, integrals, energies, projector,
        )
    return state, payload


def solution(mesh):
    split = ("pairs", "orb")
    return jax.shard_map(
        body,
        mesh=mesh,
        in_specs=(
            P(split, None, None),
            P(split, None, None),
            P(split, None),
            P(split, None, None, None),
            P(split, None),
            P(split, None),
            P(split, None),
            P(),
            P(),
        ),
        out_specs=(P(split, None, None), P(split, None, None)),
        check_vma=False,
    )
```

time: 84.2 us -> 84.5 us (level)
  the two profiles are of different devices: /device:TPU:0 before, /device:TPU:16 now
where the time goes in v2:
time: 84.5 us; the launch traced here: 84.1 us
  waiting for transfers between devices  33.3 us (39%)
  starting transfers between devices  19 us (22%)
  blocking collectives  14.1 us (17%)
  Pallas kernels  12.1 us (14%)
  local copies, waits for them, and re-layouts  4.77 us (6%)
    ppermute x8, waiting for transfers between devices, body(): lax.ppermute(outgoing[1 + i], 'pairs', [(p, p ^ near + i) for p in range(...  33.3 us
    all_gather x2, blocking collectives, body(): gathered = lax.all_gather(payload, 'orb', axis=0, tiled=False)  14.1 us
    ppermute x8, starting transfers between devices, body(): lax.ppermute(outgoing[1 + i], 'pairs', [(p, p ^ near + i) for p in range(...  11.8 us
    pallas_call x2, Pallas kernels, body(): pl.pallas_call(functools.partial(update_kernel, last, capacity, orbitals,...  7.94 us
    all_to_all x2, starting transfers between devices, body(): lax.all_to_all(outgoing[0], 'pairs', split_axis=0, concat_axis=0, axis_in...  7.26 us
    unnamed x24, local copies, waits for them, and re-layouts  4.77 us
    pallas_call x2, Pallas kernels, body(): pl.pallas_call(functools.partial(select_kernel, capacity, per_device, orb...  3.05 us
  transfers between devices with their start and end apart: 10, of which 8 were waited for; matrix products, arithmetic and copies ran while one was open for 0% of the time, Pallas kernels for 0%

profile of v2, /device:TPU:16, one launch (start us, length us, event | category | flops | bytes accessed | tf_op | source)
XLA Modules:
  0.0 84.1 jit_solution(9413449638035069656)
XLA Ops:
  0.7 1.1 %copy-done.1 = f32[4,128,128]{2,1,0:T(8,128)S(1)} copy-done((f32[4,128,128]{2,1,0:T(8,128)S(1)}, f32[4,128,128]{2,1,0:T(8,128)}, u32[]{:S(2)}) %copy-start.1) | copy-done | bytes 262168
  3.1 0.7 copy-done.8
  4.5 1.1 %setup.1 = (bf16[528,128]{1,0:T(8,128)(2,1)S(1)}, s32[3,128]{1,0:T(4,128)S(1)}, s32[16,128]{1,0:T(8,128)S(1)}) custom-call(s32[2,4]{1,0:T(2,128)S(1)} %bitcast.10, f32[4,128,128]{2,1,0:T(8,128)S(1)} %copy-done.1, f32[4,128]{1,0:T(4,128)S(1)} %copy-done.4, s32[16,128]{1,0:T(8,128)S(1)} %bitcast.13, s32[1,128]{1,0:T(1,128)S(1)} %bitcast.14), custom_call_target="tpu_custom_call" | custom-call | tf_op jit(solution)/shard_map/setup/pallas_call | solution.py:250
  5.6 7.3 %all-gather = bf16[2112,128]{1,0:T(8,128)(2,1)S(1)} all-gather(bf16[528,128]{1,0:T(8,128)(2,1)S(1)} %get-tuple-element.19), channel_id=2, replica_groups=mesh['pairs'=8,'orb'=4] {'orb'}, dimensions={0}, use_global_device_ids=true | all-gather | bytes 675840 | tf_op jit(solution)/shard_map/all_gather | solution.py:275
  12.9 1.5 %select.2 = (bf16[4,400,128]{2,1,0:T(8,128)(2,1)}, bf16[400,128]{1,0:T(8,128)(2,1)S(1)}, bf16[400,128]{1,0:T(8,128)(2,1)S(1)}, bf16[400,128]{1,0:T(8,128)(2,1)S(1)}, bf16[400,128]{1,0:T(8,128)(2,1)S(1)}) custom-call(s32[3,128]{1,0:T(4,128)S(1)} %get-tuple-element.18.send_index, bf16[4,528,128]{2,1,0:T(8,128)(2,1)S(1)} %bitcast.7), custom_call_target="tpu_custom_call" | custom-call | tf_op jit(solution)/shard_map/select/pallas_call | solution.py:276
  14.4 3.8 %all-to-all-start = ((bf16[4,400,128]{2,1,0:T(8,128)(2,1)}), bf16[4,400,128]{2,1,0:T(8,128)(2,1)S(1)}, u32[]{:S(2)}, u32[]{:S(2)}) async-start(bf16[4,400,128]{2,1,0:T(8,128)(2,1)} %get-tuple-element.20), calls=%async_computation | async-start | bytes 819200 | tf_op jit(solution)/shard_map/all_to_all | solution.py:290
  18.5 4.0 %collective-permute-start.1 = (bf16[400,128]{1,0:T(8,128)(2,1)S(1)}, bf16[400,128]{1,0:T(8,128)(2,1)S(1)}, u32[]{:S(2)}, u32[]{:S(2)}) collective-permute-start(bf16[400,128]{1,0:T(8,128)(2,1)S(1)} %get-tuple-element.22), channel_id=1, source_target_pairs={{0,20},{4,16},{8,28},{12,24},{16,4},{20,0},{24,12},{28,8},{1,21},{... | collective-permute-start | bytes 307208 | tf_op jit(solution)/shard_map/ppermute | solution.py:286
  22.9 1.1 %collective-permute-start.3 = (bf16[400,128]{1,0:T(8,128)(2,1)S(1)}, bf16[400,128]{1,0:T(8,128)(2,1)S(1)}, u32[]{:S(2)}, u32[]{:S(2)}) collective-permute-start(bf16[400,128]{1,0:T(8,128)(2,1)S(1)} %get-tuple-element.24), channel_id=1, source_target_pairs={{0,28},{4,24},{8,20},{12,16},{16,12},{20,8},{24,4},{28,0},{1,29},{... | collective-permute-start | bytes 307208 | tf_op jit(solution)/shard_map/ppermute | solution.py:286
  24.0 2.9 %collective-permute-done.refs_1_ = bf16[400,128]{1,0:T(8,128)(2,1)S(1)} collective-permute-done((bf16[400,128]{1,0:T(8,128)(2,1)S(1)}, bf16[400,128]{1,0:T(8,128)(2,1)S(1)}, u32[]{:S(2)}, u32[]{:S(2)}) %collective-permute-start) | collective-permute-done | bytes 102432 | tf_op jit(solution)/shard_map/ppermute | solution.py:286
  26.9 7.8 %collective-permute-done.1.refs_2_ = bf16[400,128]{1,0:T(8,128)(2,1)S(1)} collective-permute-done((bf16[400,128]{1,0:T(8,128)(2,1)S(1)}, bf16[400,128]{1,0:T(8,128)(2,1)S(1)}, u32[]{:S(2)}, u32[]{:S(2)}) %collective-permute-start.1) | collective-permute-done | bytes 102432 | tf_op jit(solution)/shard_map/ppermute | solution.py:286
  34.6 3.9 %collective-permute-done.2.refs_3_ = bf16[400,128]{1,0:T(8,128)(2,1)S(1)} collective-permute-done((bf16[400,128]{1,0:T(8,128)(2,1)S(1)}, bf16[400,128]{1,0:T(8,128)(2,1)S(1)}, u32[]{:S(2)}, u32[]{:S(2)}) %collective-permute-start.2) | collective-permute-done | bytes 102432 | tf_op jit(solution)/shard_map/ppermute | solution.py:286
  38.5 2.0 %collective-permute-done.3.refs_4_ = bf16[400,128]{1,0:T(8,128)(2,1)S(1)} collective-permute-done((bf16[400,128]{1,0:T(8,128)(2,1)S(1)}, bf16[400,128]{1,0:T(8,128)(2,1)S(1)}, u32[]{:S(2)}, u32[]{:S(2)}) %collective-permute-start.3) | collective-permute-done | bytes 102432 | tf_op jit(solution)/shard_map/ppermute | solution.py:286
  40.6 0.9 %copy-done.2 = f32[4,128,128]{2,1,0:T(8,128)S(1)} copy-done((f32[4,128,128]{2,1,0:T(8,128)S(1)}, f32[4,128,128]{2,1,0:T(8,128)}, u32[]{:S(2)}) %copy-start.2) | copy-done | bytes 262168
  41.5 3.7 %update.2 = (f32[4,128,128]{2,1,0:T(8,128)S(1)}, bf16[528,128]{1,0:T(8,128)(2,1)S(1)}) custom-call(s32[16,4]{1,0:T(8,128)S(1)} %bitcast.8, f32[4,16]{1,0:T(4,128)S(1)} %copy-done.9, s32[2,4]{1,0:T(2,128)S(1)} %bitcast.11, bf16[4,400,128]{2,1,0:T(8,128)(2,1)S(1)} %all-to-all-done.refs_0_, bf16[400,128]{1,0:T(8,128)(2,1)S(1)} %collective-permute-done.refs_1_, ...), custom_call_target="tpu_custom_call" | custom-call | tf_op jit(solution)/shard_map/update/pallas_call | solution.py:299
  45.3 6.9 %all-gather.1 = bf16[2112,128]{1,0:T(8,128)(2,1)S(1)} all-gather(bf16[528,128]{1,0:T(8,128)(2,1)S(1)} %get-tuple-element.25), channel_id=3, replica_groups=mesh['pairs'=8,'orb'=4] {'orb'}, dimensions={0}, use_global_device_ids=true | all-gather | bytes 675840 | tf_op jit(solution)/shard_map/all_gather | solution.py:275
  52.1 1.5 %select.3 = (bf16[4,400,128]{2,1,0:T(8,128)(2,1)}, bf16[400,128]{1,0:T(8,128)(2,1)}, bf16[400,128]{1,0:T(8,128)(2,1)}, bf16[400,128]{1,0:T(8,128)(2,1)S(1)}, bf16[400,128]{1,0:T(8,128)(2,1)S(1)}) custom-call(s32[3,128]{1,0:T(4,128)S(1)} %get-tuple-element.18.send_index, bf16[4,528,128]{2,1,0:T(8,128)(2,1)S(1)} %bitcast.6), custom_call_target="tpu_custom_call" | custom-call | tf_op jit(solution)/shard_map/select/pallas_call | solution.py:276
  53.7 3.5 %all-to-all-start.1 = ((bf16[4,400,128]{2,1,0:T(8,128)(2,1)}), bf16[4,400,128]{2,1,0:T(8,128)(2,1)S(1)}, u32[]{:S(2)}, u32[]{:S(2)}) async-start(bf16[4,400,128]{2,1,0:T(8,128)(2,1)} %get-tuple-element.26), calls=%async_computation.1 | async-start | bytes 819200 | tf_op jit(solution)/shard_map/all_to_all | solution.py:290
  57.2 4.3 %collective-permute-start.5 = (bf16[400,128]{1,0:T(8,128)(2,1)}, bf16[400,128]{1,0:T(8,128)(2,1)S(1)}, u32[]{:S(2)}, u32[]{:S(2)}) collective-permute-start(bf16[400,128]{1,0:T(8,128)(2,1)} %get-tuple-element.28), channel_id=1, source_target_pairs={{0,20},{4,16},{8,28},{12,24},{16,4},{20,0},{24,12},{28,8},{1,21},{... | collective-permute-start | bytes 307208 | tf_op jit(solution)/shard_map/ppermute | solution.py:286
  61.5 1.6 %collective-permute-start.7 = (bf16[400,128]{1,0:T(8,128)(2,1)S(1)}, bf16[400,128]{1,0:T(8,128)(2,1)S(1)}, u32[]{:S(2)}, u32[]{:S(2)}) collective-permute-start(bf16[400,128]{1,0:T(8,128)(2,1)S(1)} %get-tuple-element.30), channel_id=1, source_target_pairs={{0,28},{4,24},{8,20},{12,16},{16,12},{20,8},{24,4},{28,0},{1,29},{... | collective-permute-start | bytes 307208 | tf_op jit(solution)/shard_map/ppermute | solution.py:286
  63.1 2.2 %collective-permute-done.4.refs_1_ = bf16[400,128]{1,0:T(8,128)(2,1)S(1)} collective-permute-done((bf16[400,128]{1,0:T(8,128)(2,1)}, bf16[400,128]{1,0:T(8,128)(2,1)S(1)}, u32[]{:S(2)}, u32[]{:S(2)}) %collective-permute-start.4) | collective-permute-done | bytes 102432 | tf_op jit(solution)/shard_map/ppermute | solution.py:286
  65.2 8.6 %collective-permute-done.5.refs_2_ = bf16[400,128]{1,0:T(8,128)(2,1)S(1)} collective-permute-done((bf16[400,128]{1,0:T(8,128)(2,1)}, bf16[400,128]{1,0:T(8,128)(2,1)S(1)}, u32[]{:S(2)}, u32[]{:S(2)}) %collective-permute-start.5) | collective-permute-done | bytes 102432 | tf_op jit(solution)/shard_map/ppermute | solution.py:286
  73.9 3.5 %collective-permute-done.6.refs_3_ = bf16[400,128]{1,0:T(8,128)(2,1)S(1)} collective-permute-done((bf16[400,128]{1,0:T(8,128)(2,1)S(1)}, bf16[400,128]{1,0:T(8,128)(2,1)S(1)}, u32[]{:S(2)}, u32[]{:S(2)}) %collective-permute-start.6) | collective-permute-done | bytes 102432 | tf_op jit(solution)/shard_map/ppermute | solution.py:286
  77.4 2.5 %collective-permute-done.7.refs_4_ = bf16[400,128]{1,0:T(8,128)(2,1)S(1)} collective-permute-done((bf16[400,128]{1,0:T(8,128)(2,1)S(1)}, bf16[400,128]{1,0:T(8,128)(2,1)S(1)}, u32[]{:S(2)}, u32[]{:S(2)}) %collective-permute-start.7) | collective-permute-done | bytes 102432 | tf_op jit(solution)/shard_map/ppermute | solution.py:286
  79.9 4.2 %update.3 = (f32[4,128,128]{2,1,0:T(8,128)}, f32[4,128,128]{2,1,0:T(8,128)}) custom-call(s32[16,4]{1,0:T(8,128)S(1)} %bitcast.9, f32[4,16]{1,0:T(4,128)S(1)} %copy-done.9, s32[2,4]{1,0:T(2,128)S(1)} %bitcast.12, bf16[4,400,128]{2,1,0:T(8,128)(2,1)S(1)} %all-to-all-done.1.refs_0_, bf16[400,128]{1,0:T(8,128)(2,1)S(1)} %collective-permute-done.4.refs_1_, ...), custom_call_target="tpu_custom_call" | custom-call | tf_op jit(solution)/shard_map/update/pallas_call | solution.py:299
  (27 shorter events, 2.8 us)
Async XLA Ops:
  0.6 39.9 %copy-start = (bf16[4,16,128,128]{3,2,1,0:T(8,128)(2,1)S(1)}, bf16[4,16,128,128]{3,2,1,0:T(8,128)(2,1)}, u32[]{:S(2)}) copy-start(bf16[4,16,128,128]{3,2,1,0:T(8,128)(2,1)} %refs_5_.3) | copy-start | bytes 6291460
  0.6 1.1 %copy-start.1 = (f32[4,128,128]{2,1,0:T(8,128)S(1)}, f32[4,128,128]{2,1,0:T(8,128)}, u32[]{:S(2)}) copy-start(f32[4,128,128]{2,1,0:T(8,128)} %refs_6_.1) | copy-start | bytes 786436
  1.7 0.7 copy-start.4
  2.4 0.7 copy-start.6
  3.1 0.7 copy-start.8
  3.8 0.7 copy-start.11
  4.5 36.1 %copy-start.3 = (bf16[4,128,128]{2,1,0:T(8,128)(2,1)S(1)}, bf16[4,128,128]{2,1,0:T(8,128)(2,1)}, u32[]{:S(2)}) copy-start(bf16[4,128,128]{2,1,0:T(8,128)(2,1)} %refs_7_.3) | copy-start | bytes 393220
  4.5 36.1 %copy-start.5 = (f32[4,128]{1,0:T(4,128)S(1)}, f32[4,128]{1,0:T(4,128)}, u32[]{:S(2)}) copy-start(f32[4,128]{1,0:T(4,128)} %refs_9_.3) | copy-start | bytes 6148
  4.5 36.1 %copy-start.7 = (s32[4,2]{0,1:T(2,128)S(1)}, s32[4,2]{0,1:T(2,128)}, u32[]{:S(2)}) copy-start(s32[4,2]{0,1:T(2,128)} %param.15) | copy-start | bytes 100
  4.5 36.1 %copy-start.9 = (f32[4,16]{1,0:T(4,128)S(1)}, f32[4,16]{1,0:T(4,128)}, u32[]{:S(2)}) copy-start(f32[4,16]{1,0:T(4,128)} %couplings.3) | copy-start | bytes 772
  4.5 36.1 %copy-start.10 = (f32[4,128]{1,0:T(4,128)S(1)}, f32[4,128]{1,0:T(4,128)}, u32[]{:S(2)}) copy-start(f32[4,128]{1,0:T(4,128)} %refs_8_.3) | copy-start | bytes 6148
  14.4 26.1 %all-to-all-start = ((bf16[4,400,128]{2,1,0:T(8,128)(2,1)}), bf16[4,400,128]{2,1,0:T(8,128)(2,1)S(1)}, u32[]{:S(2)}, u32[]{:S(2)}) async-start(bf16[4,400,128]{2,1,0:T(8,128)(2,1)} %get-tuple-element.20), calls=%async_computation | async-start | bytes 819200 | tf_op jit(solution)/shard_map/all_to_all | solution.py:290
  18.2 8.7 %collective-permute-start = (bf16[400,128]{1,0:T(8,128)(2,1)S(1)}, bf16[400,128]{1,0:T(8,128)(2,1)S(1)}, u32[]{:S(2)}, u32[]{:S(2)}) collective-permute-start(bf16[400,128]{1,0:T(8,128)(2,1)S(1)} %get-tuple-element.21), channel_id=1, source_target_pairs={{0,16},{4,20},{8,24},{12,28},{16,0},{20,4},{24,8},{28,12},{1,17},{... | collective-permute-start | bytes 307208 | tf_op jit(solution)/shard_map/ppermute | solution.py:286
  18.5 16.1 %collective-permute-start.1 = (bf16[400,128]{1,0:T(8,128)(2,1)S(1)}, bf16[400,128]{1,0:T(8,128)(2,1)S(1)}, u32[]{:S(2)}, u32[]{:S(2)}) collective-permute-start(bf16[400,128]{1,0:T(8,128)(2,1)S(1)} %get-tuple-element.22), channel_id=1, source_target_pairs={{0,20},{4,16},{8,28},{12,24},{16,4},{20,0},{24,12},{28,8},{1,21},{... | collective-permute-start | bytes 307208 | tf_op jit(solution)/shard_map/ppermute | solution.py:286
  22.6 16.0 %collective-permute-start.2 = (bf16[400,128]{1,0:T(8,128)(2,1)S(1)}, bf16[400,128]{1,0:T(8,128)(2,1)S(1)}, u32[]{:S(2)}, u32[]{:S(2)}) collective-permute-start(bf16[400,128]{1,0:T(8,128)(2,1)S(1)} %get-tuple-element.23), channel_id=1, source_target_pairs={{0,24},{4,28},{8,16},{12,20},{16,8},{20,12},{24,0},{28,4},{1,25},{... | collective-permute-start | bytes 307208 | tf_op jit(solution)/shard_map/ppermute | solution.py:286
  22.9 17.6 %collective-permute-start.3 = (bf16[400,128]{1,0:T(8,128)(2,1)S(1)}, bf16[400,128]{1,0:T(8,128)(2,1)S(1)}, u32[]{:S(2)}, u32[]{:S(2)}) collective-permute-start(bf16[400,128]{1,0:T(8,128)(2,1)S(1)} %get-tuple-element.24), channel_id=1, source_target_pairs={{0,28},{4,24},{8,20},{12,16},{16,12},{20,8},{24,4},{28,0},{1,29},{... | collective-permute-start | bytes 307208 | tf_op jit(solution)/shard_map/ppermute | solution.py:286
  40.6 1.0 %copy-start.2 = (f32[4,128,128]{2,1,0:T(8,128)S(1)}, f32[4,128,128]{2,1,0:T(8,128)}, u32[]{:S(2)}) copy-start(f32[4,128,128]{2,1,0:T(8,128)} %refs_6_.1) | copy-start | bytes 786436
  53.7 26.2 %all-to-all-start.1 = ((bf16[4,400,128]{2,1,0:T(8,128)(2,1)}), bf16[4,400,128]{2,1,0:T(8,128)(2,1)S(1)}, u32[]{:S(2)}, u32[]{:S(2)}) async-start(bf16[4,400,128]{2,1,0:T(8,128)(2,1)} %get-tuple-element.26), calls=%async_computation.1 | async-start | bytes 819200 | tf_op jit(solution)/shard_map/all_to_all | solution.py:290
  57.2 8.1 %collective-permute-start.4 = (bf16[400,128]{1,0:T(8,128)(2,1)}, bf16[400,128]{1,0:T(8,128)(2,1)S(1)}, u32[]{:S(2)}, u32[]{:S(2)}) collective-permute-start(bf16[400,128]{1,0:T(8,128)(2,1)} %get-tuple-element.27), channel_id=1, source_target_pairs={{0,16},{4,20},{8,24},{12,28},{16,0},{20,4},{24,8},{28,12},{1,17},{... | collective-permute-start | bytes 307208 | tf_op jit(solution)/shard_map/ppermute | solution.py:286
  57.2 16.7 %collective-permute-start.5 = (bf16[400,128]{1,0:T(8,128)(2,1)}, bf16[400,128]{1,0:T(8,128)(2,1)S(1)}, u32[]{:S(2)}, u32[]{:S(2)}) collective-permute-start(bf16[400,128]{1,0:T(8,128)(2,1)} %get-tuple-element.28), channel_id=1, source_target_pairs={{0,20},{4,16},{8,28},{12,24},{16,4},{20,0},{24,12},{28,8},{1,21},{... | collective-permute-start | bytes 307208 | tf_op jit(solution)/shard_map/ppermute | solution.py:286
  61.5 15.9 %collective-permute-start.6 = (bf16[400,128]{1,0:T(8,128)(2,1)S(1)}, bf16[400,128]{1,0:T(8,128)(2,1)S(1)}, u32[]{:S(2)}, u32[]{:S(2)}) collective-permute-start(bf16[400,128]{1,0:T(8,128)(2,1)S(1)} %get-tuple-element.29), channel_id=1, source_target_pairs={{0,24},{4,28},{8,16},{12,20},{16,8},{20,12},{24,0},{28,4},{1,25},{... | collective-permute-start | bytes 307208 | tf_op jit(solution)/shard_map/ppermute | solution.py:286
  61.5 18.4 %collective-permute-start.7 = (bf16[400,128]{1,0:T(8,128)(2,1)S(1)}, bf16[400,128]{1,0:T(8,128)(2,1)S(1)}, u32[]{:S(2)}, u32[]{:S(2)}) collective-permute-start(bf16[400,128]{1,0:T(8,128)(2,1)S(1)} %get-tuple-element.30), channel_id=1, source_target_pairs={{0,28},{4,24},{8,20},{12,16},{16,12},{20,8},{24,4},{28,0},{1,29},{... | collective-permute-start | bytes 307208 | tf_op jit(solution)/shard_map/ppermute | solution.py:286

commit v3 on v2

v3 whole, which is shorter than its diff:
```python
import functools

import jax
import jax.numpy as jnp
from jax import lax
from jax.experimental import pallas as pl
from jax.experimental.pallas import tpu as pltpu
from jax.sharding import PartitionSpec as P

PAIRS_ORB = 32
ITERS = 2
ROWS = 16
PARTS = 3
EARLY = 20_000_000_000
CLOSE = 1_000_000_000

F32 = jnp.float32
BF16 = jnp.bfloat16
VMEM = pl.BlockSpec(memory_space=pltpu.VMEM)
SMEM = pl.BlockSpec(memory_space=pltpu.SMEM)
ANY = pl.BlockSpec(memory_space=pl.ANY)
HBM = pl.BlockSpec(memory_space=pltpu.HBM)
LIMIT = 16 * 1024 * 1024
SMALL = 8 * 1024 * 1024
WHOLE = 60 * 1024 * 1024


def eye_mask(width):
    rows = lax.broadcasted_iota(jnp.int32, (width, width), 0)
    cols = lax.broadcasted_iota(jnp.int32, (width, width), 1)
    return rows == cols


def to_row(column, eye):
    return jnp.sum(jnp.where(eye, column, 0.0), axis=0, keepdims=True)


def to_column(row, eye):
    return jnp.sum(jnp.where(eye, row, 0.0), axis=1, keepdims=True)


def split_parts(value):
    parts = []
    for _ in range(PARTS):
        part = value.astype(BF16)
        parts.append(part)
        value = value - part.astype(F32)
    return parts


def tail_rows(value, rows):
    parts = split_parts(value)
    missing = rows - sum(part.shape[0] for part in parts)
    if missing:
        parts.append(jnp.zeros((missing, value.shape[1]), BF16))
    return jnp.concatenate([part.astype(F32) for part in parts], axis=0).astype(BF16)


def join_parts(rows, orbitals):
    rows = rows.astype(F32)
    value = rows[:orbitals]
    for part in range(1, PARTS):
        value = value + rows[part * orbitals : (part + 1) * orbitals]
    return value


def singles_terms(state, projector_row, count, eye):
    projected = to_row(jnp.sum(state * projector_row, axis=1, keepdims=True), eye)
    return count * projected


def end_counts(orbitals, per_device, end):
    ids = lax.broadcasted_iota(jnp.int32, (orbitals, 1), 0)
    return [(ids == end(s)).astype(F32) for s in range(per_device)]


def fetch(pairs, sems):
    copies = [pltpu.make_async_copy(src, dst, sems.at[i]) for i, (src, dst) in enumerate(pairs)]
    for copy in copies:
        copy.start()
    return copies


def setup_kernel(
    capacity, orbitals,
    ends, state_hbm, projector_hbm, coupled_hbm, slot_hbm,
    payload, index,
    state, projector, coupled, slot, sems,
):
    copies = fetch(
        ((coupled_hbm, coupled), (slot_hbm, slot), (projector_hbm, projector), (state_hbm, state)), sems
    )
    per_device, width = state.shape[0], state.shape[1]
    count = slot.shape[1]
    pair_count, orb_count = lax.axis_size("pairs"), lax.axis_size("orb")
    pair_idx, orb_idx = lax.axis_index("pairs"), lax.axis_index("orb")
    group = orb_count * per_device
    lanes_out = index.shape[1]
    copies[0].wait()
    copies[1].wait()
    slots = slot[...]
    wanted = coupled[...]
    lanes = lax.broadcasted_iota(jnp.int32, (1, count), 1)
    members = lax.broadcasted_iota(jnp.int32, (group, 1), 0)
    pairs = jnp.sum(jnp.where(slots == pair_idx * group + members, lanes, 0), axis=1, keepdims=True)
    hits = jnp.zeros((group, count), F32)
    for g in range(group):
        hit = jnp.max((wanted == pairs[g : g + 1, :]).astype(F32), axis=0, keepdims=True)
        hits = jnp.where(members == g, hit, hits)
    slot_ids = lax.broadcasted_iota(jnp.int32, (count, lanes_out), 0)
    dest = lax.broadcasted_iota(jnp.int32, (count, lanes_out), 1)
    owner = (slot_ids // per_device == dest * orb_count + orb_idx) & (dest < pair_count)
    needed = jnp.dot(hits, owner.astype(F32), preferred_element_type=F32) > 0.5
    run = jnp.zeros((1, lanes_out), jnp.int32)
    picked = [jnp.zeros((1, lanes_out), jnp.int32) for _ in range(capacity)]
    for g in range(group):
        hit = needed[g : g + 1, :].astype(jnp.int32)
        for c in range(capacity):
            picked[c] = picked[c] + jnp.where((hit == 1) & (run == c), g, 0)
        run = run + hit
    for c, row in enumerate(picked):
        index[pl.ds(c, 1), :] = row

    eye = eye_mask(width)
    copies[2].wait()
    copies[3].wait()
    total = jnp.zeros((orbitals, width), F32)
    counts_a = end_counts(orbitals, per_device, lambda s: ends[0, s])
    counts_b = end_counts(orbitals, per_device, lambda s: ends[1, s])
    for s in range(per_device):
        block = state[s]
        payload[pl.ds(s * width, width), :] = block.astype(BF16)
        total += singles_terms(block, projector[pl.ds(s, 1), :], counts_a[s] + counts_b[s], eye)
    tail = payload.shape[0] - per_device * width
    payload[pl.ds(per_device * width, tail), :] = tail_rows(total, tail)


def tables_kernel(
    capacity, near,
    coupled_hbm, slot_hbm, couplings_hbm,
    index, coefficients,
    coupled, slot, couplings, sems,
):
    copies = fetch(((coupled_hbm, coupled), (slot_hbm, slot), (couplings_hbm, couplings)), sems)
    neighbours, count = coupled.shape
    per_device = couplings.shape[0]
    orb_count = lax.axis_size("orb")
    pair_idx, orb_idx = lax.axis_index("pairs"), lax.axis_index("orb")
    group = orb_count * per_device
    lanes_out = index.shape[1]
    for copy in copies:
        copy.wait()
    slots = slot[...]
    wanted = coupled[...]
    lanes = lax.broadcasted_iota(jnp.int32, (1, count), 1)
    eye = eye_mask(count)
    slots_c = jnp.sum(jnp.where(eye, slots, 0), axis=1, keepdims=True)
    first = (pair_idx * orb_count + orb_idx) * per_device
    entries = []
    mine = jnp.zeros((1, count), F32)
    for i in range(per_device):
        own = jnp.sum(jnp.where(lanes == first + i, wanted, 0), axis=1, keepdims=True)
        entries.append((own == lanes).astype(F32))
        mine = jnp.maximum(mine, jnp.max(entries[i], axis=0, keepdims=True))
    mine_c = to_column(mine, eye)
    before = (slots_c // group == slots // group) & (slots_c < slots)
    rank = jnp.sum(jnp.where(before, mine_c, 0.0), axis=0, keepdims=True).astype(jnp.int32)
    source = slots // group
    flip = source ^ pair_idx
    place = jnp.where(flip < near, source ^ (pair_idx & ~(near - 1)), flip) * capacity + rank
    place = place.astype(F32)
    ids = lax.broadcasted_iota(jnp.int32, (neighbours, 1), 0)
    square = eye_mask(neighbours)
    column = lax.broadcasted_iota(jnp.int32, (neighbours, lanes_out), 1)
    for i in range(per_device):
        found = jnp.sum(entries[i] * place, axis=1, keepdims=True).astype(jnp.int32)
        match = found == column
        index[pl.ds(i, 1), :] = jnp.sum(jnp.where(match, ids, 0), axis=0, keepdims=True)
        value = to_column(couplings[pl.ds(i, 1), :], square)
        coefficients[pl.ds(i, 1), :] = jnp.sum(jnp.where(match, value, 0.0), axis=0, keepdims=True)


def select_kernel(capacity, per_device, orbitals, width, mask, flips, index, gathered, *outs):
    blocks = per_device * width
    tail = gathered.shape[1] - blocks
    here = lax.axis_index("pairs")
    total = join_parts(gathered[0, pl.ds(blocks, tail), :], orbitals)
    for d in range(1, gathered.shape[0]):
        total += join_parts(gathered[d, pl.ds(blocks, tail), :], orbitals)
    rows = tail_rows(total, tail)
    for flip, out in zip(flips, outs):
        dest = (here & mask) ^ flip
        for c in range(capacity):
            j = index[c, dest]
            first = pl.multiple_of((j % per_device) * width, ROWS)
            out[pl.ds(c * width, width), :] = gathered[j // per_device, pl.ds(first, width), :]
        out[pl.ds(capacity * width, tail), :] = rows


def add_blocks(capacity, orbitals, index, coefficients, intersections, blocks, coupling, singles):
    per_device, width = intersections.shape[0], intersections.shape[2]
    slots = [(place * capacity + c, ref, c * width) for place, ref in blocks for c in range(capacity)]
    wide = [[] for _ in range(per_device)]
    scaled = [[] for _ in range(per_device)]
    empty = jnp.zeros((width, width), BF16)
    for p in range(0, len(slots), 2):
        part = slots[p : p + 2]
        mixing = [
            jnp.concatenate([intersections[s, index[s, lane]] for lane, _, _ in part], axis=1)
            for s in range(per_device)
        ]
        near = [ref[pl.ds(row, width), :] for _, ref, row in part]
        if len(part) == 2:
            near = jnp.concatenate(
                [jnp.concatenate([near[0], empty], axis=1), jnp.concatenate([empty, near[1]], axis=1)], axis=0
            )
        else:
            near = near[0]
        lifted = jnp.dot(jnp.concatenate(mixing, axis=0), near, preferred_element_type=F32)
        for s in range(per_device):
            wide[s].append(mixing[s])
            for i, (lane, _, _) in enumerate(part):
                block = lifted[s * width : (s + 1) * width, i * width : (i + 1) * width]
                scaled[s].append((coefficients[s, lane] * block).astype(BF16))
    for s in range(per_device):
        if slots:
            coupling[s] = coupling[s] + lax.dot_general(
                jnp.concatenate(scaled[s], axis=1), jnp.concatenate(wide[s], axis=1),
                (((1,), (1,)), ((), ())), preferred_element_type=F32,
            )
    for _, ref in blocks:
        tail = ref.shape[0] - capacity * width
        singles = singles + join_parts(ref[pl.ds(capacity * width, tail), :], orbitals)
    return singles


def gather_terms(capacity, orbitals, index, coefficients, intersections, near, far, first, before):
    per_device, width = intersections.shape[0], intersections.shape[2]
    coupling = [jnp.zeros((width, width), F32) for _ in range(per_device)]
    singles = jnp.zeros((orbitals, width), F32)
    if before is not None:
        coupling = [before[pl.ds(s * width, width), :] for s in range(per_device)]
        singles = before[pl.ds(per_device * width, orbitals), :]
    operands = (capacity, orbitals, index, coefficients, intersections)
    blocks = [(first + i, ref) for i, ref in enumerate(far)]
    count = 0 if near is None else near.shape[0]
    unit = min(count, 4)
    if count <= unit:
        blocks = [(i, near.at[i]) for i in range(count)] + blocks
    else:

        def step(i, carry):
            parts = list(carry[:-1])
            some = [(i * unit + u, near.at[i * unit + u]) for u in range(unit)]
            total = add_blocks(*operands, some, parts, carry[-1])
            return (*parts, total)

        *coupling, singles = lax.fori_loop(0, count // unit, step, (*coupling, singles))
    singles = add_blocks(*operands, blocks, coupling, singles)
    return coupling, singles


def terms_kernel(capacity, orbitals, has_before, has_near, first, index, coefficients, intersections, *refs):
    out = refs[-1]
    refs = list(refs[:-1])
    before = refs.pop(0) if has_before else None
    near = refs.pop(0) if has_near else None
    coupling, singles = gather_terms(
        capacity, orbitals, index, coefficients, intersections, near, refs, first, before
    )
    width = intersections.shape[2]
    for s, part in enumerate(coupling):
        out[pl.ds(s * width, width), :] = part
    out[pl.ds(len(coupling) * width, orbitals), :] = singles


def update_kernel(
    last, capacity, orbitals, first, far_count,
    index, coefficients, ends, intersections, before, *refs,
):
    far = refs[:far_count]
    state, integrals, energies, projector, out_a, out_b = refs[far_count:]
    per_device, width = state.shape[0], state.shape[1]
    coupling, singles = gather_terms(
        capacity, orbitals, index, coefficients, intersections, None, far, first, before
    )
    eye = eye_mask(width)
    total = jnp.zeros((orbitals, width), F32)
    counts_a = end_counts(orbitals, per_device, lambda s: ends[0, s])
    counts_b = end_counts(orbitals, per_device, lambda s: ends[1, s])
    for s in range(per_device):
        old = state[s]
        energy = energies[pl.ds(s, 1), :]
        energy_c = to_column(energy, eye)
        proj = projector[pl.ds(s, 1), :]
        proj_c = to_column(proj, eye)
        left = jnp.sum(counts_a[s] * singles, axis=0, keepdims=True)
        right = jnp.sum(counts_b[s] * singles, axis=0, keepdims=True)
        residual = (
            integrals[s].astype(F32) + energy_c * old + old * energy - coupling[s]
            + to_column(left, eye) * proj + proj_c * right
        )
        new = old - residual / (energy_c + energy)
        out_a[s] = new
        if last:
            out_b[s] = residual
        else:
            out_b[pl.ds(s * width, width), :] = new.astype(BF16)
            total += singles_terms(new, proj, counts_a[s] + counts_b[s], eye)
    if not last:
        tail = out_b.shape[0] - per_device * width
        out_b[pl.ds(per_device * width, tail), :] = tail_rows(total, tail)


def tail_size(orbitals):
    return -(-PARTS * orbitals // ROWS) * ROWS


def cost(flops):
    return pl.CostEstimate(flops=flops, bytes_accessed=0, transcendentals=0)


def body(
    amplitudes, integrals, energies, intersections, couplings, projector, pair_orbitals, coupled, pair_slot,
):
    pair_count = lax.axis_size("pairs")
    per_device, width = amplitudes.shape[0], amplitudes.shape[1]
    total, neighbours = coupled.shape
    capacity = 1 + neighbours // pair_count
    orbitals = total // PAIRS_ORB
    tail = tail_size(orbitals)
    stride = capacity * width + tail
    near = pair_count // 2 if pair_count <= 8 else pair_count
    lanes = -(-pair_count * capacity // 128) * 128
    ends = pair_orbitals.T
    small = pltpu.CompilerParams(vmem_limit_bytes=SMALL)
    params = pltpu.CompilerParams(vmem_limit_bytes=LIMIT)
    block_shape = jax.ShapeDtypeStruct((stride, width), BF16)
    terms_shape = jax.ShapeDtypeStruct((per_device * width + -(-orbitals // 8) * 8, width), F32)
    payload_shape = jax.ShapeDtypeStruct((per_device * width + tail, width), BF16)
    payload, send_index = pl.pallas_call(
        functools.partial(setup_kernel, capacity, orbitals),
        out_shape=(payload_shape, jax.ShapeDtypeStruct((8, lanes), jnp.int32)),
        in_specs=[SMEM, HBM, HBM, HBM, HBM],
        out_specs=(VMEM, VMEM),
        scratch_shapes=[
            pltpu.VMEM(amplitudes.shape, F32),
            pltpu.VMEM(projector.shape, F32),
            pltpu.VMEM((neighbours, total), jnp.int32),
            pltpu.VMEM((1, total), jnp.int32),
            pltpu.SemaphoreType.DMA((4,)),
        ],
        compiler_params=pltpu.CompilerParams(vmem_limit_bytes=WHOLE),
        name="setup",
    )(ends, amplitudes, projector, coupled.T, pair_slot.reshape(1, total))
    index, coefficients = pl.pallas_call(
        functools.partial(tables_kernel, capacity, near),
        out_shape=(
            jax.ShapeDtypeStruct((per_device, lanes), jnp.int32),
            jax.ShapeDtypeStruct((per_device, lanes), F32),
        ),
        in_specs=[HBM, HBM, HBM],
        out_specs=(VMEM, VMEM),
        scratch_shapes=[
            pltpu.VMEM((neighbours, total), jnp.int32),
            pltpu.VMEM((1, total), jnp.int32),
            pltpu.VMEM(couplings.shape, F32),
            pltpu.SemaphoreType.DMA((3,)),
        ],
        compiler_params=params,
        name="tables",
    )(coupled.T, pair_slot.reshape(1, total), couplings)

    def select(together, mask, flips, gathered):
        if not len(flips):
            return []

        def kernel(*refs):
            outs = [refs[2].at[i] for i in range(len(flips))] if together else refs[2:]
            select_kernel(capacity, per_device, orbitals, width, mask, list(flips), *refs[:2], *outs)

        shape = [block_shape] * len(flips)
        if together:
            shape = jax.ShapeDtypeStruct((len(flips), stride, width), BF16)
        return pl.pallas_call(
            kernel,
            out_shape=shape,
            in_specs=[SMEM, VMEM],
            out_specs=VMEM if together else [VMEM] * len(flips),
            compiler_params=small,
            name="select",
        )(send_index, gathered)

    def terms(before, close, far, first, flops):
        extra = [x for x in (before, close) if x is not None]
        return pl.pallas_call(
            functools.partial(
                terms_kernel, capacity, orbitals, before is not None, close is not None, first
            ),
            out_shape=terms_shape,
            in_specs=[SMEM, SMEM] + [VMEM] * (1 + len(extra) + len(far)),
            out_specs=VMEM,
            cost_estimate=cost(flops),
            compiler_params=params,
            name="terms",
        )(index, coefficients, intersections, *extra, *far)

    state = amplitudes
    groups = [[i + j for j in range(near)] for i in range(0, pair_count, near)]
    flips = range(near, pair_count)
    ends_of = [x for x in (len(flips) // 2,) if x > 0]
    early = ends_of[-1] if ends_of else 0
    for step in range(ITERS):
        last = step == ITERS - 1
        gathered = lax.all_gather(payload, "orb", axis=0, tiled=False)
        sent = select(False, ~0, flips, gathered)
        far = [
            lax.ppermute(block, "pairs", [(p, p ^ flip) for p in range(pair_count)])
            for flip, block in zip(flips, sent)
        ]
        outgoing = select(True, ~(near - 1), range(near), gathered)
        close = lax.all_to_all(
            outgoing, "pairs", split_axis=0, concat_axis=0, axis_index_groups=groups, tiled=True
        )
        partial, done = None, 0
        for stop in ends_of:
            partial = terms(partial, None, far[done:stop], near + done, EARLY)
            done = stop
        partial = terms(partial, close, [], 0, CLOSE)
        late = far[early:]
        second = jax.ShapeDtypeStruct(amplitudes.shape, F32) if last else payload_shape
        state, payload = pl.pallas_call(
            functools.partial(update_kernel, last, capacity, orbitals, near + early, len(late)),
            out_shape=(jax.ShapeDtypeStruct(amplitudes.shape, F32), second),
            in_specs=[SMEM, SMEM, SMEM] + [VMEM] * (6 + len(late)),
            out_specs=(VMEM, VMEM),
            compiler_params=params,
            name="update",
        )(
            index, coefficients, ends, intersections, partial, *late, state, integrals, energies, projector,
        )
    return state, payload


def solution(mesh):
    split = ("pairs", "orb")
    return jax.shard_map(
        body,
        mesh=mesh,
        in_specs=(
            P(split, None, None),
            P(split, None, None),
            P(split, None),
            P(split, None, None, None),
            P(split, None),
            P(split, None),
            P(split, None),
            P(),
            P(),
        ),
        out_specs=(P(split, None, None), P(split, None, None)),
        check_vma=False,
    )
```

time: 84.5 us -> 72.2 us (0.85)
  the two profiles are of different devices: /device:TPU:16 before, /device:TPU:0 now
where the time goes in v3:
time: 72.2 us; the launch traced here: 71.8 us
  starting transfers between devices  25.3 us (35%)
  Pallas kernels  17.5 us (24%)
  blocking collectives  15.8 us (22%)
  waiting for transfers between devices  8.36 us (12%)
  local copies, waits for them, and re-layouts  4.03 us (6%)
  between operations  0.8 us (1%)
    ppermute x8, starting transfers between devices, body(): lax.ppermute(block, 'pairs', [(p, p ^ flip) for p in range(pair_count)])  18.2 us
    all_gather x2, blocking collectives, body(): gathered = lax.all_gather(payload, 'orb', axis=0, tiled=False)  15.8 us
    all_to_all x2, starting transfers between devices, body(): lax.all_to_all(outgoing, 'pairs', split_axis=0, concat_axis=0, axis_index...  7.1 us
    pallas_call x4, Pallas kernels, terms(): pl.pallas_call(functools.partial(terms_kernel, capacity, orbitals, before...  6.08 us
    ppermute x8, waiting for transfers between devices, body(): lax.ppermute(block, 'pairs', [(p, p ^ flip) for p in range(pair_count)])  5.73 us
    pallas_call x4, Pallas kernels, select(): pl.pallas_call(kernel, out_shape=shape, in_specs=[SMEM, VMEM], out_specs=...  4.97 us
    unnamed x30, local copies, waits for them, and re-layouts  4.03 us
    pallas_call x2, Pallas kernels, body(): pl.pallas_call(functools.partial(update_kernel, last, capacity, orbitals,...  3.42 us
  transfers between devices with their start and end apart: 10, of which 7 were waited for; matrix products, arithmetic and copies ran while one was open for 0% of the time, Pallas kernels for 13%

profile of v3, /device:TPU:0, one launch (start us, length us, event | category | flops | bytes accessed | tf_op | source)
XLA Modules:
  0.0 71.8 jit_solution(9114524868484243655)
XLA Ops:
  0.6 2.7 %setup.1 = (bf16[528,128]{1,0:T(8,128)(2,1)}, s32[8,128]{1,0:T(8,128)}) custom-call(s32[2,4]{1,0:T(2,128)} %bitcast.11, f32[4,128,128]{2,1,0:T(8,128)} %refs_2_.1, f32[4,128]{1,0:T(4,128)} %refs_5_.3, s32[16,128]{1,0:T(8,128)} %bitcast.9, s32[1,128]{1,0:T(1,128)} %bitcast.14), custom_call_target="tpu_custom_call" | custom-call | tf_op jit(solution)/shard_map/setup/pallas_call | solution.py:341
  3.3 8.9 %all-gather = bf16[2112,128]{1,0:T(8,128)(2,1)S(1)} all-gather(bf16[528,128]{1,0:T(8,128)(2,1)} %get-tuple-element.19), channel_id=2, replica_groups=mesh['pairs'=8,'orb'=4] {'orb'}, dimensions={0}, use_global_device_ids=true | all-gather | bytes 675840 | tf_op jit(solution)/shard_map/all_gather | solution.py:415
  13.6 2.7 %collective-permute-start = (bf16[400,128]{1,0:T(8,128)(2,1)S(1)}, bf16[400,128]{1,0:T(8,128)(2,1)S(1)}, u32[]{:S(2)}, u32[]{:S(2)}) collective-permute-start(bf16[400,128]{1,0:T(8,128)(2,1)S(1)} %get-tuple-element.20), channel_id=1, source_target_pairs={{0,16},{4,20},{8,24},{12,28},{16,0},{20,4},{24,8},{28,12},{1,17},{... | collective-permute-start | bytes 307208 | tf_op jit(solution)/shard_map/ppermute | solution.py:418
  16.3 1.3 %collective-permute-start.1 = (bf16[400,128]{1,0:T(8,128)(2,1)S(1)}, bf16[400,128]{1,0:T(8,128)(2,1)S(1)}, u32[]{:S(2)}, u32[]{:S(2)}) collective-permute-start(bf16[400,128]{1,0:T(8,128)(2,1)S(1)} %get-tuple-element.21), channel_id=1, source_target_pairs={{0,20},{4,16},{8,28},{12,24},{16,4},{20,0},{24,12},{28,8},{1,21},{... | collective-permute-start | bytes 307208 | tf_op jit(solution)/shard_map/ppermute | solution.py:418
  17.6 1.5 %select.5 = bf16[4,400,128]{2,1,0:T(8,128)(2,1)} custom-call(s32[8,128]{1,0:T(8,128)S(1)} %copy-done.3, bf16[4,528,128]{2,1,0:T(8,128)(2,1)S(1)} %bitcast.6), custom_call_target="tpu_custom_call" | custom-call | tf_op jit(solution)/shard_map/select/pallas_call | solution.py:385
  19.1 3.5 %all-to-all-start = ((bf16[4,400,128]{2,1,0:T(8,128)(2,1)}), bf16[4,400,128]{2,1,0:T(8,128)(2,1)S(1)}, u32[]{:S(2)}, u32[]{:S(2)}) async-start(bf16[4,400,128]{2,1,0:T(8,128)(2,1)} %select.5), calls=%async_computation | async-start | bytes 819200 | tf_op jit(solution)/shard_map/all_to_all | solution.py:422
  22.5 4.0 %collective-permute-start.2 = (bf16[400,128]{1,0:T(8,128)(2,1)S(1)}, bf16[400,128]{1,0:T(8,128)(2,1)S(1)}, u32[]{:S(2)}, u32[]{:S(2)}) collective-permute-start(bf16[400,128]{1,0:T(8,128)(2,1)S(1)} %get-tuple-element.22), channel_id=1, source_target_pairs={{0,24},{4,28},{8,16},{12,20},{16,8},{20,12},{24,0},{28,4},{1,25},{... | collective-permute-start | bytes 307208 | tf_op jit(solution)/shard_map/ppermute | solution.py:418
  26.5 1.2 %collective-permute-start.3 = (bf16[400,128]{1,0:T(8,128)(2,1)S(1)}, bf16[400,128]{1,0:T(8,128)(2,1)S(1)}, u32[]{:S(2)}, u32[]{:S(2)}) collective-permute-start(bf16[400,128]{1,0:T(8,128)(2,1)S(1)} %get-tuple-element.23), channel_id=1, source_target_pairs={{0,28},{4,24},{8,20},{12,16},{16,12},{20,8},{24,4},{28,0},{1,29},{... | collective-permute-start | bytes 307208 | tf_op jit(solution)/shard_map/ppermute | solution.py:418
  28.2 1.3 %terms.4.refs_0_ = f32[520,128]{1,0:T(8,128)S(1)} custom-call(s32[4,128]{1,0:T(4,128)S(1)} %get-tuple-element.16.index, f32[4,128]{1,0:T(4,128)S(1)} %get-tuple-element.17.coefficients, bf16[4,16,128,128]{3,2,1,0:T(8,128)(2,1)S(1)} %copy-done, bf16[400,128]{1,0:T(8,128)(2,1)S(1)} %collective-permute-done.refs_0_, ...), custom_call_target="tpu_custom_call" | custom-call | flops 20000000000 | tf_op jit(solution)/shard_map/terms/pallas_call | solution.py:396
  30.2 1.2 %all-to-all-done.refs_1_ = bf16[4,400,128]{2,1,0:T(8,128)(2,1)S(1)} async-done(((bf16[4,400,128]{2,1,0:T(8,128)(2,1)}), bf16[4,400,128]{2,1,0:T(8,128)(2,1)S(1)}, u32[]{:S(2)}, u32[]{:S(2)}) %all-to-all-start) | async-done | bytes 409632 | tf_op jit(solution)/shard_map/all_to_all | solution.py:422
  32.3 1.6 %terms.5.before = f32[520,128]{1,0:T(8,128)S(1)} custom-call(s32[4,128]{1,0:T(4,128)S(1)} %get-tuple-element.16.index, f32[4,128]{1,0:T(4,128)S(1)} %get-tuple-element.17.coefficients, bf16[4,16,128,128]{3,2,1,0:T(8,128)(2,1)S(1)} %copy-done, f32[520,128]{1,0:T(8,128)S(1)} %copy-done.12, bf16[4,400,128]{2,1,0:T(8,128)(2,1)S(1)} %all-to-all-done.refs_1_), custom_call_target="tpu_custom_call" | custom-call | flops 1000000000 | tf_op jit(solution)/shard_map/terms/pallas_call | solution.py:396
  34.8 2.0 %collective-permute-done.3.refs_1_ = bf16[400,128]{1,0:T(8,128)(2,1)S(1)} collective-permute-done((bf16[400,128]{1,0:T(8,128)(2,1)S(1)}, bf16[400,128]{1,0:T(8,128)(2,1)S(1)}, u32[]{:S(2)}, u32[]{:S(2)}) %collective-permute-start.3) | collective-permute-done | bytes 102432 | tf_op jit(solution)/shard_map/ppermute | solution.py:418
  36.9 1.4 %update.2 = (f32[4,128,128]{2,1,0:T(8,128)S(1)}, bf16[528,128]{1,0:T(8,128)(2,1)S(1)}) custom-call(s32[4,128]{1,0:T(4,128)S(1)} %get-tuple-element.16.index, f32[4,128]{1,0:T(4,128)S(1)} %get-tuple-element.17.coefficients, s32[2,4]{1,0:T(2,128)S(1)} %bitcast.12, bf16[4,16,128,128]{3,2,1,0:T(8,128)(2,1)S(1)} %copy-done, f32[520,128]{1,0:T(8,128)S(1)} %terms.5.before, ...), custom_call_target="tpu_custom_call" | custom-call | tf_op jit(solution)/shard_map/update/pallas_call | solution.py:432
  38.2 6.9 %all-gather.1 = bf16[2112,128]{1,0:T(8,128)(2,1)S(1)} all-gather(bf16[528,128]{1,0:T(8,128)(2,1)S(1)} %get-tuple-element.24), channel_id=3, replica_groups=mesh['pairs'=8,'orb'=4] {'orb'}, dimensions={0}, use_global_device_ids=true | all-gather | bytes 675840 | tf_op jit(solution)/shard_map/all_gather | solution.py:415
  45.1 1.3 %select.6 = (bf16[400,128]{1,0:T(8,128)(2,1)}, bf16[400,128]{1,0:T(8,128)(2,1)S(1)}, bf16[400,128]{1,0:T(8,128)(2,1)S(1)}, bf16[400,128]{1,0:T(8,128)(2,1)S(1)}) custom-call(s32[8,128]{1,0:T(8,128)S(1)} %copy-done.4, bf16[4,528,128]{2,1,0:T(8,128)(2,1)S(1)} %bitcast.7), custom_call_target="tpu_custom_call" | custom-call | tf_op jit(solution)/shard_map/select/pallas_call | solution.py:385
  46.4 2.8 %collective-permute-start.4 = (bf16[400,128]{1,0:T(8,128)(2,1)}, bf16[400,128]{1,0:T(8,128)(2,1)}, u32[]{:S(2)}, u32[]{:S(2)}) collective-permute-start(bf16[400,128]{1,0:T(8,128)(2,1)} %get-tuple-element.25), channel_id=1, source_target_pairs={{0,16},{4,20},{8,24},{12,28},{16,0},{20,4},{24,8},{28,12},{1,17},{... | collective-permute-start | bytes 307208 | tf_op jit(solution)/shard_map/ppermute | solution.py:418
  50.2 1.5 %select.7 = bf16[4,400,128]{2,1,0:T(8,128)(2,1)} custom-call(s32[8,128]{1,0:T(8,128)S(1)} %copy-done.4, bf16[4,528,128]{2,1,0:T(8,128)(2,1)S(1)} %bitcast.8), custom_call_target="tpu_custom_call" | custom-call | tf_op jit(solution)/shard_map/select/pallas_call | solution.py:385
  51.6 3.6 %all-to-all-start.1 = ((bf16[4,400,128]{2,1,0:T(8,128)(2,1)}), bf16[4,400,128]{2,1,0:T(8,128)(2,1)S(1)}, u32[]{:S(2)}, u32[]{:S(2)}) async-start(bf16[4,400,128]{2,1,0:T(8,128)(2,1)} %select.7), calls=%async_computation.1 | async-start | bytes 819200 | tf_op jit(solution)/shard_map/all_to_all | solution.py:422
  55.3 4.6 %collective-permute-start.6 = (bf16[400,128]{1,0:T(8,128)(2,1)S(1)}, bf16[400,128]{1,0:T(8,128)(2,1)S(1)}, u32[]{:S(2)}, u32[]{:S(2)}) collective-permute-start(bf16[400,128]{1,0:T(8,128)(2,1)S(1)} %get-tuple-element.27), channel_id=1, source_target_pairs={{0,24},{4,28},{8,16},{12,20},{16,8},{20,12},{24,0},{28,4},{1,25},{... | collective-permute-start | bytes 307208 | tf_op jit(solution)/shard_map/ppermute | solution.py:418
  60.7 1.6 %terms.6.refs_0_ = f32[520,128]{1,0:T(8,128)S(1)} custom-call(s32[4,128]{1,0:T(4,128)S(1)} %get-tuple-element.16.index, f32[4,128]{1,0:T(4,128)S(1)} %get-tuple-element.17.coefficients, bf16[4,16,128,128]{3,2,1,0:T(8,128)(2,1)S(1)} %copy-done, bf16[400,128]{1,0:T(8,128)(2,1)} %collective-permute-done.4.refs_0_, bf16[400,128]{1,0:T(8,128)(2,1)} %collective-permute-done.5.refs_1_), custom_call_target="tpu_custom_call" | custom-call | flops 20000000000 | tf_op jit(solution)/shard_map/terms/pallas_call | solution.py:396
  63.1 1.4 %all-to-all-done.1.refs_1_ = bf16[4,400,128]{2,1,0:T(8,128)(2,1)S(1)} async-done(((bf16[4,400,128]{2,1,0:T(8,128)(2,1)}), bf16[4,400,128]{2,1,0:T(8,128)(2,1)S(1)}, u32[]{:S(2)}, u32[]{:S(2)}) %all-to-all-start.1) | async-done | bytes 409632 | tf_op jit(solution)/shard_map/all_to_all | solution.py:422
  65.5 1.6 %terms.7.before = f32[520,128]{1,0:T(8,128)S(1)} custom-call(s32[4,128]{1,0:T(4,128)S(1)} %get-tuple-element.16.index, f32[4,128]{1,0:T(4,128)S(1)} %get-tuple-element.17.coefficients, bf16[4,16,128,128]{3,2,1,0:T(8,128)(2,1)S(1)} %copy-done, f32[520,128]{1,0:T(8,128)S(1)} %copy-done.14, bf16[4,400,128]{2,1,0:T(8,128)(2,1)S(1)} %all-to-all-done.1.refs_1_), custom_call_target="tpu_custom_call" | custom-call | flops 1000000000 | tf_op jit(solution)/shard_map/terms/pallas_call | solution.py:396
  68.2 1.6 %collective-permute-done.7.refs_1_ = bf16[400,128]{1,0:T(8,128)(2,1)S(1)} collective-permute-done((bf16[400,128]{1,0:T(8,128)(2,1)S(1)}, bf16[400,128]{1,0:T(8,128)(2,1)S(1)}, u32[]{:S(2)}, u32[]{:S(2)}) %collective-permute-start.7) | collective-permute-done | bytes 102432 | tf_op jit(solution)/shard_map/ppermute | solution.py:418
  69.7 2.1 %update.3 = (f32[4,128,128]{2,1,0:T(8,128)}, f32[4,128,128]{2,1,0:T(8,128)}) custom-call(s32[4,128]{1,0:T(4,128)S(1)} %get-tuple-element.16.index, f32[4,128]{1,0:T(4,128)S(1)} %get-tuple-element.17.coefficients, s32[2,4]{1,0:T(2,128)S(1)} %bitcast.13, bf16[4,16,128,128]{3,2,1,0:T(8,128)(2,1)S(1)} %copy-done, f32[520,128]{1,0:T(8,128)S(1)} %terms.7.before, ...), custom_call_target="tpu_custom_call" | custom-call | tf_op jit(solution)/shard_map/update/pallas_call | solution.py:432
  (40 shorter events, 8.9 us)
Async XLA Ops:
  0.6 27.5 %copy-start = (bf16[4,16,128,128]{3,2,1,0:T(8,128)(2,1)S(1)}, bf16[4,16,128,128]{3,2,1,0:T(8,128)(2,1)}, u32[]{:S(2)}) copy-start(bf16[4,16,128,128]{3,2,1,0:T(8,128)(2,1)} %intersections.11) | copy-start | bytes 6291460
  12.9 14.8 %copy-start.5 = (s32[128,16]{0,1:T(8,128)S(1)}, s32[128,16]{0,1:T(8,128)}, u32[]{:S(2)}) copy-start(s32[128,16]{0,1:T(8,128)} %param.16) | copy-start | bytes 24580
  12.9 14.8 %copy-start.9 = (s32[128]{0:T(128)S(1)}, s32[128]{0:T(128)}, u32[]{:S(2)}) copy-start(s32[128]{0:T(128)} %param.17) | copy-start | bytes 1540
  12.9 14.8 %copy-start.10 = (f32[4,16]{1,0:T(4,128)S(1)}, f32[4,16]{1,0:T(4,128)}, u32[]{:S(2)}) copy-start(f32[4,16]{1,0:T(4,128)} %couplings_hbm.1) | copy-start | bytes 772
  13.6 14.5 %collective-permute-start = (bf16[400,128]{1,0:T(8,128)(2,1)S(1)}, bf16[400,128]{1,0:T(8,128)(2,1)S(1)}, u32[]{:S(2)}, u32[]{:S(2)}) collective-permute-start(bf16[400,128]{1,0:T(8,128)(2,1)S(1)} %get-tuple-element.20), channel_id=1, source_target_pairs={{0,16},{4,20},{8,24},{12,28},{16,0},{20,4},{24,8},{28,12},{1,17},{... | collective-permute-start | bytes 307208 | tf_op jit(solution)/shard_map/ppermute | solution.py:418
  16.3 11.9 %collective-permute-start.1 = (bf16[400,128]{1,0:T(8,128)(2,1)S(1)}, bf16[400,128]{1,0:T(8,128)(2,1)S(1)}, u32[]{:S(2)}, u32[]{:S(2)}) collective-permute-start(bf16[400,128]{1,0:T(8,128)(2,1)S(1)} %get-tuple-element.21), channel_id=1, source_target_pairs={{0,20},{4,16},{8,28},{12,24},{16,4},{20,0},{24,12},{28,8},{1,21},{... | collective-permute-start | bytes 307208 | tf_op jit(solution)/shard_map/ppermute | solution.py:418
  19.1 12.3 %all-to-all-start = ((bf16[4,400,128]{2,1,0:T(8,128)(2,1)}), bf16[4,400,128]{2,1,0:T(8,128)(2,1)S(1)}, u32[]{:S(2)}, u32[]{:S(2)}) async-start(bf16[4,400,128]{2,1,0:T(8,128)(2,1)} %select.5), calls=%async_computation | async-start | bytes 819200 | tf_op jit(solution)/shard_map/all_to_all | solution.py:422
  22.5 12.3 %collective-permute-start.2 = (bf16[400,128]{1,0:T(8,128)(2,1)S(1)}, bf16[400,128]{1,0:T(8,128)(2,1)S(1)}, u32[]{:S(2)}, u32[]{:S(2)}) collective-permute-start(bf16[400,128]{1,0:T(8,128)(2,1)S(1)} %get-tuple-element.22), channel_id=1, source_target_pairs={{0,24},{4,28},{8,16},{12,20},{16,8},{20,12},{24,0},{28,4},{1,25},{... | collective-permute-start | bytes 307208 | tf_op jit(solution)/shard_map/ppermute | solution.py:418
  26.5 10.3 %collective-permute-start.3 = (bf16[400,128]{1,0:T(8,128)(2,1)S(1)}, bf16[400,128]{1,0:T(8,128)(2,1)S(1)}, u32[]{:S(2)}, u32[]{:S(2)}) collective-permute-start(bf16[400,128]{1,0:T(8,128)(2,1)S(1)} %get-tuple-element.23), channel_id=1, source_target_pairs={{0,28},{4,24},{8,20},{12,16},{16,12},{20,8},{24,4},{28,0},{1,29},{... | collective-permute-start | bytes 307208 | tf_op jit(solution)/shard_map/ppermute | solution.py:418
  29.5 0.7 copy-start.11
  30.2 6.7 %copy-start.1 = (f32[4,128,128]{2,1,0:T(8,128)S(1)}, f32[4,128,128]{2,1,0:T(8,128)}, u32[]{:S(2)}) copy-start(f32[4,128,128]{2,1,0:T(8,128)} %refs_2_.1) | copy-start | bytes 786436
  30.2 6.7 %copy-start.2 = (bf16[4,128,128]{2,1,0:T(8,128)(2,1)S(1)}, bf16[4,128,128]{2,1,0:T(8,128)(2,1)}, u32[]{:S(2)}) copy-start(bf16[4,128,128]{2,1,0:T(8,128)(2,1)} %refs_3_.3) | copy-start | bytes 393220
  30.2 6.7 %copy-start.6 = (f32[4,128]{1,0:T(4,128)S(1)}, f32[4,128]{1,0:T(4,128)}, u32[]{:S(2)}) copy-start(f32[4,128]{1,0:T(4,128)} %refs_5_.3) | copy-start | bytes 6148
  30.2 6.7 %copy-start.7 = (s32[4,2]{0,1:T(2,128)S(1)}, s32[4,2]{0,1:T(2,128)}, u32[]{:S(2)}) copy-start(s32[4,2]{0,1:T(2,128)} %param.15) | copy-start | bytes 100
  30.2 6.7 %copy-start.8 = (f32[4,128]{1,0:T(4,128)S(1)}, f32[4,128]{1,0:T(4,128)}, u32[]{:S(2)}) copy-start(f32[4,128]{1,0:T(4,128)} %refs_4_.3) | copy-start | bytes 6148
  31.4 1.0 %copy-start.12 = (f32[520,128]{1,0:T(8,128)S(1)}, f32[520,128]{1,0:T(8,128)}, u32[]{:S(2)}) copy-start(f32[520,128]{1,0:T(8,128)} %copy-done.11) | copy-start | bytes 798724
  33.9 11.2 %copy-start.4 = (s32[8,128]{1,0:T(8,128)S(1)}, s32[8,128]{1,0:T(8,128)}, u32[]{:S(2)}) copy-start(s32[8,128]{1,0:T(8,128)} %get-tuple-element.18.refs_0_) | copy-start | bytes 12292
  46.4 14.1 %collective-permute-start.4 = (bf16[400,128]{1,0:T(8,128)(2,1)}, bf16[400,128]{1,0:T(8,128)(2,1)}, u32[]{:S(2)}, u32[]{:S(2)}) collective-permute-start(bf16[400,128]{1,0:T(8,128)(2,1)} %get-tuple-element.25), channel_id=1, source_target_pairs={{0,16},{4,20},{8,24},{12,28},{16,0},{20,4},{24,8},{28,12},{1,17},{... | collective-permute-start | bytes 307208 | tf_op jit(solution)/shard_map/ppermute | solution.py:418
  49.2 11.5 %collective-permute-start.5 = (bf16[400,128]{1,0:T(8,128)(2,1)S(1)}, bf16[400,128]{1,0:T(8,128)(2,1)}, u32[]{:S(2)}, u32[]{:S(2)}) collective-permute-start(bf16[400,128]{1,0:T(8,128)(2,1)S(1)} %get-tuple-element.26), channel_id=1, source_target_pairs={{0,20},{4,16},{8,28},{12,24},{16,4},{20,0},{24,12},{28,8},{1,21},{... | collective-permute-start | bytes 307208 | tf_op jit(solution)/shard_map/ppermute | solution.py:418
  51.6 12.9 %all-to-all-start.1 = ((bf16[4,400,128]{2,1,0:T(8,128)(2,1)}), bf16[4,400,128]{2,1,0:T(8,128)(2,1)S(1)}, u32[]{:S(2)}, u32[]{:S(2)}) async-start(bf16[4,400,128]{2,1,0:T(8,128)(2,1)} %select.7), calls=%async_computation.1 | async-start | bytes 819200 | tf_op jit(solution)/shard_map/all_to_all | solution.py:422
  55.3 12.9 %collective-permute-start.6 = (bf16[400,128]{1,0:T(8,128)(2,1)S(1)}, bf16[400,128]{1,0:T(8,128)(2,1)S(1)}, u32[]{:S(2)}, u32[]{:S(2)}) collective-permute-start(bf16[400,128]{1,0:T(8,128)(2,1)S(1)} %get-tuple-element.27), channel_id=1, source_target_pairs={{0,24},{4,28},{8,16},{12,20},{16,8},{20,12},{24,0},{28,4},{1,25},{... | collective-permute-start | bytes 307208 | tf_op jit(solution)/shard_map/ppermute | solution.py:418
  59.9 9.8 %collective-permute-start.7 = (bf16[400,128]{1,0:T(8,128)(2,1)S(1)}, bf16[400,128]{1,0:T(8,128)(2,1)S(1)}, u32[]{:S(2)}, u32[]{:S(2)}) collective-permute-start(bf16[400,128]{1,0:T(8,128)(2,1)S(1)} %get-tuple-element.28), channel_id=1, source_target_pairs={{0,28},{4,24},{8,20},{12,16},{16,12},{20,8},{24,4},{28,0},{1,29},{... | collective-permute-start | bytes 307208 | tf_op jit(solution)/shard_map/ppermute | solution.py:418
  62.4 0.7 copy-start.13
  64.5 1.0 %copy-start.14 = (f32[520,128]{1,0:T(8,128)S(1)}, f32[520,128]{1,0:T(8,128)}, u32[]{:S(2)}) copy-start(f32[520,128]{1,0:T(8,128)} %copy-done.13) | copy-start | bytes 798724
  (1 other events, 0.7 us)

commit v4 on v3

v4 whole, which is shorter than its diff:
```python
import functools

import jax
import jax.numpy as jnp
from jax import lax
from jax.experimental import pallas as pl
from jax.experimental.pallas import tpu as pltpu
from jax.sharding import PartitionSpec as P

PAIRS_ORB = 32
ITERS = 2
ROWS = 16
PARTS = 3
EARLY = 20_000_000_000
CLOSE = 1_000_000_000

F32 = jnp.float32
BF16 = jnp.bfloat16
VMEM = pl.BlockSpec(memory_space=pltpu.VMEM)
SMEM = pl.BlockSpec(memory_space=pltpu.SMEM)
ANY = pl.BlockSpec(memory_space=pl.ANY)
HBM = pl.BlockSpec(memory_space=pltpu.HBM)
LIMIT = 16 * 1024 * 1024
SMALL = 8 * 1024 * 1024
WHOLE = 60 * 1024 * 1024


def eye_mask(width):
    rows = lax.broadcasted_iota(jnp.int32, (width, width), 0)
    cols = lax.broadcasted_iota(jnp.int32, (width, width), 1)
    return rows == cols


def to_row(column, eye):
    return jnp.sum(jnp.where(eye, column, 0.0), axis=0, keepdims=True)


def to_column(row, eye):
    return jnp.sum(jnp.where(eye, row, 0.0), axis=1, keepdims=True)


def split_parts(value):
    parts = []
    for _ in range(PARTS):
        part = value.astype(BF16)
        parts.append(part)
        value = value - part.astype(F32)
    return parts


def tail_rows(value, rows):
    parts = split_parts(value)
    missing = rows - sum(part.shape[0] for part in parts)
    if missing:
        parts.append(jnp.zeros((missing, value.shape[1]), BF16))
    return jnp.concatenate([part.astype(F32) for part in parts], axis=0).astype(BF16)


def join_parts(rows, orbitals):
    rows = rows.astype(F32)
    value = rows[:orbitals]
    for part in range(1, PARTS):
        value = value + rows[part * orbitals : (part + 1) * orbitals]
    return value


def singles_terms(state, projector_row, count, eye):
    projected = to_row(jnp.sum(state * projector_row, axis=1, keepdims=True), eye)
    return count * projected


def end_counts(orbitals, per_device, end):
    ids = lax.broadcasted_iota(jnp.int32, (orbitals, 1), 0)
    return [(ids == end(s)).astype(F32) for s in range(per_device)]


def fetch(pairs, sems):
    copies = [pltpu.make_async_copy(src, dst, sems.at[i]) for i, (src, dst) in enumerate(pairs)]
    for copy in copies:
        copy.start()
    return copies


def setup_kernel(
    capacity, orbitals, near, mirrors,
    ends, state_hbm, projector_hbm, coupled_hbm, slot_hbm, couplings_hbm,
    payload, index, table, coefficients,
    state, projector, coupled, slot, couplings, sems,
):
    copies = fetch(
        (
            (coupled_hbm, coupled), (slot_hbm, slot), (projector_hbm, projector), (state_hbm, state),
            (couplings_hbm, couplings),
        ),
        sems,
    )
    per_device, width = state.shape[0], state.shape[1]
    count = slot.shape[1]
    pair_count, orb_count = lax.axis_size("pairs"), lax.axis_size("orb")
    pair_idx, orb_idx = lax.axis_index("pairs"), lax.axis_index("orb")
    group = orb_count * per_device
    lanes_out = index.shape[1]
    copies[0].wait()
    copies[1].wait()
    slots = slot[...]
    wanted = coupled[...]
    lanes = lax.broadcasted_iota(jnp.int32, (1, count), 1)
    members = lax.broadcasted_iota(jnp.int32, (group, 1), 0)
    slot_ids = lax.broadcasted_iota(jnp.int32, (count, lanes_out), 0)
    dest = lax.broadcasted_iota(jnp.int32, (count, lanes_out), 1)
    owner = (slot_ids // per_device == dest * orb_count + orb_idx) & (dest < pair_count)
    for m, flip in enumerate(mirrors):
        base = (pair_idx ^ flip) * group
        pairs = jnp.sum(jnp.where(slots == base + members, lanes, 0), axis=1, keepdims=True)
        hits = jnp.zeros((group, count), F32)
        for g in range(group):
            hit = jnp.max((wanted == pairs[g : g + 1, :]).astype(F32), axis=0, keepdims=True)
            hits = jnp.where(members == g, hit, hits)
        needed = jnp.dot(hits, owner.astype(F32), preferred_element_type=F32) > 0.5
        run = jnp.zeros((1, lanes_out), jnp.int32)
        picked = [jnp.zeros((1, lanes_out), jnp.int32) for _ in range(capacity)]
        for g in range(group):
            hit = needed[g : g + 1, :].astype(jnp.int32)
            for c in range(capacity):
                picked[c] = picked[c] + jnp.where((hit == 1) & (run == c), g, 0)
            run = run + hit
        for c, row in enumerate(picked):
            index[pl.ds(m * capacity + c, 1), :] = row

    eye = eye_mask(count)
    slots_c = jnp.sum(jnp.where(eye, slots, 0), axis=1, keepdims=True)
    first = (pair_idx * orb_count + orb_idx) * per_device
    entries = []
    mine = jnp.zeros((1, count), F32)
    for i in range(per_device):
        own = jnp.sum(jnp.where(lanes == first + i, wanted, 0), axis=1, keepdims=True)
        entries.append((own == lanes).astype(F32))
        mine = jnp.maximum(mine, jnp.max(entries[i], axis=0, keepdims=True))
    mine_c = to_column(mine, eye)
    before = (slots_c // group == slots // group) & (slots_c < slots)
    rank = jnp.sum(jnp.where(before, mine_c, 0.0), axis=0, keepdims=True).astype(jnp.int32)
    source = slots // group
    flip = source ^ pair_idx
    place = jnp.where(flip < near, source ^ (pair_idx & ~(near - 1)), flip) * capacity + rank
    place = place.astype(F32)
    neighbours = coupled.shape[0]
    ids = lax.broadcasted_iota(jnp.int32, (neighbours, 1), 0)
    square = eye_mask(neighbours)
    column = lax.broadcasted_iota(jnp.int32, (neighbours, lanes_out), 1)
    copies[4].wait()
    for i in range(per_device):
        found = jnp.sum(entries[i] * place, axis=1, keepdims=True).astype(jnp.int32)
        match = found == column
        table[pl.ds(i, 1), :] = jnp.sum(jnp.where(match, ids, 0), axis=0, keepdims=True)
        value = to_column(couplings[pl.ds(i, 1), :], square)
        coefficients[pl.ds(i, 1), :] = jnp.sum(jnp.where(match, value, 0.0), axis=0, keepdims=True)

    eye = eye_mask(width)
    copies[2].wait()
    copies[3].wait()
    total = jnp.zeros((orbitals, width), F32)
    counts_a = end_counts(orbitals, per_device, lambda s: ends[0, s])
    counts_b = end_counts(orbitals, per_device, lambda s: ends[1, s])
    for s in range(per_device):
        block = state[s]
        payload[pl.ds(s * width, width), :] = block.astype(BF16)
        total += singles_terms(block, projector[pl.ds(s, 1), :], counts_a[s] + counts_b[s], eye)
    tail = payload.shape[0] - per_device * width
    payload[pl.ds(per_device * width, tail), :] = tail_rows(total, tail)


def select_kernel(capacity, per_device, orbitals, width, dests, row, swap, index, gathered, outs):
    blocks = per_device * width
    tail = gathered.shape[1] - blocks
    total = join_parts(gathered[0, pl.ds(blocks, tail), :], orbitals)
    for d in range(1, gathered.shape[0]):
        total += join_parts(gathered[d, pl.ds(blocks, tail), :], orbitals)
    rows = tail_rows(total, tail)
    for dest, out in zip(dests, outs):
        for c in range(capacity):
            j = index[row + c, dest]
            first = pl.multiple_of((j % per_device) * width, ROWS)
            out[pl.ds(c * width, width), :] = gathered[(j // per_device) ^ swap, pl.ds(first, width), :]
        out[pl.ds(capacity * width, tail), :] = rows


def add_blocks(capacity, orbitals, index, coefficients, intersections, blocks, coupling, singles):
    per_device, width = intersections.shape[0], intersections.shape[2]
    slots = [(place * capacity + c, ref, c * width) for place, ref in blocks for c in range(capacity)]
    wide = [[] for _ in range(per_device)]
    scaled = [[] for _ in range(per_device)]
    empty = jnp.zeros((width, width), BF16)
    for p in range(0, len(slots), 2):
        part = slots[p : p + 2]
        mixing = [
            jnp.concatenate([intersections[s, index[s, lane]] for lane, _, _ in part], axis=1)
            for s in range(per_device)
        ]
        near = [ref[pl.ds(row, width), :] for _, ref, row in part]
        if len(part) == 2:
            near = jnp.concatenate(
                [jnp.concatenate([near[0], empty], axis=1), jnp.concatenate([empty, near[1]], axis=1)], axis=0
            )
        else:
            near = near[0]
        lifted = jnp.dot(jnp.concatenate(mixing, axis=0), near, preferred_element_type=F32)
        for s in range(per_device):
            wide[s].append(mixing[s])
            for i, (lane, _, _) in enumerate(part):
                block = lifted[s * width : (s + 1) * width, i * width : (i + 1) * width]
                scaled[s].append((coefficients[s, lane] * block).astype(BF16))
    for s in range(per_device):
        if slots:
            coupling[s] = coupling[s] + lax.dot_general(
                jnp.concatenate(scaled[s], axis=1), jnp.concatenate(wide[s], axis=1),
                (((1,), (1,)), ((), ())), preferred_element_type=F32,
            )
    for _, ref in blocks:
        tail = ref.shape[0] - capacity * width
        singles = singles + join_parts(ref[pl.ds(capacity * width, tail), :], orbitals)
    return singles


def gather_terms(capacity, orbitals, index, coefficients, intersections, every, places, blocks, before):
    per_device, width = intersections.shape[0], intersections.shape[2]
    coupling = [jnp.zeros((width, width), F32) for _ in range(per_device)]
    singles = jnp.zeros((orbitals, width), F32)
    if before is not None:
        coupling = [before[pl.ds(s * width, width), :] for s in range(per_device)]
        singles = before[pl.ds(per_device * width, orbitals), :]
    operands = (capacity, orbitals, index, coefficients, intersections)
    if every is not None:
        unit = min(every.shape[0], 4)

        def step(i, carry):
            parts = list(carry[:-1])
            some = [(i * unit + u, every.at[i * unit + u]) for u in range(unit)]
            total = add_blocks(*operands, some, parts, carry[-1])
            return (*parts, total)

        *coupling, singles = lax.fori_loop(0, every.shape[0] // unit, step, (*coupling, singles))
    singles = add_blocks(*operands, list(zip(places, blocks)), coupling, singles)
    return coupling, singles


def terms_kernel(
    capacity, orbitals, has_before, has_every, places, index, coefficients, intersections, *refs
):
    out = refs[-1]
    refs = list(refs[:-1])
    before = refs.pop(0) if has_before else None
    every = refs.pop(0) if has_every else None
    coupling, singles = gather_terms(
        capacity, orbitals, index, coefficients, intersections, every, places, refs, before
    )
    width = intersections.shape[2]
    for s, part in enumerate(coupling):
        out[pl.ds(s * width, width), :] = part
    out[pl.ds(len(coupling) * width, orbitals), :] = singles


def update_kernel(
    last, capacity, orbitals, places,
    index, coefficients, ends, intersections, before, *refs,
):
    blocks = refs[: len(places)]
    state, integrals, energies, projector, out_a, out_b = refs[len(places) :]
    per_device, width = state.shape[0], state.shape[1]
    coupling, singles = gather_terms(
        capacity, orbitals, index, coefficients, intersections, None, places, blocks, before
    )
    eye = eye_mask(width)
    total = jnp.zeros((orbitals, width), F32)
    counts_a = end_counts(orbitals, per_device, lambda s: ends[0, s])
    counts_b = end_counts(orbitals, per_device, lambda s: ends[1, s])
    for s in range(per_device):
        old = state[s]
        energy = energies[pl.ds(s, 1), :]
        energy_c = to_column(energy, eye)
        proj = projector[pl.ds(s, 1), :]
        proj_c = to_column(proj, eye)
        left = jnp.sum(counts_a[s] * singles, axis=0, keepdims=True)
        right = jnp.sum(counts_b[s] * singles, axis=0, keepdims=True)
        residual = (
            integrals[s].astype(F32) + energy_c * old + old * energy - coupling[s]
            + to_column(left, eye) * proj + proj_c * right
        )
        new = old - residual / (energy_c + energy)
        out_a[s] = new
        if last:
            out_b[s] = residual
        else:
            out_b[pl.ds(s * width, width), :] = new.astype(BF16)
            total += singles_terms(new, proj, counts_a[s] + counts_b[s], eye)
    if not last:
        tail = out_b.shape[0] - per_device * width
        out_b[pl.ds(per_device * width, tail), :] = tail_rows(total, tail)


def tail_size(orbitals):
    return -(-PARTS * orbitals // ROWS) * ROWS


def cost(flops):
    return pl.CostEstimate(flops=flops, bytes_accessed=0, transcendentals=0)


def body(
    amplitudes, integrals, energies, intersections, couplings, projector, pair_orbitals, coupled, pair_slot,
):
    pair_count = lax.axis_size("pairs")
    per_device, width = amplitudes.shape[0], amplitudes.shape[1]
    total, neighbours = coupled.shape
    capacity = 1 + neighbours // pair_count
    orbitals = total // PAIRS_ORB
    tail = tail_size(orbitals)
    stride = capacity * width + tail
    orb_count = lax.axis_size("orb")
    direct = pair_count in (4, 8) and orb_count == 4
    half = pair_count // 2
    mirrors = [0, half] if direct else [0]
    near = 1 if direct else pair_count
    lanes = -(-pair_count * capacity // 128) * 128
    ends = pair_orbitals.T
    small = pltpu.CompilerParams(vmem_limit_bytes=SMALL)
    params = pltpu.CompilerParams(vmem_limit_bytes=LIMIT)
    block_shape = jax.ShapeDtypeStruct((stride, width), BF16)
    terms_shape = jax.ShapeDtypeStruct((per_device * width + -(-orbitals // 8) * 8, width), F32)
    payload_shape = jax.ShapeDtypeStruct((per_device * width + tail, width), BF16)
    payload, send_index, index, coefficients = pl.pallas_call(
        functools.partial(setup_kernel, capacity, orbitals, near, mirrors),
        out_shape=(
            payload_shape,
            jax.ShapeDtypeStruct((-(-len(mirrors) * capacity // 8) * 8, lanes), jnp.int32),
            jax.ShapeDtypeStruct((per_device, lanes), jnp.int32),
            jax.ShapeDtypeStruct((per_device, lanes), F32),
        ),
        in_specs=[SMEM] + [HBM] * 5,
        out_specs=[VMEM] * 4,
        scratch_shapes=[
            pltpu.VMEM(amplitudes.shape, F32),
            pltpu.VMEM(projector.shape, F32),
            pltpu.VMEM((neighbours, total), jnp.int32),
            pltpu.VMEM((1, total), jnp.int32),
            pltpu.VMEM(couplings.shape, F32),
            pltpu.SemaphoreType.DMA((5,)),
        ],
        compiler_params=pltpu.CompilerParams(vmem_limit_bytes=WHOLE),
        name="setup",
    )(ends, amplitudes, projector, coupled.T, pair_slot.reshape(1, total), couplings)

    def join(*parts, after=()):
        def kernel(*refs):
            for i in range(len(parts)):
                refs[-1][i] = refs[i][...]

        return pl.pallas_call(
            kernel,
            out_shape=jax.ShapeDtypeStruct((len(parts), *payload_shape.shape), BF16),
            in_specs=[VMEM] * len(parts) + [ANY] * len(after),
            out_specs=VMEM,
            compiler_params=small,
            cost_estimate=cost(0),
            name="join",
        )(*parts, *after)

    def select(row, flips, gathered):
        def kernel(index, source, *refs):
            outs = refs[: len(flips)]
            here, swap = lax.axis_index("pairs"), 0
            if row:
                held, source, swap = source, refs[-1], lax.axis_index("orb") // 2 * 2
                for c in range(2):
                    for x in range(2):
                        source[2 * x + c] = held[c, x]
            dests = [here ^ flip for flip in flips]
            select_kernel(capacity, per_device, orbitals, width, dests, row, swap, index, source, outs)

        return pl.pallas_call(
            kernel,
            out_shape=[block_shape] * len(flips),
            in_specs=[SMEM, VMEM],
            out_specs=[VMEM] * len(flips),
            scratch_shapes=[pltpu.VMEM((4, *payload_shape.shape), BF16)] if row else [],
            compiler_params=small,
            cost_estimate=cost(0),
            name="select",
        )(send_index, gathered)

    def select_all(gathered):
        def kernel(index, source, out):
            outs = [out.at[i] for i in range(pair_count)]
            select_kernel(capacity, per_device, orbitals, width, range(pair_count), 0, 0, index, source, outs)

        return pl.pallas_call(
            kernel,
            out_shape=jax.ShapeDtypeStruct((pair_count, stride, width), BF16),
            in_specs=[SMEM, VMEM],
            out_specs=VMEM,
            compiler_params=small,
            name="select",
        )(send_index, gathered)

    def exchange(block, axis, flip):
        return lax.ppermute(block, axis, [(p, p ^ flip) for p in range(pair_count * orb_count if isinstance(axis, tuple) else lax.axis_size(axis))])

    def terms(before, every, places, blocks, flops):
        extra = [x for x in (before, every) if x is not None]
        return pl.pallas_call(
            functools.partial(
                terms_kernel, capacity, orbitals, before is not None, every is not None, places
            ),
            out_shape=terms_shape,
            in_specs=[SMEM, SMEM] + [VMEM] * (1 + len(extra) + len(blocks)),
            out_specs=VMEM,
            cost_estimate=cost(flops),
            compiler_params=params,
            name="terms",
        )(index, coefficients, intersections, *extra, *blocks)

    state = amplitudes
    for step in range(ITERS):
        last = step == ITERS - 1
        gathered = lax.all_gather(payload, "orb", axis=0, tiled=False)
        partial, places, late = None, [], []
        if direct:
            mirror = [exchange(payload, "pairs", half), exchange(payload, ("pairs", "orb"), half * orb_count + 2)]
            flips = [0, *range(half - 1, 0, -1)]
            cores = [[o, o + 1] for o in range(0, orb_count, 2)]
            sent = select(0, flips, gathered)
            arrived = [sent[0]] + [exchange(part, "pairs", flip) for flip, part in zip(flips[1:], sent[1:])]
            held = join(*mirror, after=arrived[:1])
            held = lax.all_gather(held, "orb", axis=0, axis_index_groups=cores)
            sent = select(capacity, flips, held)
            partial = terms(None, None, flips + [half], arrived + [sent[0]], EARLY)
            places = [half + flip for flip in flips[1:]]
            late = [exchange(part, "pairs", flip) for flip, part in zip(flips[1:], sent[1:])]
        else:
            outgoing = select_all(gathered)
            every = lax.all_to_all(outgoing, "pairs", split_axis=0, concat_axis=0, tiled=True)
            partial = terms(None, every, [], [], CLOSE)
        second = jax.ShapeDtypeStruct(amplitudes.shape, F32) if last else payload_shape
        state, payload = pl.pallas_call(
            functools.partial(update_kernel, last, capacity, orbitals, places),
            out_shape=(jax.ShapeDtypeStruct(amplitudes.shape, F32), second),
            in_specs=[SMEM, SMEM, SMEM] + [VMEM] * (6 + len(late)),
            out_specs=(VMEM, VMEM),
            compiler_params=params,
            name="update",
        )(
            index, coefficients, ends, intersections, partial, *late, state, integrals, energies, projector,
        )
    return state, payload


def solution(mesh):
    split = ("pairs", "orb")
    return jax.shard_map(
        body,
        mesh=mesh,
        in_specs=(
            P(split, None, None),
            P(split, None, None),
            P(split, None),
            P(split, None, None, None),
            P(split, None),
            P(split, None),
            P(split, None),
            P(),
            P(),
        ),
        out_specs=(P(split, None, None), P(split, None, None)),
        check_vma=False,
    )
```

time: 72.2 us -> 63.2 us (0.88)
  Pallas kernels: 17.5 us -> 13.4 us
  local copies, waits for them, and re-layouts: 4.03 us -> 0.74 us
  waiting for transfers between devices: 8.36 us -> 6.18 us
  blocking collectives: 15.8 us -> 17.7 us
  starting transfers between devices: 25.3 us -> 24.1 us
    all_to_all x2 -> x0, starting transfers between devices: 7.1 us -> none  [body(): lax.all_to_all(outgoing, 'pairs', split_axis=0, concat_axis=0, axis_index...]
    ppermute x8 -> x16, starting transfers between devices: 18.2 us -> 24.1 us  [exchange(): lax.ppermute(block, axis, [(p, p ^ flip) for p in range(pair_count * orb_...]
    all_gather x0 -> x2, blocking collectives: none -> 4.39 us  [body(): held = lax.all_gather(held, 'orb', axis=0, axis_index_groups=cores)]
    unnamed x30 -> x20, local copies, waits for them, and re-layouts: 4.03 us -> 0.74 us
    all_to_all x2 -> x0, waiting for transfers between devices: 2.63 us -> none  [body(): lax.all_to_all(outgoing, 'pairs', split_axis=0, concat_axis=0, axis_index...]
    all_gather x2, blocking collectives: 15.8 us -> 13.3 us  [body(): gathered = lax.all_gather(payload, 'orb', axis=0, tiled=False)]
    pallas_call x4 -> x2, Pallas kernels: 6.08 us -> 3.8 us  [terms(): pl.pallas_call(functools.partial(terms_kernel, capacity, orbitals, before...]
    pallas_call x6 -> x7, Pallas kernels: 8 us -> 5.74 us  [the longest x1 2.86 us: body(): pl.pallas_call(functools.partial(setup_kernel, capacity, orbitals, near,...]
  transfers between devices with their start and end apart: 10 -> 16, of which waited for: 7 -> 6; matrix products, arithmetic and copies ran while one was open for 0% -> 0% of each run, Pallas kernels for 13% -> 11%
where the time goes in v4:
time: 63.2 us; the launch traced here: 62.9 us
  starting transfers between devices  24.1 us (38%)
  blocking collectives  17.7 us (28%)
  Pallas kernels  13.4 us (21%)
  waiting for transfers between devices  6.18 us (10%)
  between operations  0.82 us (1%)
  local copies, waits for them, and re-layouts  0.74 us (1%)
    ppermute x16, starting transfers between devices, exchange(): lax.ppermute(block, axis, [(p, p ^ flip) for p in range(pair_count * orb_...  24.1 us
    all_gather x2, blocking collectives, body(): gathered = lax.all_gather(payload, 'orb', axis=0, tiled=False)  13.3 us
    ppermute x16, waiting for transfers between devices, exchange(): lax.ppermute(block, axis, [(p, p ^ flip) for p in range(pair_count * orb_...  6.18 us
    all_gather x2, blocking collectives, body(): held = lax.all_gather(held, 'orb', axis=0, axis_index_groups=cores)  4.39 us
    pallas_call x2, Pallas kernels, body(): pl.pallas_call(functools.partial(update_kernel, last, capacity, orbitals,...  3.91 us
    pallas_call x2, Pallas kernels, terms(): pl.pallas_call(functools.partial(terms_kernel, capacity, orbitals, before...  3.8 us
    pallas_call x1, Pallas kernels, body(): pl.pallas_call(functools.partial(setup_kernel, capacity, orbitals, near,...  2.86 us
    pallas_call x4, Pallas kernels, select(): pl.pallas_call(kernel, out_shape=[block_shape] * len(flips), in_specs=[SM...  2.85 us
  transfers between devices with their start and end apart: 16, of which 6 were waited for; matrix products, arithmetic and copies ran while one was open for 0% of the time, Pallas kernels for 11%

profile of v4, /device:TPU:0, one launch (start us, length us, event | category | flops | bytes accessed | tf_op | source)
XLA Modules:
  0.0 62.9 jit_solution(18159970423248390286)
XLA Ops:
  0.6 2.9 %setup.1 = (bf16[528,128]{1,0:T(8,128)(2,1)}, s32[8,128]{1,0:T(8,128)}, s32[4,128]{1,0:T(4,128)}, f32[4,128]{1,0:T(4,128)}) custom-call(s32[2,4]{1,0:T(2,128)} %bitcast.11, f32[4,128,128]{2,1,0:T(8,128)} %refs_3_.1, f32[4,128]{1,0:T(4,128)} %refs_6_.3, s32[16,128]{1,0:T(8,128)} %bitcast.14, s32[1,128]{1,0:T(1,128)} %bitcast.15, f32[4,16]{1,0:T(4,128)} %couplings_hbm.1), custom_call_target="tpu_custom_call" | custom-call | tf_op jit(solution)/shard_map/setup/pallas_call | solution.py:330
  3.5 5.0 %collective-permute-start.4 = (bf16[528,128]{1,0:T(8,128)(2,1)}, bf16[528,128]{1,0:T(8,128)(2,1)S(1)}, u32[]{:S(2)}, u32[]{:S(2)}) collective-permute-start(bf16[528,128]{1,0:T(8,128)(2,1)} %get-tuple-element.27), channel_id=1, source_target_pairs={{0,18},{1,19},{2,16},{3,17},{4,22},{5,23},{6,20},{7,21},{8,26},{9,... | collective-permute-start | bytes 405512 | tf_op jit(solution)/shard_map/ppermute | solution.py:405
  8.9 6.8 %all-gather = bf16[2112,128]{1,0:T(8,128)(2,1)S(1)} all-gather(bf16[528,128]{1,0:T(8,128)(2,1)} %get-tuple-element.27), channel_id=2, replica_groups=mesh['pairs'=8,'orb'=4] {'orb'}, dimensions={0}, use_global_device_ids=true | all-gather | bytes 675840 | tf_op jit(solution)/shard_map/all_gather | solution.py:424
  16.3 0.7 %select.4 = (bf16[400,128]{1,0:T(8,128)(2,1)S(1)}, bf16[400,128]{1,0:T(8,128)(2,1)S(1)}, bf16[400,128]{1,0:T(8,128)(2,1)S(1)}, bf16[400,128]{1,0:T(8,128)(2,1)S(1)}) custom-call(s32[8,128]{1,0:T(8,128)S(1)} %copy-done.3, bf16[4,528,128]{2,1,0:T(8,128)(2,1)S(1)} %bitcast.9), custom_call_target="tpu_custom_call" | custom-call | tf_op jit(solution)/shard_map/select/pallas_call | solution.py:379
  17.0 3.2 %collective-permute-start = (bf16[400,128]{1,0:T(8,128)(2,1)S(1)}, bf16[400,128]{1,0:T(8,128)(2,1)S(1)}, u32[]{:S(2)}, u32[]{:S(2)}) collective-permute-start(bf16[400,128]{1,0:T(8,128)(2,1)S(1)} %get-tuple-element.29), channel_id=1, source_target_pairs={{0,12},{4,8},{8,4},{12,0},{16,28},{20,24},{24,20},{28,16},{1,13},{... | collective-permute-start | bytes 307208 | tf_op jit(solution)/shard_map/ppermute | solution.py:405
  21.1 2.2 %all-gather.1 = bf16[4,528,128]{2,1,0:T(8,128)(2,1)S(1)} all-gather(bf16[2,528,128]{2,1,0:T(8,128)(2,1)S(1)} %join.2), channel_id=3, replica_groups={{0,1},{2,3},{4,5},{6,7},{8,9},{10,11},{12,13},{14,15},{16,17},{18,19},{..., dimensions={0}, use_global_device_ids=true | all-gather | bytes 811008 | tf_op jit(solution)/shard_map/all_gather | solution.py:433
  23.3 0.7 %select.5 = (bf16[400,128]{1,0:T(8,128)(2,1)S(1)}, bf16[400,128]{1,0:T(8,128)(2,1)S(1)}, bf16[400,128]{1,0:T(8,128)(2,1)S(1)}, bf16[400,128]{1,0:T(8,128)(2,1)S(1)}) custom-call(s32[8,128]{1,0:T(8,128)S(1)} %copy-done.3, bf16[2,2,528,128]{3,2,1,0:T(8,128)(2,1)S(1)} %bitcast.8), custom_call_target="tpu_custom_call" | custom-call | tf_op jit(solution)/shard_map/select/pallas_call | solution.py:379
  24.0 2.7 %collective-permute-start.5 = (bf16[400,128]{1,0:T(8,128)(2,1)S(1)}, bf16[400,128]{1,0:T(8,128)(2,1)S(1)}, u32[]{:S(2)}, u32[]{:S(2)}) collective-permute-start(bf16[400,128]{1,0:T(8,128)(2,1)S(1)} %get-tuple-element.33), channel_id=1, source_target_pairs={{0,12},{4,8},{8,4},{12,0},{16,28},{20,24},{24,20},{28,16},{1,13},{... | collective-permute-start | bytes 307208 | tf_op jit(solution)/shard_map/ppermute | solution.py:405
  27.7 1.9 %terms.2.before = f32[520,128]{1,0:T(8,128)S(1)} custom-call(s32[4,128]{1,0:T(4,128)S(1)} %copy-done.8, f32[4,128]{1,0:T(4,128)S(1)} %copy-done.9, bf16[4,16,128,128]{3,2,1,0:T(8,128)(2,1)S(1)} %copy-done, bf16[400,128]{1,0:T(8,128)(2,1)S(1)} %get-tuple-element.28.refs_2_.refs_0_, bf16[400,128]{1,0:T(8,128)(2,1)S(1)} %collective-permute-done.refs_1_, ...), custom_call_target="tpu_custom_call" | custom-call | flops 20000000000 | tf_op jit(solution)/shard_map/terms/pallas_call | solution.py:409
  29.6 1.1 %collective-permute-done.5.refs_0_ = bf16[400,128]{1,0:T(8,128)(2,1)S(1)} collective-permute-done((bf16[400,128]{1,0:T(8,128)(2,1)S(1)}, bf16[400,128]{1,0:T(8,128)(2,1)S(1)}, u32[]{:S(2)}, u32[]{:S(2)}) %collective-permute-start.5) | collective-permute-done | bytes 102432 | tf_op jit(solution)/shard_map/ppermute | solution.py:405
  30.7 1.5 %collective-permute-done.6.refs_1_ = bf16[400,128]{1,0:T(8,128)(2,1)S(1)} collective-permute-done((bf16[400,128]{1,0:T(8,128)(2,1)S(1)}, bf16[400,128]{1,0:T(8,128)(2,1)S(1)}, u32[]{:S(2)}, u32[]{:S(2)}) %collective-permute-start.6) | collective-permute-done | bytes 102432 | tf_op jit(solution)/shard_map/ppermute | solution.py:405
  32.3 1.6 %update.2 = (f32[4,128,128]{2,1,0:T(8,128)S(1)}, bf16[528,128]{1,0:T(8,128)(2,1)S(1)}) custom-call(s32[4,128]{1,0:T(4,128)S(1)} %copy-done.8, f32[4,128]{1,0:T(4,128)S(1)} %copy-done.9, s32[2,4]{1,0:T(2,128)S(1)} %bitcast.12, bf16[4,16,128,128]{3,2,1,0:T(8,128)(2,1)S(1)} %copy-done, f32[520,128]{1,0:T(8,128)S(1)} %terms.2.before, ...), custom_call_target="tpu_custom_call" | custom-call | tf_op jit(solution)/shard_map/update/pallas_call | solution.py:443
  33.9 3.8 %collective-permute-start.12 = (bf16[528,128]{1,0:T(8,128)(2,1)S(1)}, bf16[528,128]{1,0:T(8,128)(2,1)S(1)}, u32[]{:S(2)}, u32[]{:S(2)}) collective-permute-start(bf16[528,128]{1,0:T(8,128)(2,1)S(1)} %get-tuple-element.36), channel_id=1, source_target_pairs={{0,18},{1,19},{2,16},{3,17},{4,22},{5,23},{6,20},{7,21},{8,26},{9,... | collective-permute-start | bytes 405512 | tf_op jit(solution)/shard_map/ppermute | solution.py:405
  37.7 6.5 %all-gather.2 = bf16[2112,128]{1,0:T(8,128)(2,1)S(1)} all-gather(bf16[528,128]{1,0:T(8,128)(2,1)S(1)} %get-tuple-element.36), channel_id=4, replica_groups=mesh['pairs'=8,'orb'=4] {'orb'}, dimensions={0}, use_global_device_ids=true | all-gather | bytes 675840 | tf_op jit(solution)/shard_map/all_gather | solution.py:424
  44.2 0.7 %select.6 = (bf16[400,128]{1,0:T(8,128)(2,1)S(1)}, bf16[400,128]{1,0:T(8,128)(2,1)S(1)}, bf16[400,128]{1,0:T(8,128)(2,1)S(1)}, bf16[400,128]{1,0:T(8,128)(2,1)S(1)}) custom-call(s32[8,128]{1,0:T(8,128)S(1)} %copy-done.4, bf16[4,528,128]{2,1,0:T(8,128)(2,1)S(1)} %bitcast.10), custom_call_target="tpu_custom_call" | custom-call | tf_op jit(solution)/shard_map/select/pallas_call | solution.py:379
  44.9 3.3 %collective-permute-start.8 = (bf16[400,128]{1,0:T(8,128)(2,1)S(1)}, bf16[400,128]{1,0:T(8,128)(2,1)S(1)}, u32[]{:S(2)}, u32[]{:S(2)}) collective-permute-start(bf16[400,128]{1,0:T(8,128)(2,1)S(1)} %get-tuple-element.38), channel_id=1, source_target_pairs={{0,12},{4,8},{8,4},{12,0},{16,28},{20,24},{24,20},{28,16},{1,13},{... | collective-permute-start | bytes 307208 | tf_op jit(solution)/shard_map/ppermute | solution.py:405
  49.5 2.2 %all-gather.3 = bf16[4,528,128]{2,1,0:T(8,128)(2,1)S(1)} all-gather(bf16[2,528,128]{2,1,0:T(8,128)(2,1)S(1)} %join.3), channel_id=5, replica_groups={{0,1},{2,3},{4,5},{6,7},{8,9},{10,11},{12,13},{14,15},{16,17},{18,19},{..., dimensions={0}, use_global_device_ids=true | all-gather | bytes 811008 | tf_op jit(solution)/shard_map/all_gather | solution.py:433
  51.7 0.7 %select.7 = (bf16[400,128]{1,0:T(8,128)(2,1)S(1)}, bf16[400,128]{1,0:T(8,128)(2,1)S(1)}, bf16[400,128]{1,0:T(8,128)(2,1)S(1)}, bf16[400,128]{1,0:T(8,128)(2,1)S(1)}) custom-call(s32[8,128]{1,0:T(8,128)S(1)} %copy-done.4, bf16[2,2,528,128]{3,2,1,0:T(8,128)(2,1)S(1)} %bitcast.7), custom_call_target="tpu_custom_call" | custom-call | tf_op jit(solution)/shard_map/select/pallas_call | solution.py:379
  52.4 2.3 %collective-permute-start.13 = (bf16[400,128]{1,0:T(8,128)(2,1)S(1)}, bf16[400,128]{1,0:T(8,128)(2,1)S(1)}, u32[]{:S(2)}, u32[]{:S(2)}) collective-permute-start(bf16[400,128]{1,0:T(8,128)(2,1)S(1)} %get-tuple-element.42), channel_id=1, source_target_pairs={{0,12},{4,8},{8,4},{12,0},{16,28},{20,24},{24,20},{28,16},{1,13},{... | collective-permute-start | bytes 307208 | tf_op jit(solution)/shard_map/ppermute | solution.py:405
  54.7 0.8 %collective-permute-start.14 = (bf16[400,128]{1,0:T(8,128)(2,1)S(1)}, bf16[400,128]{1,0:T(8,128)(2,1)S(1)}, u32[]{:S(2)}, u32[]{:S(2)}) collective-permute-start(bf16[400,128]{1,0:T(8,128)(2,1)S(1)} %get-tuple-element.43), channel_id=1, source_target_pairs={{0,8},{4,12},{8,0},{12,4},{16,24},{20,28},{24,16},{28,20},{1,9},{5... | collective-permute-start | bytes 307208 | tf_op jit(solution)/shard_map/ppermute | solution.py:405
  56.0 1.9 %terms.3.before = f32[520,128]{1,0:T(8,128)S(1)} custom-call(s32[4,128]{1,0:T(4,128)S(1)} %copy-done.8, f32[4,128]{1,0:T(4,128)S(1)} %copy-done.9, bf16[4,16,128,128]{3,2,1,0:T(8,128)(2,1)S(1)} %copy-done, bf16[400,128]{1,0:T(8,128)(2,1)S(1)} %get-tuple-element.37.refs_2_.refs_0_, bf16[400,128]{1,0:T(8,128)(2,1)S(1)} %collective-permute-done.8.refs_1_, ...), custom_call_target="tpu_custom_call" | custom-call | flops 20000000000 | tf_op jit(solution)/shard_map/terms/pallas_call | solution.py:409
  57.9 1.2 %collective-permute-done.13.refs_0_ = bf16[400,128]{1,0:T(8,128)(2,1)S(1)} collective-permute-done((bf16[400,128]{1,0:T(8,128)(2,1)S(1)}, bf16[400,128]{1,0:T(8,128)(2,1)S(1)}, u32[]{:S(2)}, u32[]{:S(2)}) %collective-permute-start.13) | collective-permute-done | bytes 102432 | tf_op jit(solution)/shard_map/ppermute | solution.py:405
  59.1 1.5 %collective-permute-done.14.refs_1_ = bf16[400,128]{1,0:T(8,128)(2,1)S(1)} collective-permute-done((bf16[400,128]{1,0:T(8,128)(2,1)S(1)}, bf16[400,128]{1,0:T(8,128)(2,1)S(1)}, u32[]{:S(2)}, u32[]{:S(2)}) %collective-permute-start.14) | collective-permute-done | bytes 102432 | tf_op jit(solution)/shard_map/ppermute | solution.py:405
  60.6 2.3 %update.3 = (f32[4,128,128]{2,1,0:T(8,128)}, f32[4,128,128]{2,1,0:T(8,128)}) custom-call(s32[4,128]{1,0:T(4,128)S(1)} %copy-done.8, f32[4,128]{1,0:T(4,128)S(1)} %copy-done.9, s32[2,4]{1,0:T(2,128)S(1)} %bitcast.13, bf16[4,16,128,128]{3,2,1,0:T(8,128)(2,1)S(1)} %copy-done, f32[520,128]{1,0:T(8,128)S(1)} %terms.3.before, ...), custom_call_target="tpu_custom_call" | custom-call | tf_op jit(solution)/shard_map/update/pallas_call | solution.py:443
  (43 shorter events, 4.6 us)
Async XLA Ops:
  0.6 27.0 %copy-start = (bf16[4,16,128,128]{3,2,1,0:T(8,128)(2,1)S(1)}, bf16[4,16,128,128]{3,2,1,0:T(8,128)(2,1)}, u32[]{:S(2)}) copy-start(bf16[4,16,128,128]{3,2,1,0:T(8,128)(2,1)} %intersections.7) | copy-start | bytes 6291460
  3.5 17.4 %collective-permute-start.4 = (bf16[528,128]{1,0:T(8,128)(2,1)}, bf16[528,128]{1,0:T(8,128)(2,1)S(1)}, u32[]{:S(2)}, u32[]{:S(2)}) collective-permute-start(bf16[528,128]{1,0:T(8,128)(2,1)} %get-tuple-element.27), channel_id=1, source_target_pairs={{0,18},{1,19},{2,16},{3,17},{4,22},{5,23},{6,20},{7,21},{8,26},{9,... | collective-permute-start | bytes 405512 | tf_op jit(solution)/shard_map/ppermute | solution.py:405
  8.5 12.5 %collective-permute-start.3 = (bf16[528,128]{1,0:T(8,128)(2,1)}, bf16[528,128]{1,0:T(8,128)(2,1)S(1)}, u32[]{:S(2)}, u32[]{:S(2)}) collective-permute-start(bf16[528,128]{1,0:T(8,128)(2,1)} %get-tuple-element.27), channel_id=1, source_target_pairs={{0,16},{4,20},{8,24},{12,28},{16,0},{20,4},{24,8},{28,12},{1,17},{... | collective-permute-start | bytes 405512 | tf_op jit(solution)/shard_map/ppermute | solution.py:405
  16.3 11.3 %copy-start.8 = (s32[4,128]{1,0:T(4,128)S(1)}, s32[4,128]{1,0:T(4,128)}, u32[]{:S(2)}) copy-start(s32[4,128]{1,0:T(4,128)} %get-tuple-element.24.index) | copy-start | bytes 6148
  16.3 11.3 %copy-start.9 = (f32[4,128]{1,0:T(4,128)S(1)}, f32[4,128]{1,0:T(4,128)}, u32[]{:S(2)}) copy-start(f32[4,128]{1,0:T(4,128)} %get-tuple-element.25.coefficients) | copy-start | bytes 6148
  17.0 10.1 %collective-permute-start = (bf16[400,128]{1,0:T(8,128)(2,1)S(1)}, bf16[400,128]{1,0:T(8,128)(2,1)S(1)}, u32[]{:S(2)}, u32[]{:S(2)}) collective-permute-start(bf16[400,128]{1,0:T(8,128)(2,1)S(1)} %get-tuple-element.29), channel_id=1, source_target_pairs={{0,12},{4,8},{8,4},{12,0},{16,28},{20,24},{24,20},{28,16},{1,13},{... | collective-permute-start | bytes 307208 | tf_op jit(solution)/shard_map/ppermute | solution.py:405
  20.2 7.4 %collective-permute-start.1 = (bf16[400,128]{1,0:T(8,128)(2,1)S(1)}, bf16[400,128]{1,0:T(8,128)(2,1)S(1)}, u32[]{:S(2)}, u32[]{:S(2)}) collective-permute-start(bf16[400,128]{1,0:T(8,128)(2,1)S(1)} %get-tuple-element.30), channel_id=1, source_target_pairs={{0,8},{4,12},{8,0},{12,4},{16,24},{20,28},{24,16},{28,20},{1,9},{5... | collective-permute-start | bytes 307208 | tf_op jit(solution)/shard_map/ppermute | solution.py:405
  20.2 7.4 %collective-permute-start.2 = (bf16[400,128]{1,0:T(8,128)(2,1)S(1)}, bf16[400,128]{1,0:T(8,128)(2,1)S(1)}, u32[]{:S(2)}, u32[]{:S(2)}) collective-permute-start(bf16[400,128]{1,0:T(8,128)(2,1)S(1)} %get-tuple-element.31), channel_id=1, source_target_pairs={{0,4},{4,0},{8,12},{12,8},{16,20},{20,16},{24,28},{28,24},{1,5},{5... | collective-permute-start | bytes 307208 | tf_op jit(solution)/shard_map/ppermute | solution.py:405
  24.0 6.7 %collective-permute-start.5 = (bf16[400,128]{1,0:T(8,128)(2,1)S(1)}, bf16[400,128]{1,0:T(8,128)(2,1)S(1)}, u32[]{:S(2)}, u32[]{:S(2)}) collective-permute-start(bf16[400,128]{1,0:T(8,128)(2,1)S(1)} %get-tuple-element.33), channel_id=1, source_target_pairs={{0,12},{4,8},{8,4},{12,0},{16,28},{20,24},{24,20},{28,16},{1,13},{... | collective-permute-start | bytes 307208 | tf_op jit(solution)/shard_map/ppermute | solution.py:405
  26.7 5.5 %collective-permute-start.6 = (bf16[400,128]{1,0:T(8,128)(2,1)S(1)}, bf16[400,128]{1,0:T(8,128)(2,1)S(1)}, u32[]{:S(2)}, u32[]{:S(2)}) collective-permute-start(bf16[400,128]{1,0:T(8,128)(2,1)S(1)} %get-tuple-element.34), channel_id=1, source_target_pairs={{0,8},{4,12},{8,0},{12,4},{16,24},{20,28},{24,16},{28,20},{1,9},{5... | collective-permute-start | bytes 307208 | tf_op jit(solution)/shard_map/ppermute | solution.py:405
  27.1 5.1 %collective-permute-start.7 = (bf16[400,128]{1,0:T(8,128)(2,1)S(1)}, bf16[400,128]{1,0:T(8,128)(2,1)S(1)}, u32[]{:S(2)}, u32[]{:S(2)}) collective-permute-start(bf16[400,128]{1,0:T(8,128)(2,1)S(1)} %get-tuple-element.35), channel_id=1, source_target_pairs={{0,4},{4,0},{8,12},{12,8},{16,20},{20,16},{24,28},{28,24},{1,5},{5... | collective-permute-start | bytes 307208 | tf_op jit(solution)/shard_map/ppermute | solution.py:405
  27.6 4.6 %copy-start.1 = (f32[4,128,128]{2,1,0:T(8,128)S(1)}, f32[4,128,128]{2,1,0:T(8,128)}, u32[]{:S(2)}) copy-start(f32[4,128,128]{2,1,0:T(8,128)} %refs_3_.1) | copy-start | bytes 786436
  27.6 4.6 %copy-start.2 = (bf16[4,128,128]{2,1,0:T(8,128)(2,1)S(1)}, bf16[4,128,128]{2,1,0:T(8,128)(2,1)}, u32[]{:S(2)}) copy-start(bf16[4,128,128]{2,1,0:T(8,128)(2,1)} %refs_4_.3) | copy-start | bytes 393220
  27.6 4.6 %copy-start.5 = (f32[4,128]{1,0:T(4,128)S(1)}, f32[4,128]{1,0:T(4,128)}, u32[]{:S(2)}) copy-start(f32[4,128]{1,0:T(4,128)} %refs_6_.3) | copy-start | bytes 6148
  27.6 4.6 %copy-start.6 = (s32[4,2]{0,1:T(2,128)S(1)}, s32[4,2]{0,1:T(2,128)}, u32[]{:S(2)}) copy-start(s32[4,2]{0,1:T(2,128)} %param.15) | copy-start | bytes 100
  29.6 14.6 %copy-start.4 = (s32[8,128]{1,0:T(8,128)S(1)}, s32[8,128]{1,0:T(8,128)}, u32[]{:S(2)}) copy-start(s32[8,128]{1,0:T(8,128)} %get-tuple-element.26.index) | copy-start | bytes 12292
  33.9 15.0 %collective-permute-start.12 = (bf16[528,128]{1,0:T(8,128)(2,1)S(1)}, bf16[528,128]{1,0:T(8,128)(2,1)S(1)}, u32[]{:S(2)}, u32[]{:S(2)}) collective-permute-start(bf16[528,128]{1,0:T(8,128)(2,1)S(1)} %get-tuple-element.36), channel_id=1, source_target_pairs={{0,18},{1,19},{2,16},{3,17},{4,22},{5,23},{6,20},{7,21},{8,26},{9,... | collective-permute-start | bytes 405512 | tf_op jit(solution)/shard_map/ppermute | solution.py:405
  37.6 11.8 %collective-permute-start.11 = (bf16[528,128]{1,0:T(8,128)(2,1)S(1)}, bf16[528,128]{1,0:T(8,128)(2,1)S(1)}, u32[]{:S(2)}, u32[]{:S(2)}) collective-permute-start(bf16[528,128]{1,0:T(8,128)(2,1)S(1)} %get-tuple-element.36), channel_id=1, source_target_pairs={{0,16},{4,20},{8,24},{12,28},{16,0},{20,4},{24,8},{28,12},{1,17},{... | collective-permute-start | bytes 405512 | tf_op jit(solution)/shard_map/ppermute | solution.py:405
  44.9 10.6 %collective-permute-start.8 = (bf16[400,128]{1,0:T(8,128)(2,1)S(1)}, bf16[400,128]{1,0:T(8,128)(2,1)S(1)}, u32[]{:S(2)}, u32[]{:S(2)}) collective-permute-start(bf16[400,128]{1,0:T(8,128)(2,1)S(1)} %get-tuple-element.38), channel_id=1, source_target_pairs={{0,12},{4,8},{8,4},{12,0},{16,28},{20,24},{24,20},{28,16},{1,13},{... | collective-permute-start | bytes 307208 | tf_op jit(solution)/shard_map/ppermute | solution.py:405
  48.2 7.8 %collective-permute-start.9 = (bf16[400,128]{1,0:T(8,128)(2,1)S(1)}, bf16[400,128]{1,0:T(8,128)(2,1)S(1)}, u32[]{:S(2)}, u32[]{:S(2)}) collective-permute-start(bf16[400,128]{1,0:T(8,128)(2,1)S(1)} %get-tuple-element.39), channel_id=1, source_target_pairs={{0,8},{4,12},{8,0},{12,4},{16,24},{20,28},{24,16},{28,20},{1,9},{5... | collective-permute-start | bytes 307208 | tf_op jit(solution)/shard_map/ppermute | solution.py:405
  48.2 7.8 %collective-permute-start.10 = (bf16[400,128]{1,0:T(8,128)(2,1)S(1)}, bf16[400,128]{1,0:T(8,128)(2,1)S(1)}, u32[]{:S(2)}, u32[]{:S(2)}) collective-permute-start(bf16[400,128]{1,0:T(8,128)(2,1)S(1)} %get-tuple-element.40), channel_id=1, source_target_pairs={{0,4},{4,0},{8,12},{12,8},{16,20},{20,16},{24,28},{28,24},{1,5},{5... | collective-permute-start | bytes 307208 | tf_op jit(solution)/shard_map/ppermute | solution.py:405
  52.4 6.7 %collective-permute-start.13 = (bf16[400,128]{1,0:T(8,128)(2,1)S(1)}, bf16[400,128]{1,0:T(8,128)(2,1)S(1)}, u32[]{:S(2)}, u32[]{:S(2)}) collective-permute-start(bf16[400,128]{1,0:T(8,128)(2,1)S(1)} %get-tuple-element.42), channel_id=1, source_target_pairs={{0,12},{4,8},{8,4},{12,0},{16,28},{20,24},{24,20},{28,16},{1,13},{... | collective-permute-start | bytes 307208 | tf_op jit(solution)/shard_map/ppermute | solution.py:405
  54.7 5.9 %collective-permute-start.14 = (bf16[400,128]{1,0:T(8,128)(2,1)S(1)}, bf16[400,128]{1,0:T(8,128)(2,1)S(1)}, u32[]{:S(2)}, u32[]{:S(2)}) collective-permute-start(bf16[400,128]{1,0:T(8,128)(2,1)S(1)} %get-tuple-element.43), channel_id=1, source_target_pairs={{0,8},{4,12},{8,0},{12,4},{16,24},{20,28},{24,16},{28,20},{1,9},{5... | collective-permute-start | bytes 307208 | tf_op jit(solution)/shard_map/ppermute | solution.py:405
  55.5 5.1 %collective-permute-start.15 = (bf16[400,128]{1,0:T(8,128)(2,1)S(1)}, bf16[400,128]{1,0:T(8,128)(2,1)S(1)}, u32[]{:S(2)}, u32[]{:S(2)}) collective-permute-start(bf16[400,128]{1,0:T(8,128)(2,1)S(1)} %get-tuple-element.44), channel_id=1, source_target_pairs={{0,4},{4,0},{8,12},{12,8},{16,20},{20,16},{24,28},{28,24},{1,5},{5... | collective-permute-start | bytes 307208 | tf_op jit(solution)/shard_map/ppermute | solution.py:405
  (2 other events, 5.3 us)

commit v5 on v4

--- a/solution.py
+++ b/solution.py
@@ -82,15 +82,15 @@
 
 
 def setup_kernel(
-    capacity, orbitals, near, mirrors,
-    ends, state_hbm, projector_hbm, coupled_hbm, slot_hbm, couplings_hbm,
+    capacity, orbitals, near, mirrors, direct,
+    ends_hbm, state_hbm, projector_hbm, coupled_hbm, slot_hbm, couplings_hbm,
     payload, index, table, coefficients,
-    state, projector, coupled, slot, couplings, sems,
+    ends, state, projector, coupled, slot, couplings, sems,
 ):
     copies = fetch(
         (
             (coupled_hbm, coupled), (slot_hbm, slot), (projector_hbm, projector), (state_hbm, state),
-            (couplings_hbm, couplings),
+            (couplings_hbm, couplings), (ends_hbm, ends),
         ),
         sems,
     )
@@ -107,8 +107,9 @@
     lanes = lax.broadcasted_iota(jnp.int32, (1, count), 1)
     members = lax.broadcasted_iota(jnp.int32, (group, 1), 0)
     slot_ids = lax.broadcasted_iota(jnp.int32, (count, lanes_out), 0)
-    dest = lax.broadcasted_iota(jnp.int32, (count, lanes_out), 1)
-    owner = (slot_ids // per_device == dest * orb_count + orb_idx) & (dest < pair_count)
+    column = lax.broadcasted_iota(jnp.int32, (count, lanes_out), 1)
+    dest = column ^ pair_idx if direct else column
+    owner = (slot_ids // per_device == dest * orb_count + orb_idx) & (column < pair_count)
     for m, flip in enumerate(mirrors):
         base = (pair_idx ^ flip) * group
         pairs = jnp.sum(jnp.where(slots == base + members, lanes, 0), axis=1, keepdims=True)
@@ -158,6 +159,7 @@
     eye = eye_mask(width)
     copies[2].wait()
     copies[3].wait()
+    copies[5].wait()
     total = jnp.zeros((orbitals, width), F32)
     counts_a = end_counts(orbitals, per_device, lambda s: ends[0, s])
     counts_b = end_counts(orbitals, per_device, lambda s: ends[1, s])
@@ -169,16 +171,16 @@
     payload[pl.ds(per_device * width, tail), :] = tail_rows(total, tail)
 
 
-def select_kernel(capacity, per_device, orbitals, width, dests, row, swap, index, gathered, outs):
+def select_kernel(capacity, per_device, orbitals, width, lanes, row, swap, index, gathered, outs):
     blocks = per_device * width
     tail = gathered.shape[1] - blocks
     total = join_parts(gathered[0, pl.ds(blocks, tail), :], orbitals)
     for d in range(1, gathered.shape[0]):
         total += join_parts(gathered[d, pl.ds(blocks, tail), :], orbitals)
     rows = tail_rows(total, tail)
-    for dest, out in zip(dests, outs):
+    for lane, out in zip(lanes, outs):
         for c in range(capacity):
-            j = index[row + c, dest]
+            j = index[row + c, lane]
             first = pl.multiple_of((j % per_device) * width, ROWS)
             out[pl.ds(c * width, width), :] = gathered[(j // per_device) ^ swap, pl.ds(first, width), :]
         out[pl.ds(capacity * width, tail), :] = rows
@@ -317,6 +319,7 @@
     stride = capacity * width + tail
     orb_count = lax.axis_size("orb")
     direct = pair_count in (4, 8) and orb_count == 4
+    tables = VMEM if direct else SMEM
     half = pair_count // 2
     mirrors = [0, half] if direct else [0]
     near = 1 if direct else pair_count
@@ -328,22 +331,23 @@
     terms_shape = jax.ShapeDtypeStruct((per_device * width + -(-orbitals // 8) * 8, width), F32)
     payload_shape = jax.ShapeDtypeStruct((per_device * width + tail, width), BF16)
     payload, send_index, index, coefficients = pl.pallas_call(
-        functools.partial(setup_kernel, capacity, orbitals, near, mirrors),
+        functools.partial(setup_kernel, capacity, orbitals, near, mirrors, direct),
         out_shape=(
             payload_shape,
             jax.ShapeDtypeStruct((-(-len(mirrors) * capacity // 8) * 8, lanes), jnp.int32),
             jax.ShapeDtypeStruct((per_device, lanes), jnp.int32),
             jax.ShapeDtypeStruct((per_device, lanes), F32),
         ),
-        in_specs=[SMEM] + [HBM] * 5,
+        in_specs=[HBM] * 6,
         out_specs=[VMEM] * 4,
         scratch_shapes=[
+            pltpu.VMEM(ends.shape, jnp.int32),
             pltpu.VMEM(amplitudes.shape, F32),
             pltpu.VMEM(projector.shape, F32),
             pltpu.VMEM((neighbours, total), jnp.int32),
             pltpu.VMEM((1, total), jnp.int32),
             pltpu.VMEM(couplings.shape, F32),
-            pltpu.SemaphoreType.DMA((5,)),
+            pltpu.SemaphoreType.DMA((6,)),
         ],
         compiler_params=pltpu.CompilerParams(vmem_limit_bytes=WHOLE),
         name="setup",
@@ -351,12 +355,16 @@
 
     def join(*parts, after=()):
         def kernel(*refs):
-            for i in range(len(parts)):
-                refs[-1][i] = refs[i][...]
-
+            if len(parts) == 1:
+                refs[-1][...] = refs[0][...]
+            else:
+                for i in range(len(parts)):
+                    refs[-1][i] = refs[i][...]
+
+        shape = payload_shape.shape if len(parts) == 1 else (len(parts), *payload_shape.shape)
         return pl.pallas_call(
             kernel,
-            out_shape=jax.ShapeDtypeStruct((len(parts), *payload_shape.shape), BF16),
+            out_shape=jax.ShapeDtypeStruct(shape, BF16),
             in_specs=[VMEM] * len(parts) + [ANY] * len(after),
             out_specs=VMEM,
             compiler_params=small,
@@ -366,22 +374,19 @@
 
     def select(row, flips, gathered):
         def kernel(index, source, *refs):
-            outs = refs[: len(flips)]
-            here, swap = lax.axis_index("pairs"), 0
-            if row:
-                held, source, swap = source, refs[-1], lax.axis_index("orb") // 2 * 2
-                for c in range(2):
-                    for x in range(2):
-                        source[2 * x + c] = held[c, x]
-            dests = [here ^ flip for flip in flips]
-            select_kernel(capacity, per_device, orbitals, width, dests, row, swap, index, source, outs)
+            outs, held = refs[: len(flips)], refs[-1]
+            for c in range(2):
+                for x in range(2):
+                    held[2 * x + c] = source[c, x]
+            swap = lax.axis_index("orb") // 2 * 2
+            select_kernel(capacity, per_device, orbitals, width, flips, row, swap, index, held, outs)
 
         return pl.pallas_call(
             kernel,
             out_shape=[block_shape] * len(flips),
-            in_specs=[SMEM, VMEM],
+            in_specs=[VMEM, VMEM],
             out_specs=[VMEM] * len(flips),
-            scratch_shapes=[pltpu.VMEM((4, *payload_shape.shape), BF16)] if row else [],
+            scratch_shapes=[pltpu.VMEM((4, *payload_shape.shape), BF16)],
             compiler_params=small,
             cost_estimate=cost(0),
             name="select",
@@ -395,7 +400,7 @@
         return pl.pallas_call(
             kernel,
             out_shape=jax.ShapeDtypeStruct((pair_count, stride, width), BF16),
-            in_specs=[SMEM, VMEM],
+            in_specs=[VMEM, VMEM],
             out_specs=VMEM,
             compiler_params=small,
             name="select",
@@ -411,7 +416,7 @@
                 terms_kernel, capacity, orbitals, before is not None, every is not None, places
             ),
             out_shape=terms_shape,
-            in_specs=[SMEM, SMEM] + [VMEM] * (1 + len(extra) + len(blocks)),
+            in_specs=[tables, tables] + [VMEM] * (1 + len(extra) + len(blocks)),
             out_specs=VMEM,
             cost_estimate=cost(flops),
             compiler_params=params,
@@ -421,21 +426,24 @@
     state = amplitudes
     for step in range(ITERS):
         last = step == ITERS - 1
-        gathered = lax.all_gather(payload, "orb", axis=0, tiled=False)
         partial, places, late = None, [], []
         if direct:
-            mirror = [exchange(payload, "pairs", half), exchange(payload, ("pairs", "orb"), half * orb_count + 2)]
+            mirror = exchange(payload, "pairs", half)
             flips = [0, *range(half - 1, 0, -1)]
             cores = [[o, o + 1] for o in range(0, orb_count, 2)]
-            sent = select(0, flips, gathered)
+            held = join(payload, exchange(payload, "orb", 2))
+            held = lax.all_gather(held, "orb", axis=0, axis_index_groups=cores)
+            sent = select(0, flips, held)
             arrived = [sent[0]] + [exchange(part, "pairs", flip) for flip, part in zip(flips[1:], sent[1:])]
-            held = join(*mirror, after=arrived[:1])
+            mirror = join(mirror, after=[held])
+            held = join(mirror, exchange(mirror, "orb", 2), after=arrived[:1])
             held = lax.all_gather(held, "orb", axis=0, axis_index_groups=cores)
             sent = select(capacity, flips, held)
             partial = terms(None, None, flips + [half], arrived + [sent[0]], EARLY)
             places = [half + flip for flip in flips[1:]]
             late = [exchange(part, "pairs", flip) for flip, part in zip(flips[1:], sent[1:])]
         else:
+            gathered = lax.all_gather(payload, "orb", axis=0, tiled=False)
             outgoing = select_all(gathered)
             every = lax.all_to_all(outgoing, "pairs", split_axis=0, concat_axis=0, tiled=True)
             partial = terms(None, every, [], [], CLOSE)
@@ -443,7 +451,7 @@
         state, payload = pl.pallas_call(
             functools.partial(update_kernel, last, capacity, orbitals, places),
             out_shape=(jax.ShapeDtypeStruct(amplitudes.shape, F32), second),
-            in_specs=[SMEM, SMEM, SMEM] + [VMEM] * (6 + len(late)),
+            in_specs=[VMEM] * (9 + len(late)),
             out_specs=(VMEM, VMEM),
             compiler_params=params,
             name="update",

time: 63.2 us -> 58.9 us (0.932)
  blocking collectives: 17.7 us -> 8.9 us
  waiting for transfers between devices: 6.18 us -> 14 us
  Pallas kernels: 13.4 us -> 8.72 us
  starting transfers between devices: 24.1 us -> 25.3 us
    all_gather x2 -> x0, blocking collectives: 13.3 us -> none  [body(): gathered = lax.all_gather(payload, 'orb', axis=0, tiled=False)]
    ppermute x16 -> x18, waiting for transfers between devices: 6.18 us -> 14 us  [exchange(): lax.ppermute(block, axis, [(p, p ^ flip) for p in range(pair_count * orb_...]
    all_gather x2 -> x4, blocking collectives: 4.39 us -> 8.9 us  [body(): held = lax.all_gather(held, 'orb', axis=0, axis_index_groups=cores)]
    pallas_call x6 -> x10, Pallas kernels: 2.88 us -> 0.78 us  [the longest x4 0.69 us: select(): pl.pallas_call(kernel, out_shape=[block_shape] * len(flips), in_specs=[VM...]
    ppermute x16 -> x18, starting transfers between devices: 24.1 us -> 25.3 us  [exchange(): lax.ppermute(block, axis, [(p, p ^ flip) for p in range(pair_count * orb_...]
    pallas_call x2, Pallas kernels: 3.91 us -> 2.97 us  [body(): pl.pallas_call(functools.partial(update_kernel, last, capacity, orbitals,...]
    pallas_call x2, Pallas kernels: 3.8 us -> 2.89 us  [terms(): pl.pallas_call(functools.partial(terms_kernel, capacity, orbitals, before...]
    pallas_call x1, Pallas kernels: 2.86 us -> 2.08 us  [body(): pl.pallas_call(functools.partial(setup_kernel, capacity, orbitals, near,...]
  transfers between devices with their start and end apart: 16 -> 18, of which waited for: 6 -> 9; matrix products, arithmetic and copies ran while one was open for 0% -> 0% of each run, Pallas kernels for 11% -> 6%
where the time goes in v5:
time: 58.9 us; the launch traced here: 58.7 us
  starting transfers between devices  25.3 us (43%)
  waiting for transfers between devices  14 us (24%)
  blocking collectives  8.9 us (15%)
  Pallas kernels  8.72 us (15%)
  local copies, waits for them, and re-layouts  0.96 us (2%)
  between operations  0.83 us (1%)
    ppermute x18, starting transfers between devices, exchange(): lax.ppermute(block, axis, [(p, p ^ flip) for p in range(pair_count * orb_...  25.3 us
    ppermute x18, waiting for transfers between devices, exchange(): lax.ppermute(block, axis, [(p, p ^ flip) for p in range(pair_count * orb_...  14 us
    all_gather x4, blocking collectives, body(): held = lax.all_gather(held, 'orb', axis=0, axis_index_groups=cores)  8.9 us
    pallas_call x2, Pallas kernels, body(): pl.pallas_call(functools.partial(update_kernel, last, capacity, orbitals,...  2.97 us
    pallas_call x2, Pallas kernels, terms(): pl.pallas_call(functools.partial(terms_kernel, capacity, orbitals, before...  2.89 us
    pallas_call x1, Pallas kernels, body(): pl.pallas_call(functools.partial(setup_kernel, capacity, orbitals, near,...  2.08 us
  transfers between devices with their start and end apart: 18, of which 9 were waited for; matrix products, arithmetic and copies ran while one was open for 0% of the time, Pallas kernels for 6%

profile of v5, /device:TPU:0, one launch (start us, length us, event | category | flops | bytes accessed | tf_op | source)
XLA Modules:
  0.0 58.7 jit_solution(4261497979060950168)
XLA Ops:
  0.6 2.1 %setup.1 = (bf16[528,128]{1,0:T(8,128)(2,1)}, s32[8,128]{1,0:T(8,128)}, s32[4,128]{1,0:T(4,128)}, f32[4,128]{1,0:T(4,128)}) custom-call(s32[2,4]{1,0:T(2,128)} %bitcast.13, f32[4,128,128]{2,1,0:T(8,128)} %refs_3_.1, f32[4,128]{1,0:T(4,128)} %refs_6_.3, s32[16,128]{1,0:T(8,128)} %bitcast.16, s32[1,128]{1,0:T(1,128)} %bitcast.17, f32[4,16]{1,0:T(4,128)} %couplings_hbm.1), custom_call_target="tpu_custom_call" | custom-call | tf_op jit(solution)/shard_map/setup/pallas_call | solution.py:333
  2.7 3.0 %collective-permute-start = (bf16[528,128]{1,0:T(8,128)(2,1)}, bf16[528,128]{1,0:T(8,128)(2,1)S(1)}, u32[]{:S(2)}, u32[]{:S(2)}) collective-permute-start(bf16[528,128]{1,0:T(8,128)(2,1)} %get-tuple-element.27.refs_0_), channel_id=1, source_target_pairs={{0,2},{1,3},{2,0},{3,1},{4,6},{5,7},{6,4},{7,5},{8,10},{9,11},{10,... | collective-permute-start | bytes 405512 | tf_op jit(solution)/shard_map/ppermute | solution.py:410
  5.7 2.6 %collective-permute-start.4 = (bf16[528,128]{1,0:T(8,128)(2,1)}, bf16[528,128]{1,0:T(8,128)(2,1)S(1)}, u32[]{:S(2)}, u32[]{:S(2)}) collective-permute-start(bf16[528,128]{1,0:T(8,128)(2,1)} %get-tuple-element.27.refs_0_), channel_id=1, source_target_pairs={{0,16},{4,20},{8,24},{12,28},{16,0},{20,4},{24,8},{28,12},{1,17},{... | collective-permute-start | bytes 405512 | tf_op jit(solution)/shard_map/ppermute | solution.py:410
  10.5 2.3 %all-gather = bf16[4,528,128]{2,1,0:T(8,128)(2,1)S(1)} all-gather(bf16[2,528,128]{2,1,0:T(8,128)(2,1)S(1)} %join.6), channel_id=2, replica_groups={{0,1},{2,3},{4,5},{6,7},{8,9},{10,11},{12,13},{14,15},{16,17},{18,19},{..., dimensions={0}, use_global_device_ids=true | all-gather | bytes 811008 | tf_op jit(solution)/shard_map/all_gather | solution.py:435
  12.8 2.0 %collective-permute-done.4.refs_0_ = bf16[528,128]{1,0:T(8,128)(2,1)S(1)} collective-permute-done((bf16[528,128]{1,0:T(8,128)(2,1)}, bf16[528,128]{1,0:T(8,128)(2,1)S(1)}, u32[]{:S(2)}, u32[]{:S(2)}) %collective-permute-start.4) | collective-permute-done | bytes 135200 | tf_op jit(solution)/shard_map/ppermute | solution.py:410
  15.6 1.9 %collective-permute-start.1 = (bf16[400,128]{1,0:T(8,128)(2,1)S(1)}, bf16[400,128]{1,0:T(8,128)(2,1)S(1)}, u32[]{:S(2)}, u32[]{:S(2)}) collective-permute-start(bf16[400,128]{1,0:T(8,128)(2,1)S(1)} %get-tuple-element.29), channel_id=1, source_target_pairs={{0,12},{4,8},{8,4},{12,0},{16,28},{20,24},{24,20},{28,16},{1,13},{... | collective-permute-start | bytes 307208 | tf_op jit(solution)/shard_map/ppermute | solution.py:410
  17.4 1.2 %collective-permute-start.2 = (bf16[400,128]{1,0:T(8,128)(2,1)S(1)}, bf16[400,128]{1,0:T(8,128)(2,1)S(1)}, u32[]{:S(2)}, u32[]{:S(2)}) collective-permute-start(bf16[400,128]{1,0:T(8,128)(2,1)S(1)} %get-tuple-element.30), channel_id=1, source_target_pairs={{0,8},{4,12},{8,0},{12,4},{16,24},{20,28},{24,16},{28,20},{1,9},{5... | collective-permute-start | bytes 307208 | tf_op jit(solution)/shard_map/ppermute | solution.py:410
  19.9 2.2 %all-gather.1 = bf16[4,528,128]{2,1,0:T(8,128)(2,1)S(1)} all-gather(bf16[2,528,128]{2,1,0:T(8,128)(2,1)S(1)} %join.8), channel_id=3, replica_groups={{0,1},{2,3},{4,5},{6,7},{8,9},{10,11},{12,13},{14,15},{16,17},{18,19},{..., dimensions={0}, use_global_device_ids=true | all-gather | bytes 811008 | tf_op jit(solution)/shard_map/all_gather | solution.py:440
  22.3 2.3 %collective-permute-start.6 = (bf16[400,128]{1,0:T(8,128)(2,1)S(1)}, bf16[400,128]{1,0:T(8,128)(2,1)S(1)}, u32[]{:S(2)}, u32[]{:S(2)}) collective-permute-start(bf16[400,128]{1,0:T(8,128)(2,1)S(1)} %get-tuple-element.33), channel_id=1, source_target_pairs={{0,12},{4,8},{8,4},{12,0},{16,28},{20,24},{24,20},{28,16},{1,13},{... | collective-permute-start | bytes 307208 | tf_op jit(solution)/shard_map/ppermute | solution.py:410
  25.9 1.4 %terms.2.before = f32[520,128]{1,0:T(8,128)S(1)} custom-call(s32[4,128]{1,0:T(4,128)S(1)} %copy-done.8, f32[4,128]{1,0:T(4,128)S(1)} %copy-done.9, bf16[4,16,128,128]{3,2,1,0:T(8,128)(2,1)S(1)} %copy-done, bf16[400,128]{1,0:T(8,128)(2,1)S(1)} %get-tuple-element.28.refs_2_.refs_0_, bf16[400,128]{1,0:T(8,128)(2,1)S(1)} %collective-permute-done.1.refs_1_, ...), custom_call_target="tpu_custom_call" | custom-call | flops 20000000000 | tf_op jit(solution)/shard_map/terms/pallas_call | solution.py:414
  27.4 1.6 %collective-permute-done.6.refs_0_ = bf16[400,128]{1,0:T(8,128)(2,1)S(1)} collective-permute-done((bf16[400,128]{1,0:T(8,128)(2,1)S(1)}, bf16[400,128]{1,0:T(8,128)(2,1)S(1)}, u32[]{:S(2)}, u32[]{:S(2)}) %collective-permute-start.6) | collective-permute-done | bytes 102432 | tf_op jit(solution)/shard_map/ppermute | solution.py:410
  29.0 1.4 %collective-permute-done.7.refs_1_ = bf16[400,128]{1,0:T(8,128)(2,1)S(1)} collective-permute-done((bf16[400,128]{1,0:T(8,128)(2,1)S(1)}, bf16[400,128]{1,0:T(8,128)(2,1)S(1)}, u32[]{:S(2)}, u32[]{:S(2)}) %collective-permute-start.7) | collective-permute-done | bytes 102432 | tf_op jit(solution)/shard_map/ppermute | solution.py:410
  32.4 2.6 %collective-permute-start.13 = (bf16[528,128]{1,0:T(8,128)(2,1)S(1)}, bf16[528,128]{1,0:T(8,128)(2,1)S(1)}, u32[]{:S(2)}, u32[]{:S(2)}) collective-permute-start(bf16[528,128]{1,0:T(8,128)(2,1)S(1)} %get-tuple-element.36.refs_0_), channel_id=1, source_target_pairs={{0,16},{4,20},{8,24},{12,28},{16,0},{20,4},{24,8},{28,12},{1,17},{... | collective-permute-start | bytes 405512 | tf_op jit(solution)/shard_map/ppermute | solution.py:410
  35.0 1.7 %collective-permute-done.9.refs_1_ = bf16[528,128]{1,0:T(8,128)(2,1)S(1)} collective-permute-done((bf16[528,128]{1,0:T(8,128)(2,1)S(1)}, bf16[528,128]{1,0:T(8,128)(2,1)S(1)}, u32[]{:S(2)}, u32[]{:S(2)}) %collective-permute-start.9) | collective-permute-done | bytes 135200 | tf_op jit(solution)/shard_map/ppermute | solution.py:410
  36.7 2.2 %all-gather.2 = bf16[4,528,128]{2,1,0:T(8,128)(2,1)S(1)} all-gather(bf16[2,528,128]{2,1,0:T(8,128)(2,1)S(1)} %join.9), channel_id=4, replica_groups={{0,1},{2,3},{4,5},{6,7},{8,9},{10,11},{12,13},{14,15},{16,17},{18,19},{..., dimensions={0}, use_global_device_ids=true | all-gather | bytes 811008 | tf_op jit(solution)/shard_map/all_gather | solution.py:435
  38.9 2.1 %collective-permute-done.13.refs_0_ = bf16[528,128]{1,0:T(8,128)(2,1)S(1)} collective-permute-done((bf16[528,128]{1,0:T(8,128)(2,1)S(1)}, bf16[528,128]{1,0:T(8,128)(2,1)S(1)}, u32[]{:S(2)}, u32[]{:S(2)}) %collective-permute-start.13) | collective-permute-done | bytes 135200 | tf_op jit(solution)/shard_map/ppermute | solution.py:410
  41.0 1.6 %collective-permute-start.14 = (bf16[528,128]{1,0:T(8,128)(2,1)S(1)}, bf16[528,128]{1,0:T(8,128)(2,1)S(1)}, u32[]{:S(2)}, u32[]{:S(2)}) collective-permute-start(bf16[528,128]{1,0:T(8,128)(2,1)S(1)} %join.10.refs_0_), channel_id=1, source_target_pairs={{0,2},{1,3},{2,0},{3,1},{4,6},{5,7},{6,4},{7,5},{8,10},{9,11},{10,... | collective-permute-start | bytes 405512 | tf_op jit(solution)/shard_map/ppermute | solution.py:410
  43.5 2.3 %collective-permute-start.11 = (bf16[400,128]{1,0:T(8,128)(2,1)S(1)}, bf16[400,128]{1,0:T(8,128)(2,1)S(1)}, u32[]{:S(2)}, u32[]{:S(2)}) collective-permute-start(bf16[400,128]{1,0:T(8,128)(2,1)S(1)} %get-tuple-element.39), channel_id=1, source_target_pairs={{0,8},{4,12},{8,0},{12,4},{16,24},{20,28},{24,16},{28,20},{1,9},{5... | collective-permute-start | bytes 307208 | tf_op jit(solution)/shard_map/ppermute | solution.py:410
  46.3 2.2 %all-gather.3 = bf16[4,528,128]{2,1,0:T(8,128)(2,1)S(1)} all-gather(bf16[2,528,128]{2,1,0:T(8,128)(2,1)S(1)} %join.11), channel_id=5, replica_groups={{0,1},{2,3},{4,5},{6,7},{8,9},{10,11},{12,13},{14,15},{16,17},{18,19},{..., dimensions={0}, use_global_device_ids=true | all-gather | bytes 811008 | tf_op jit(solution)/shard_map/all_gather | solution.py:440
  48.7 1.9 %collective-permute-start.15 = (bf16[400,128]{1,0:T(8,128)(2,1)S(1)}, bf16[400,128]{1,0:T(8,128)(2,1)S(1)}, u32[]{:S(2)}, u32[]{:S(2)}) collective-permute-start(bf16[400,128]{1,0:T(8,128)(2,1)S(1)} %get-tuple-element.42), channel_id=1, source_target_pairs={{0,12},{4,8},{8,4},{12,0},{16,28},{20,24},{24,20},{28,16},{1,13},{... | collective-permute-start | bytes 307208 | tf_op jit(solution)/shard_map/ppermute | solution.py:410
  52.3 1.4 %terms.3.before = f32[520,128]{1,0:T(8,128)S(1)} custom-call(s32[4,128]{1,0:T(4,128)S(1)} %copy-done.8, f32[4,128]{1,0:T(4,128)S(1)} %copy-done.9, bf16[4,16,128,128]{3,2,1,0:T(8,128)(2,1)S(1)} %copy-done, bf16[400,128]{1,0:T(8,128)(2,1)S(1)} %get-tuple-element.37.refs_2_.refs_0_, bf16[400,128]{1,0:T(8,128)(2,1)S(1)} %collective-permute-done.10.refs_1_, ...), custom_call_target="tpu_custom_call" | custom-call | flops 20000000000 | tf_op jit(solution)/shard_map/terms/pallas_call | solution.py:414
  53.7 1.7 %collective-permute-done.15.refs_0_ = bf16[400,128]{1,0:T(8,128)(2,1)S(1)} collective-permute-done((bf16[400,128]{1,0:T(8,128)(2,1)S(1)}, bf16[400,128]{1,0:T(8,128)(2,1)S(1)}, u32[]{:S(2)}, u32[]{:S(2)}) %collective-permute-start.15) | collective-permute-done | bytes 102432 | tf_op jit(solution)/shard_map/ppermute | solution.py:410
  55.4 1.4 %collective-permute-done.16.refs_1_ = bf16[400,128]{1,0:T(8,128)(2,1)S(1)} collective-permute-done((bf16[400,128]{1,0:T(8,128)(2,1)S(1)}, bf16[400,128]{1,0:T(8,128)(2,1)S(1)}, u32[]{:S(2)}, u32[]{:S(2)}) %collective-permute-start.16) | collective-permute-done | bytes 102432 | tf_op jit(solution)/shard_map/ppermute | solution.py:410
  56.9 1.8 %update.3 = (f32[4,128,128]{2,1,0:T(8,128)}, f32[4,128,128]{2,1,0:T(8,128)}) custom-call(s32[4,128]{1,0:T(4,128)S(1)} %copy-done.8, f32[4,128]{1,0:T(4,128)S(1)} %copy-done.9, s32[2,4]{1,0:T(2,128)S(1)} %bitcast.15, bf16[4,16,128,128]{3,2,1,0:T(8,128)(2,1)S(1)} %copy-done, f32[520,128]{1,0:T(8,128)S(1)} %terms.3.before, ...), custom_call_target="tpu_custom_call" | custom-call | tf_op jit(solution)/shard_map/update/pallas_call | solution.py:451
  (51 shorter events, 11.0 us)
Async XLA Ops:
  2.7 6.8 %collective-permute-start = (bf16[528,128]{1,0:T(8,128)(2,1)}, bf16[528,128]{1,0:T(8,128)(2,1)S(1)}, u32[]{:S(2)}, u32[]{:S(2)}) collective-permute-start(bf16[528,128]{1,0:T(8,128)(2,1)} %get-tuple-element.27.refs_0_), channel_id=1, source_target_pairs={{0,2},{1,3},{2,0},{3,1},{4,6},{5,7},{6,4},{7,5},{8,10},{9,11},{10,... | collective-permute-start | bytes 405512 | tf_op jit(solution)/shard_map/ppermute | solution.py:410
  5.7 9.1 %collective-permute-start.4 = (bf16[528,128]{1,0:T(8,128)(2,1)}, bf16[528,128]{1,0:T(8,128)(2,1)S(1)}, u32[]{:S(2)}, u32[]{:S(2)}) collective-permute-start(bf16[528,128]{1,0:T(8,128)(2,1)} %get-tuple-element.27.refs_0_), channel_id=1, source_target_pairs={{0,16},{4,20},{8,24},{12,28},{16,0},{20,4},{24,8},{28,12},{1,17},{... | collective-permute-start | bytes 405512 | tf_op jit(solution)/shard_map/ppermute | solution.py:410
  10.4 4.9 %copy-start.4 = (s32[8,128]{1,0:T(8,128)S(1)}, s32[8,128]{1,0:T(8,128)}, u32[]{:S(2)}) copy-start(s32[8,128]{1,0:T(8,128)} %get-tuple-element.26.index) | copy-start | bytes 12292
  10.4 15.4 %copy-start = (bf16[4,16,128,128]{3,2,1,0:T(8,128)(2,1)S(1)}, bf16[4,16,128,128]{3,2,1,0:T(8,128)(2,1)}, u32[]{:S(2)}) copy-start(bf16[4,16,128,128]{3,2,1,0:T(8,128)(2,1)} %intersections.7) | copy-start | bytes 6291460
  10.5 15.4 %copy-start.8 = (s32[4,128]{1,0:T(4,128)S(1)}, s32[4,128]{1,0:T(4,128)}, u32[]{:S(2)}) copy-start(s32[4,128]{1,0:T(4,128)} %get-tuple-element.24.index) | copy-start | bytes 6148
  10.5 15.4 %copy-start.9 = (f32[4,128]{1,0:T(4,128)S(1)}, f32[4,128]{1,0:T(4,128)}, u32[]{:S(2)}) copy-start(f32[4,128]{1,0:T(4,128)} %get-tuple-element.25.coefficients) | copy-start | bytes 6148
  14.8 5.1 %collective-permute-start.5 = (bf16[528,128]{1,0:T(8,128)(2,1)S(1)}, bf16[528,128]{1,0:T(8,128)(2,1)S(1)}, u32[]{:S(2)}, u32[]{:S(2)}) collective-permute-start(bf16[528,128]{1,0:T(8,128)(2,1)S(1)} %join.7.refs_0_), channel_id=1, source_target_pairs={{0,2},{1,3},{2,0},{3,1},{4,6},{5,7},{6,4},{7,5},{8,10},{9,11},{10,... | collective-permute-start | bytes 405512 | tf_op jit(solution)/shard_map/ppermute | solution.py:410
  15.6 9.8 %collective-permute-start.1 = (bf16[400,128]{1,0:T(8,128)(2,1)S(1)}, bf16[400,128]{1,0:T(8,128)(2,1)S(1)}, u32[]{:S(2)}, u32[]{:S(2)}) collective-permute-start(bf16[400,128]{1,0:T(8,128)(2,1)S(1)} %get-tuple-element.29), channel_id=1, source_target_pairs={{0,12},{4,8},{8,4},{12,0},{16,28},{20,24},{24,20},{28,16},{1,13},{... | collective-permute-start | bytes 307208 | tf_op jit(solution)/shard_map/ppermute | solution.py:410
  17.4 8.4 %collective-permute-start.2 = (bf16[400,128]{1,0:T(8,128)(2,1)S(1)}, bf16[400,128]{1,0:T(8,128)(2,1)S(1)}, u32[]{:S(2)}, u32[]{:S(2)}) collective-permute-start(bf16[400,128]{1,0:T(8,128)(2,1)S(1)} %get-tuple-element.30), channel_id=1, source_target_pairs={{0,8},{4,12},{8,0},{12,4},{16,24},{20,28},{24,16},{28,20},{1,9},{5... | collective-permute-start | bytes 307208 | tf_op jit(solution)/shard_map/ppermute | solution.py:410
  18.6 7.2 %collective-permute-start.3 = (bf16[400,128]{1,0:T(8,128)(2,1)S(1)}, bf16[400,128]{1,0:T(8,128)(2,1)S(1)}, u32[]{:S(2)}, u32[]{:S(2)}) collective-permute-start(bf16[400,128]{1,0:T(8,128)(2,1)S(1)} %get-tuple-element.31), channel_id=1, source_target_pairs={{0,4},{4,0},{8,12},{12,8},{16,20},{20,16},{24,28},{28,24},{1,5},{5... | collective-permute-start | bytes 307208 | tf_op jit(solution)/shard_map/ppermute | solution.py:410
  22.3 6.7 %collective-permute-start.6 = (bf16[400,128]{1,0:T(8,128)(2,1)S(1)}, bf16[400,128]{1,0:T(8,128)(2,1)S(1)}, u32[]{:S(2)}, u32[]{:S(2)}) collective-permute-start(bf16[400,128]{1,0:T(8,128)(2,1)S(1)} %get-tuple-element.33), channel_id=1, source_target_pairs={{0,12},{4,8},{8,4},{12,0},{16,28},{20,24},{24,20},{28,16},{1,13},{... | collective-permute-start | bytes 307208 | tf_op jit(solution)/shard_map/ppermute | solution.py:410
  24.6 5.9 %collective-permute-start.7 = (bf16[400,128]{1,0:T(8,128)(2,1)S(1)}, bf16[400,128]{1,0:T(8,128)(2,1)S(1)}, u32[]{:S(2)}, u32[]{:S(2)}) collective-permute-start(bf16[400,128]{1,0:T(8,128)(2,1)S(1)} %get-tuple-element.34), channel_id=1, source_target_pairs={{0,8},{4,12},{8,0},{12,4},{16,24},{20,28},{24,16},{28,20},{1,9},{5... | collective-permute-start | bytes 307208 | tf_op jit(solution)/shard_map/ppermute | solution.py:410
  25.3 5.1 %collective-permute-start.8 = (bf16[400,128]{1,0:T(8,128)(2,1)S(1)}, bf16[400,128]{1,0:T(8,128)(2,1)S(1)}, u32[]{:S(2)}, u32[]{:S(2)}) collective-permute-start(bf16[400,128]{1,0:T(8,128)(2,1)S(1)} %get-tuple-element.35), channel_id=1, source_target_pairs={{0,4},{4,0},{8,12},{12,8},{16,20},{20,16},{24,28},{28,24},{1,5},{5... | collective-permute-start | bytes 307208 | tf_op jit(solution)/shard_map/ppermute | solution.py:410
  25.9 4.6 %copy-start.1 = (f32[4,128,128]{2,1,0:T(8,128)S(1)}, f32[4,128,128]{2,1,0:T(8,128)}, u32[]{:S(2)}) copy-start(f32[4,128,128]{2,1,0:T(8,128)} %refs_3_.1) | copy-start | bytes 786436
  25.9 4.6 %copy-start.2 = (bf16[4,128,128]{2,1,0:T(8,128)(2,1)S(1)}, bf16[4,128,128]{2,1,0:T(8,128)(2,1)}, u32[]{:S(2)}) copy-start(bf16[4,128,128]{2,1,0:T(8,128)(2,1)} %refs_4_.3) | copy-start | bytes 393220
  31.6 5.1 %collective-permute-start.9 = (bf16[528,128]{1,0:T(8,128)(2,1)S(1)}, bf16[528,128]{1,0:T(8,128)(2,1)S(1)}, u32[]{:S(2)}, u32[]{:S(2)}) collective-permute-start(bf16[528,128]{1,0:T(8,128)(2,1)S(1)} %get-tuple-element.36.refs_0_), channel_id=1, source_target_pairs={{0,2},{1,3},{2,0},{3,1},{4,6},{5,7},{6,4},{7,5},{8,10},{9,11},{10,... | collective-permute-start | bytes 405512 | tf_op jit(solution)/shard_map/ppermute | solution.py:410
  32.4 8.6 %collective-permute-start.13 = (bf16[528,128]{1,0:T(8,128)(2,1)S(1)}, bf16[528,128]{1,0:T(8,128)(2,1)S(1)}, u32[]{:S(2)}, u32[]{:S(2)}) collective-permute-start(bf16[528,128]{1,0:T(8,128)(2,1)S(1)} %get-tuple-element.36.refs_0_), channel_id=1, source_target_pairs={{0,16},{4,20},{8,24},{12,28},{16,0},{20,4},{24,8},{28,12},{1,17},{... | collective-permute-start | bytes 405512 | tf_op jit(solution)/shard_map/ppermute | solution.py:410
  41.0 5.3 %collective-permute-start.14 = (bf16[528,128]{1,0:T(8,128)(2,1)S(1)}, bf16[528,128]{1,0:T(8,128)(2,1)S(1)}, u32[]{:S(2)}, u32[]{:S(2)}) collective-permute-start(bf16[528,128]{1,0:T(8,128)(2,1)S(1)} %join.10.refs_0_), channel_id=1, source_target_pairs={{0,2},{1,3},{2,0},{3,1},{4,6},{5,7},{6,4},{7,5},{8,10},{9,11},{10,... | collective-permute-start | bytes 405512 | tf_op jit(solution)/shard_map/ppermute | solution.py:410
  42.8 9.0 %collective-permute-start.10 = (bf16[400,128]{1,0:T(8,128)(2,1)S(1)}, bf16[400,128]{1,0:T(8,128)(2,1)S(1)}, u32[]{:S(2)}, u32[]{:S(2)}) collective-permute-start(bf16[400,128]{1,0:T(8,128)(2,1)S(1)} %get-tuple-element.38), channel_id=1, source_target_pairs={{0,12},{4,8},{8,4},{12,0},{16,28},{20,24},{24,20},{28,16},{1,13},{... | collective-permute-start | bytes 307208 | tf_op jit(solution)/shard_map/ppermute | solution.py:410
  43.5 8.8 %collective-permute-start.11 = (bf16[400,128]{1,0:T(8,128)(2,1)S(1)}, bf16[400,128]{1,0:T(8,128)(2,1)S(1)}, u32[]{:S(2)}, u32[]{:S(2)}) collective-permute-start(bf16[400,128]{1,0:T(8,128)(2,1)S(1)} %get-tuple-element.39), channel_id=1, source_target_pairs={{0,8},{4,12},{8,0},{12,4},{16,24},{20,28},{24,16},{28,20},{1,9},{5... | collective-permute-start | bytes 307208 | tf_op jit(solution)/shard_map/ppermute | solution.py:410
  45.8 6.5 %collective-permute-start.12 = (bf16[400,128]{1,0:T(8,128)(2,1)S(1)}, bf16[400,128]{1,0:T(8,128)(2,1)S(1)}, u32[]{:S(2)}, u32[]{:S(2)}) collective-permute-start(bf16[400,128]{1,0:T(8,128)(2,1)S(1)} %get-tuple-element.40), channel_id=1, source_target_pairs={{0,4},{4,0},{8,12},{12,8},{16,20},{20,16},{24,28},{28,24},{1,5},{5... | collective-permute-start | bytes 307208 | tf_op jit(solution)/shard_map/ppermute | solution.py:410
  48.7 6.7 %collective-permute-start.15 = (bf16[400,128]{1,0:T(8,128)(2,1)S(1)}, bf16[400,128]{1,0:T(8,128)(2,1)S(1)}, u32[]{:S(2)}, u32[]{:S(2)}) collective-permute-start(bf16[400,128]{1,0:T(8,128)(2,1)S(1)} %get-tuple-element.42), channel_id=1, source_target_pairs={{0,12},{4,8},{8,4},{12,0},{16,28},{20,24},{24,20},{28,16},{1,13},{... | collective-permute-start | bytes 307208 | tf_op jit(solution)/shard_map/ppermute | solution.py:410
  50.6 6.2 %collective-permute-start.16 = (bf16[400,128]{1,0:T(8,128)(2,1)S(1)}, bf16[400,128]{1,0:T(8,128)(2,1)S(1)}, u32[]{:S(2)}, u32[]{:S(2)}) collective-permute-start(bf16[400,128]{1,0:T(8,128)(2,1)S(1)} %get-tuple-element.43), channel_id=1, source_target_pairs={{0,8},{4,12},{8,0},{12,4},{16,24},{20,28},{24,16},{28,20},{1,9},{5... | collective-permute-start | bytes 307208 | tf_op jit(solution)/shard_map/ppermute | solution.py:410
  51.7 5.1 %collective-permute-start.17 = (bf16[400,128]{1,0:T(8,128)(2,1)S(1)}, bf16[400,128]{1,0:T(8,128)(2,1)S(1)}, u32[]{:S(2)}, u32[]{:S(2)}) collective-permute-start(bf16[400,128]{1,0:T(8,128)(2,1)S(1)} %get-tuple-element.44), channel_id=1, source_target_pairs={{0,4},{4,0},{8,12},{12,8},{16,20},{20,16},{24,28},{28,24},{1,5},{5... | collective-permute-start | bytes 307208 | tf_op jit(solution)/shard_map/ppermute | solution.py:410
  (4 other events, 14.5 us)

commit v6 on v5

--- a/solution.py
+++ b/solution.py
@@ -266,7 +266,11 @@
     index, coefficients, ends, intersections, before, *refs,
 ):
     blocks = refs[: len(places)]
-    state, integrals, energies, projector, out_a, out_b = refs[len(places) :]
+    state, integrals, energies, projector, out_a, out_b = refs[len(places) : len(places) + 6]
+    final = out_a, out_b
+    if last:
+        out_a, out_b, sems = refs[-3:]
+    copies = []
     per_device, width = state.shape[0], state.shape[1]
     coupling, singles = gather_terms(
         capacity, orbitals, index, coefficients, intersections, None, places, blocks, before
@@ -291,9 +295,14 @@
         out_a[s] = new
         if last:
             out_b[s] = residual
+            for i in range(2):
+                copies.append(pltpu.make_async_copy((out_a, out_b)[i].at[s], final[i].at[s], sems.at[i, s]))
+                copies[-1].start()
         else:
             out_b[pl.ds(s * width, width), :] = new.astype(BF16)
             total += singles_terms(new, proj, counts_a[s] + counts_b[s], eye)
+    for copy in copies:
+        copy.wait()
     if not last:
         tail = out_b.shape[0] - per_device * width
         out_b[pl.ds(per_device * width, tail), :] = tail_rows(total, tail)
@@ -349,9 +358,14 @@
             pltpu.VMEM(couplings.shape, F32),
             pltpu.SemaphoreType.DMA((6,)),
         ],
-        compiler_params=pltpu.CompilerParams(vmem_limit_bytes=WHOLE),
+        compiler_params=small if direct else pltpu.CompilerParams(vmem_limit_bytes=WHOLE),
         name="setup",
-    )(ends, amplitudes, projector, coupled.T, pair_slot.reshape(1, total), couplings)
+    )(
+        *[
+            pltpu.with_memory_space_constraint(x, pltpu.HBM)
+            for x in (ends, amplitudes, projector, coupled.T, pair_slot.reshape(1, total), couplings)
+        ]
+    )
 
     def join(*parts, after=()):
         def kernel(*refs):
@@ -375,10 +389,14 @@
     def select(row, flips, gathered):
         def kernel(index, source, *refs):
             outs, held = refs[: len(flips)], refs[-1]
-            for c in range(2):
-                for x in range(2):
-                    held[2 * x + c] = source[c, x]
-            swap = lax.axis_index("orb") // 2 * 2
+            swap = 0
+            if row:
+                swap = lax.axis_index("orb") // 2 * 2
+                for c in range(2):
+                    for x in range(2):
+                        held[2 * x + c] = source[c, x]
+            else:
+                held = source
             select_kernel(capacity, per_device, orbitals, width, flips, row, swap, index, held, outs)
 
         return pl.pallas_call(
@@ -431,17 +449,19 @@
             mirror = exchange(payload, "pairs", half)
             flips = [0, *range(half - 1, 0, -1)]
             cores = [[o, o + 1] for o in range(0, orb_count, 2)]
-            held = join(payload, exchange(payload, "orb", 2))
-            held = lax.all_gather(held, "orb", axis=0, axis_index_groups=cores)
-            sent = select(0, flips, held)
-            arrived = [sent[0]] + [exchange(part, "pairs", flip) for flip, part in zip(flips[1:], sent[1:])]
-            mirror = join(mirror, after=[held])
+            held = lax.all_gather(payload, "orb", axis=0, tiled=False)
+            across = pair_count - 1
+            order = [0, across, *flips[1:]]
+            sent = select(0, order, held)
+            arrived = [sent[0]] + [exchange(part, "pairs", flip) for flip, part in zip(order[1:], sent[1:])]
+            mirror = join(mirror, after=sent[:1])
             held = join(mirror, exchange(mirror, "orb", 2), after=arrived[:1])
             held = lax.all_gather(held, "orb", axis=0, axis_index_groups=cores)
-            sent = select(capacity, flips, held)
-            partial = terms(None, None, flips + [half], arrived + [sent[0]], EARLY)
-            places = [half + flip for flip in flips[1:]]
-            late = [exchange(part, "pairs", flip) for flip, part in zip(flips[1:], sent[1:])]
+            close = [flip for flip in flips if flip + half != across]
+            sent = select(capacity, close, held)
+            partial = terms(None, None, [*order, half], arrived + [sent[0]], EARLY)
+            places = [half + flip for flip in close[1:]]
+            late = [exchange(part, "pairs", flip) for flip, part in zip(close[1:], sent[1:])]
         else:
             gathered = lax.all_gather(payload, "orb", axis=0, tiled=False)
             outgoing = select_all(gathered)
@@ -452,7 +472,14 @@
             functools.partial(update_kernel, last, capacity, orbitals, places),
             out_shape=(jax.ShapeDtypeStruct(amplitudes.shape, F32), second),
             in_specs=[VMEM] * (9 + len(late)),
-            out_specs=(VMEM, VMEM),
+            out_specs=(HBM, HBM) if last else (VMEM, VMEM),
+            scratch_shapes=[
+                pltpu.VMEM(amplitudes.shape, F32),
+                pltpu.VMEM(amplitudes.shape, F32),
+                pltpu.SemaphoreType.DMA((2, per_device)),
+            ]
+            if last
+            else [],
             compiler_params=params,
             name="update",
         )(

time: 58.9 us -> 55.5 us (0.942)
  blocking collectives: 8.9 us -> 18.6 us
  waiting for transfers between devices: 14 us -> 5.35 us
  starting transfers between devices: 25.3 us -> 22.8 us
  Pallas kernels: 8.72 us -> 7.75 us
  local copies, waits for them, and re-layouts: 0.96 us -> 0.03 us
    all_gather x0 -> x2, blocking collectives: none -> 14.2 us  [body(): held = lax.all_gather(payload, 'orb', axis=0, tiled=False)]
    ppermute x18 -> x16, waiting for transfers between devices: 14 us -> 5.35 us  [exchange(): lax.ppermute(block, axis, [(p, p ^ flip) for p in range(pair_count * orb_...]
    all_gather x4 -> x2, blocking collectives: 8.9 us -> 4.39 us  [body(): held = lax.all_gather(held, 'orb', axis=0, axis_index_groups=cores)]
    ppermute x18 -> x16, starting transfers between devices: 25.3 us -> 22.8 us  [exchange(): lax.ppermute(block, axis, [(p, p ^ flip) for p in range(pair_count * orb_...]
    unnamed x20 -> x12, local copies, waits for them, and re-layouts: 0.96 us -> 0.03 us
    pallas_call x2, Pallas kernels: 2.97 us -> 2.27 us  [body(): pl.pallas_call(functools.partial(update_kernel, last, capacity, orbitals,...]
  transfers between devices with their start and end apart: 18 -> 16, of which waited for: 9 -> 8; matrix products, arithmetic and copies ran while one was open for 0% -> 0% of each run, Pallas kernels for 6% -> 7%
where the time goes in v6:
time: 55.5 us; the launch traced here: 55.3 us
  starting transfers between devices  22.8 us (41%)
  blocking collectives  18.6 us (34%)
  Pallas kernels  7.75 us (14%)
  waiting for transfers between devices  5.35 us (10%)
  between operations  0.8 us (1%)
    ppermute x16, starting transfers between devices, exchange(): lax.ppermute(block, axis, [(p, p ^ flip) for p in range(pair_count * orb_...  22.8 us
    all_gather x2, blocking collectives, body(): held = lax.all_gather(payload, 'orb', axis=0, tiled=False)  14.2 us
    ppermute x16, waiting for transfers between devices, exchange(): lax.ppermute(block, axis, [(p, p ^ flip) for p in range(pair_count * orb_...  5.35 us
    all_gather x2, blocking collectives, body(): held = lax.all_gather(held, 'orb', axis=0, axis_index_groups=cores)  4.39 us
    pallas_call x2, Pallas kernels, terms(): pl.pallas_call(functools.partial(terms_kernel, capacity, orbitals, before...  3.17 us
    pallas_call x2, Pallas kernels, body(): pl.pallas_call(functools.partial(update_kernel, last, capacity, orbitals,...  2.27 us
    pallas_call x1, Pallas kernels, body(): pl.pallas_call(functools.partial(setup_kernel, capacity, orbitals, near,...  1.57 us
  transfers between devices with their start and end apart: 16, of which 8 were waited for; matrix products, arithmetic and copies ran while one was open for 0% of the time, Pallas kernels for 7%

profile of v6, /device:TPU:0, one launch (start us, length us, event | category | flops | bytes accessed | tf_op | source)
XLA Modules:
  0.0 55.3 jit_solution(15432821546512540170)
XLA Ops:
  0.6 1.6 %setup.1 = (bf16[528,128]{1,0:T(8,128)(2,1)S(1)}, s32[8,128]{1,0:T(8,128)S(1)}, s32[4,128]{1,0:T(4,128)S(1)}, f32[4,128]{1,0:T(4,128)S(1)}) custom-call(s32[2,4]{1,0:T(2,128)} %bitcast.11, f32[4,128,128]{2,1,0:T(8,128)} %refs_2_.1, f32[4,128]{1,0:T(4,128)} %refs_5_.3, s32[16,128]{1,0:T(8,128)} %bitcast.14, s32[1,128]{1,0:T(1,128)} %bitcast.15, ...), custom_call_target="tpu_custom_call" | custom-call | tf_op jit(solution)/shard_map/setup/pallas_call | solution.py:342
  2.2 4.1 %collective-permute-start.4 = (bf16[528,128]{1,0:T(8,128)(2,1)S(1)}, bf16[528,128]{1,0:T(8,128)(2,1)S(1)}, u32[]{:S(2)}, u32[]{:S(2)}) collective-permute-start(bf16[528,128]{1,0:T(8,128)(2,1)S(1)} %get-tuple-element.27), channel_id=1, source_target_pairs={{0,16},{4,20},{8,24},{12,28},{16,0},{20,4},{24,8},{28,12},{1,17},{... | collective-permute-start | bytes 405512 | tf_op jit(solution)/shard_map/ppermute | solution.py:428
  6.3 7.2 %all-gather = bf16[2112,128]{1,0:T(8,128)(2,1)S(1)} all-gather(bf16[528,128]{1,0:T(8,128)(2,1)S(1)} %get-tuple-element.27), channel_id=2, replica_groups=mesh['pairs'=8,'orb'=4] {'orb'}, dimensions={0}, use_global_device_ids=true | all-gather | bytes 675840 | tf_op jit(solution)/shard_map/all_gather | solution.py:452
  13.8 0.9 %collective-permute-start.5 = (bf16[528,128]{1,0:T(8,128)(2,1)S(1)}, bf16[528,128]{1,0:T(8,128)(2,1)S(1)}, u32[]{:S(2)}, u32[]{:S(2)}) collective-permute-start(bf16[528,128]{1,0:T(8,128)(2,1)S(1)} %join.4.refs_0_), channel_id=1, source_target_pairs={{0,2},{1,3},{2,0},{3,1},{4,6},{5,7},{6,4},{7,5},{8,10},{9,11},{10,... | collective-permute-start | bytes 405512 | tf_op jit(solution)/shard_map/ppermute | solution.py:428
  14.7 4.2 %collective-permute-start = (bf16[400,128]{1,0:T(8,128)(2,1)S(1)}, bf16[400,128]{1,0:T(8,128)(2,1)S(1)}, u32[]{:S(2)}, u32[]{:S(2)}) collective-permute-start(bf16[400,128]{1,0:T(8,128)(2,1)S(1)} %get-tuple-element.29), channel_id=1, source_target_pairs={{0,28},{4,24},{8,20},{12,16},{16,12},{20,8},{24,4},{28,0},{1,29},{... | collective-permute-start | bytes 307208 | tf_op jit(solution)/shard_map/ppermute | solution.py:428
  18.9 2.0 %collective-permute-start.2 = (bf16[400,128]{1,0:T(8,128)(2,1)S(1)}, bf16[400,128]{1,0:T(8,128)(2,1)S(1)}, u32[]{:S(2)}, u32[]{:S(2)}) collective-permute-start(bf16[400,128]{1,0:T(8,128)(2,1)S(1)} %get-tuple-element.31), channel_id=1, source_target_pairs={{0,8},{4,12},{8,0},{12,4},{16,24},{20,28},{24,16},{28,20},{1,9},{5... | collective-permute-start | bytes 307208 | tf_op jit(solution)/shard_map/ppermute | solution.py:428
  20.8 1.5 %collective-permute-start.3 = (bf16[400,128]{1,0:T(8,128)(2,1)S(1)}, bf16[400,128]{1,0:T(8,128)(2,1)S(1)}, u32[]{:S(2)}, u32[]{:S(2)}) collective-permute-start(bf16[400,128]{1,0:T(8,128)(2,1)S(1)} %get-tuple-element.32), channel_id=1, source_target_pairs={{0,4},{4,0},{8,12},{12,8},{16,20},{20,16},{24,28},{28,24},{1,5},{5... | collective-permute-start | bytes 307208 | tf_op jit(solution)/shard_map/ppermute | solution.py:428
  22.4 2.2 %all-gather.1 = bf16[4,528,128]{2,1,0:T(8,128)(2,1)S(1)} all-gather(bf16[2,528,128]{2,1,0:T(8,128)(2,1)S(1)} %join.5), channel_id=3, replica_groups={{0,1},{2,3},{4,5},{6,7},{8,9},{10,11},{12,13},{14,15},{16,17},{18,19},{..., dimensions={0}, use_global_device_ids=true | all-gather | bytes 811008 | tf_op jit(solution)/shard_map/all_gather | solution.py:459
  24.8 0.6 %collective-permute-start.7 = (bf16[400,128]{1,0:T(8,128)(2,1)S(1)}, bf16[400,128]{1,0:T(8,128)(2,1)S(1)}, u32[]{:S(2)}, u32[]{:S(2)}) collective-permute-start(bf16[400,128]{1,0:T(8,128)(2,1)S(1)} %get-tuple-element.35), channel_id=1, source_target_pairs={{0,4},{4,0},{8,12},{12,8},{16,20},{20,16},{24,28},{28,24},{1,5},{5... | collective-permute-start | bytes 307208 | tf_op jit(solution)/shard_map/ppermute | solution.py:428
  25.6 1.2 %collective-permute-done.2.refs_3_ = bf16[400,128]{1,0:T(8,128)(2,1)S(1)} collective-permute-done((bf16[400,128]{1,0:T(8,128)(2,1)S(1)}, bf16[400,128]{1,0:T(8,128)(2,1)S(1)}, u32[]{:S(2)}, u32[]{:S(2)}) %collective-permute-start.2) | collective-permute-done | bytes 102432 | tf_op jit(solution)/shard_map/ppermute | solution.py:428
  26.9 1.6 %terms.2.before = f32[520,128]{1,0:T(8,128)S(1)} custom-call(s32[4,128]{1,0:T(4,128)S(1)} %get-tuple-element.24.index, f32[4,128]{1,0:T(4,128)S(1)} %get-tuple-element.25.coefficients, bf16[4,16,128,128]{3,2,1,0:T(8,128)(2,1)S(1)} %copy-done, bf16[400,128]{1,0:T(8,128)(2,1)S(1)} %get-tuple-element.28.refs_1_.refs_2_.refs_0_, ...), custom_call_target="tpu_custom_call" | custom-call | flops 20000000000 | tf_op jit(solution)/shard_map/terms/pallas_call | solution.py:432
  28.5 1.2 %collective-permute-done.6.refs_0_ = bf16[400,128]{1,0:T(8,128)(2,1)S(1)} collective-permute-done((bf16[400,128]{1,0:T(8,128)(2,1)S(1)}, bf16[400,128]{1,0:T(8,128)(2,1)S(1)}, u32[]{:S(2)}, u32[]{:S(2)}) %collective-permute-start.6) | collective-permute-done | bytes 102432 | tf_op jit(solution)/shard_map/ppermute | solution.py:428
  29.8 0.8 %update.2 = (f32[4,128,128]{2,1,0:T(8,128)S(1)}, bf16[528,128]{1,0:T(8,128)(2,1)S(1)}) custom-call(s32[4,128]{1,0:T(4,128)S(1)} %get-tuple-element.24.index, f32[4,128]{1,0:T(4,128)S(1)} %get-tuple-element.25.coefficients, s32[2,4]{1,0:T(2,128)S(1)} %bitcast.12, bf16[4,16,128,128]{3,2,1,0:T(8,128)(2,1)S(1)} %copy-done, f32[520,128]{1,0:T(8,128)S(1)} %terms.2.before, ...), custom_call_target="tpu_custom_call" | custom-call | tf_op jit(solution)/shard_map/update/pallas_call | solution.py:471
  30.7 0.9 %collective-permute-start.12 = (bf16[528,128]{1,0:T(8,128)(2,1)S(1)}, bf16[528,128]{1,0:T(8,128)(2,1)S(1)}, u32[]{:S(2)}, u32[]{:S(2)}) collective-permute-start(bf16[528,128]{1,0:T(8,128)(2,1)S(1)} %get-tuple-element.36), channel_id=1, source_target_pairs={{0,16},{4,20},{8,24},{12,28},{16,0},{20,4},{24,8},{28,12},{1,17},{... | collective-permute-start | bytes 405512 | tf_op jit(solution)/shard_map/ppermute | solution.py:428
  31.5 7.0 %all-gather.2 = bf16[2112,128]{1,0:T(8,128)(2,1)S(1)} all-gather(bf16[528,128]{1,0:T(8,128)(2,1)S(1)} %get-tuple-element.36), channel_id=4, replica_groups=mesh['pairs'=8,'orb'=4] {'orb'}, dimensions={0}, use_global_device_ids=true | all-gather | bytes 675840 | tf_op jit(solution)/shard_map/all_gather | solution.py:452
  38.7 0.6 %collective-permute-done.12.refs_0_ = bf16[528,128]{1,0:T(8,128)(2,1)S(1)} collective-permute-done((bf16[528,128]{1,0:T(8,128)(2,1)S(1)}, bf16[528,128]{1,0:T(8,128)(2,1)S(1)}, u32[]{:S(2)}, u32[]{:S(2)}) %collective-permute-start.12) | collective-permute-done | bytes 135200 | tf_op jit(solution)/shard_map/ppermute | solution.py:428
  39.3 0.6 %collective-permute-start.13 = (bf16[528,128]{1,0:T(8,128)(2,1)S(1)}, bf16[528,128]{1,0:T(8,128)(2,1)S(1)}, u32[]{:S(2)}, u32[]{:S(2)}) collective-permute-start(bf16[528,128]{1,0:T(8,128)(2,1)S(1)} %join.6.refs_0_), channel_id=1, source_target_pairs={{0,2},{1,3},{2,0},{3,1},{4,6},{5,7},{6,4},{7,5},{8,10},{9,11},{10,... | collective-permute-start | bytes 405512 | tf_op jit(solution)/shard_map/ppermute | solution.py:428
  40.0 2.8 %collective-permute-start.8 = (bf16[400,128]{1,0:T(8,128)(2,1)S(1)}, bf16[400,128]{1,0:T(8,128)(2,1)S(1)}, u32[]{:S(2)}, u32[]{:S(2)}) collective-permute-start(bf16[400,128]{1,0:T(8,128)(2,1)S(1)} %get-tuple-element.38), channel_id=1, source_target_pairs={{0,28},{4,24},{8,20},{12,16},{16,12},{20,8},{24,4},{28,0},{1,29},{... | collective-permute-start | bytes 307208 | tf_op jit(solution)/shard_map/ppermute | solution.py:428
  43.2 2.6 %collective-permute-start.10 = (bf16[400,128]{1,0:T(8,128)(2,1)S(1)}, bf16[400,128]{1,0:T(8,128)(2,1)S(1)}, u32[]{:S(2)}, u32[]{:S(2)}) collective-permute-start(bf16[400,128]{1,0:T(8,128)(2,1)S(1)} %get-tuple-element.40), channel_id=1, source_target_pairs={{0,8},{4,12},{8,0},{12,4},{16,24},{20,28},{24,16},{28,20},{1,9},{5... | collective-permute-start | bytes 307208 | tf_op jit(solution)/shard_map/ppermute | solution.py:428
  46.3 2.2 %all-gather.3 = bf16[4,528,128]{2,1,0:T(8,128)(2,1)S(1)} all-gather(bf16[2,528,128]{2,1,0:T(8,128)(2,1)S(1)} %join.7), channel_id=5, replica_groups={{0,1},{2,3},{4,5},{6,7},{8,9},{10,11},{12,13},{14,15},{16,17},{18,19},{..., dimensions={0}, use_global_device_ids=true | all-gather | bytes 811008 | tf_op jit(solution)/shard_map/all_gather | solution.py:459
  48.8 1.5 %collective-permute-start.15 = (bf16[400,128]{1,0:T(8,128)(2,1)S(1)}, bf16[400,128]{1,0:T(8,128)(2,1)S(1)}, u32[]{:S(2)}, u32[]{:S(2)}) collective-permute-start(bf16[400,128]{1,0:T(8,128)(2,1)S(1)} %get-tuple-element.44), channel_id=1, source_target_pairs={{0,4},{4,0},{8,12},{12,8},{16,20},{20,16},{24,28},{28,24},{1,5},{5... | collective-permute-start | bytes 307208 | tf_op jit(solution)/shard_map/ppermute | solution.py:428
  50.3 1.5 %collective-permute-done.10.refs_3_ = bf16[400,128]{1,0:T(8,128)(2,1)S(1)} collective-permute-done((bf16[400,128]{1,0:T(8,128)(2,1)S(1)}, bf16[400,128]{1,0:T(8,128)(2,1)S(1)}, u32[]{:S(2)}, u32[]{:S(2)}) %collective-permute-start.10) | collective-permute-done | bytes 102432 | tf_op jit(solution)/shard_map/ppermute | solution.py:428
  51.8 1.6 %terms.3.before = f32[520,128]{1,0:T(8,128)S(1)} custom-call(s32[4,128]{1,0:T(4,128)S(1)} %get-tuple-element.24.index, f32[4,128]{1,0:T(4,128)S(1)} %get-tuple-element.25.coefficients, bf16[4,16,128,128]{3,2,1,0:T(8,128)(2,1)S(1)} %copy-done, bf16[400,128]{1,0:T(8,128)(2,1)S(1)} %get-tuple-element.37.refs_1_.refs_2_.refs_0_, ...), custom_call_target="tpu_custom_call" | custom-call | flops 20000000000 | tf_op jit(solution)/shard_map/terms/pallas_call | solution.py:432
  53.9 1.4 %update.3 = (f32[4,128,128]{2,1,0:T(8,128)}, f32[4,128,128]{2,1,0:T(8,128)}) custom-call(s32[4,128]{1,0:T(4,128)S(1)} %get-tuple-element.24.index, f32[4,128]{1,0:T(4,128)S(1)} %get-tuple-element.25.coefficients, s32[2,4]{1,0:T(2,128)S(1)} %bitcast.13, bf16[4,16,128,128]{3,2,1,0:T(8,128)(2,1)S(1)} %copy-done, f32[520,128]{1,0:T(8,128)S(1)} %terms.3.before, ...), custom_call_target="tpu_custom_call" | custom-call | tf_op jit(solution)/shard_map/update/pallas_call | solution.py:471
  (37 shorter events, 2.7 us)
Async XLA Ops:
  0.6 26.2 %copy-start = (bf16[4,16,128,128]{3,2,1,0:T(8,128)(2,1)S(1)}, bf16[4,16,128,128]{3,2,1,0:T(8,128)(2,1)}, u32[]{:S(2)}) copy-start(bf16[4,16,128,128]{3,2,1,0:T(8,128)(2,1)} %intersections.7) | copy-start | bytes 6291460
  2.2 11.5 %collective-permute-start.4 = (bf16[528,128]{1,0:T(8,128)(2,1)S(1)}, bf16[528,128]{1,0:T(8,128)(2,1)S(1)}, u32[]{:S(2)}, u32[]{:S(2)}) collective-permute-start(bf16[528,128]{1,0:T(8,128)(2,1)S(1)} %get-tuple-element.27), channel_id=1, source_target_pairs={{0,16},{4,20},{8,24},{12,28},{16,0},{20,4},{24,8},{28,12},{1,17},{... | collective-permute-start | bytes 405512 | tf_op jit(solution)/shard_map/ppermute | solution.py:428
  13.8 8.6 %collective-permute-start.5 = (bf16[528,128]{1,0:T(8,128)(2,1)S(1)}, bf16[528,128]{1,0:T(8,128)(2,1)S(1)}, u32[]{:S(2)}, u32[]{:S(2)}) collective-permute-start(bf16[528,128]{1,0:T(8,128)(2,1)S(1)} %join.4.refs_0_), channel_id=1, source_target_pairs={{0,2},{1,3},{2,0},{3,1},{4,6},{5,7},{6,4},{7,5},{8,10},{9,11},{10,... | collective-permute-start | bytes 405512 | tf_op jit(solution)/shard_map/ppermute | solution.py:428
  14.7 10.1 %collective-permute-start = (bf16[400,128]{1,0:T(8,128)(2,1)S(1)}, bf16[400,128]{1,0:T(8,128)(2,1)S(1)}, u32[]{:S(2)}, u32[]{:S(2)}) collective-permute-start(bf16[400,128]{1,0:T(8,128)(2,1)S(1)} %get-tuple-element.29), channel_id=1, source_target_pairs={{0,28},{4,24},{8,20},{12,16},{16,12},{20,8},{24,4},{28,0},{1,29},{... | collective-permute-start | bytes 307208 | tf_op jit(solution)/shard_map/ppermute | solution.py:428
  18.9 6.7 %collective-permute-start.1 = (bf16[400,128]{1,0:T(8,128)(2,1)S(1)}, bf16[400,128]{1,0:T(8,128)(2,1)S(1)}, u32[]{:S(2)}, u32[]{:S(2)}) collective-permute-start(bf16[400,128]{1,0:T(8,128)(2,1)S(1)} %get-tuple-element.30), channel_id=1, source_target_pairs={{0,12},{4,8},{8,4},{12,0},{16,28},{20,24},{24,20},{28,16},{1,13},{... | collective-permute-start | bytes 307208 | tf_op jit(solution)/shard_map/ppermute | solution.py:428
  18.9 7.9 %collective-permute-start.2 = (bf16[400,128]{1,0:T(8,128)(2,1)S(1)}, bf16[400,128]{1,0:T(8,128)(2,1)S(1)}, u32[]{:S(2)}, u32[]{:S(2)}) collective-permute-start(bf16[400,128]{1,0:T(8,128)(2,1)S(1)} %get-tuple-element.31), channel_id=1, source_target_pairs={{0,8},{4,12},{8,0},{12,4},{16,24},{20,28},{24,16},{28,20},{1,9},{5... | collective-permute-start | bytes 307208 | tf_op jit(solution)/shard_map/ppermute | solution.py:428
  20.8 6.0 %collective-permute-start.3 = (bf16[400,128]{1,0:T(8,128)(2,1)S(1)}, bf16[400,128]{1,0:T(8,128)(2,1)S(1)}, u32[]{:S(2)}, u32[]{:S(2)}) collective-permute-start(bf16[400,128]{1,0:T(8,128)(2,1)S(1)} %get-tuple-element.32), channel_id=1, source_target_pairs={{0,4},{4,0},{8,12},{12,8},{16,20},{20,16},{24,28},{28,24},{1,5},{5... | collective-permute-start | bytes 307208 | tf_op jit(solution)/shard_map/ppermute | solution.py:428
  24.7 5.0 %collective-permute-start.6 = (bf16[400,128]{1,0:T(8,128)(2,1)S(1)}, bf16[400,128]{1,0:T(8,128)(2,1)S(1)}, u32[]{:S(2)}, u32[]{:S(2)}) collective-permute-start(bf16[400,128]{1,0:T(8,128)(2,1)S(1)} %get-tuple-element.34), channel_id=1, source_target_pairs={{0,8},{4,12},{8,0},{12,4},{16,24},{20,28},{24,16},{28,20},{1,9},{5... | collective-permute-start | bytes 307208 | tf_op jit(solution)/shard_map/ppermute | solution.py:428
  24.8 5.0 %collective-permute-start.7 = (bf16[400,128]{1,0:T(8,128)(2,1)S(1)}, bf16[400,128]{1,0:T(8,128)(2,1)S(1)}, u32[]{:S(2)}, u32[]{:S(2)}) collective-permute-start(bf16[400,128]{1,0:T(8,128)(2,1)S(1)} %get-tuple-element.35), channel_id=1, source_target_pairs={{0,4},{4,0},{8,12},{12,8},{16,20},{20,16},{24,28},{28,24},{1,5},{5... | collective-permute-start | bytes 307208 | tf_op jit(solution)/shard_map/ppermute | solution.py:428
  26.9 2.9 %copy-start.1 = (f32[4,128,128]{2,1,0:T(8,128)S(1)}, f32[4,128,128]{2,1,0:T(8,128)}, u32[]{:S(2)}) copy-start(f32[4,128,128]{2,1,0:T(8,128)} %refs_2_.1) | copy-start | bytes 786436
  26.9 2.9 %copy-start.2 = (bf16[4,128,128]{2,1,0:T(8,128)(2,1)S(1)}, bf16[4,128,128]{2,1,0:T(8,128)(2,1)}, u32[]{:S(2)}) copy-start(bf16[4,128,128]{2,1,0:T(8,128)(2,1)} %refs_3_.3) | copy-start | bytes 393220
  26.9 2.9 %copy-start.3 = (f32[4,128]{1,0:T(4,128)S(1)}, f32[4,128]{1,0:T(4,128)}, u32[]{:S(2)}) copy-start(f32[4,128]{1,0:T(4,128)} %refs_5_.3) | copy-start | bytes 6148
  26.9 2.9 %copy-start.4 = (s32[4,2]{0,1:T(2,128)S(1)}, s32[4,2]{0,1:T(2,128)}, u32[]{:S(2)}) copy-start(s32[4,2]{0,1:T(2,128)} %param.15) | copy-start | bytes 100
  26.9 2.9 %copy-start.5 = (f32[4,128]{1,0:T(4,128)S(1)}, f32[4,128]{1,0:T(4,128)}, u32[]{:S(2)}) copy-start(f32[4,128]{1,0:T(4,128)} %refs_4_.3) | copy-start | bytes 6148
  30.7 8.7 %collective-permute-start.12 = (bf16[528,128]{1,0:T(8,128)(2,1)S(1)}, bf16[528,128]{1,0:T(8,128)(2,1)S(1)}, u32[]{:S(2)}, u32[]{:S(2)}) collective-permute-start(bf16[528,128]{1,0:T(8,128)(2,1)S(1)} %get-tuple-element.36), channel_id=1, source_target_pairs={{0,16},{4,20},{8,24},{12,28},{16,0},{20,4},{24,8},{28,12},{1,17},{... | collective-permute-start | bytes 405512 | tf_op jit(solution)/shard_map/ppermute | solution.py:428
  39.3 6.9 %collective-permute-start.13 = (bf16[528,128]{1,0:T(8,128)(2,1)S(1)}, bf16[528,128]{1,0:T(8,128)(2,1)S(1)}, u32[]{:S(2)}, u32[]{:S(2)}) collective-permute-start(bf16[528,128]{1,0:T(8,128)(2,1)S(1)} %join.6.refs_0_), channel_id=1, source_target_pairs={{0,2},{1,3},{2,0},{3,1},{4,6},{5,7},{6,4},{7,5},{8,10},{9,11},{10,... | collective-permute-start | bytes 405512 | tf_op jit(solution)/shard_map/ppermute | solution.py:428
  40.0 8.8 %collective-permute-start.8 = (bf16[400,128]{1,0:T(8,128)(2,1)S(1)}, bf16[400,128]{1,0:T(8,128)(2,1)S(1)}, u32[]{:S(2)}, u32[]{:S(2)}) collective-permute-start(bf16[400,128]{1,0:T(8,128)(2,1)S(1)} %get-tuple-element.38), channel_id=1, source_target_pairs={{0,28},{4,24},{8,20},{12,16},{16,12},{20,8},{24,4},{28,0},{1,29},{... | collective-permute-start | bytes 307208 | tf_op jit(solution)/shard_map/ppermute | solution.py:428
  42.8 7.5 %collective-permute-start.9 = (bf16[400,128]{1,0:T(8,128)(2,1)S(1)}, bf16[400,128]{1,0:T(8,128)(2,1)S(1)}, u32[]{:S(2)}, u32[]{:S(2)}) collective-permute-start(bf16[400,128]{1,0:T(8,128)(2,1)S(1)} %get-tuple-element.39), channel_id=1, source_target_pairs={{0,12},{4,8},{8,4},{12,0},{16,28},{20,24},{24,20},{28,16},{1,13},{... | collective-permute-start | bytes 307208 | tf_op jit(solution)/shard_map/ppermute | solution.py:428
  43.2 8.6 %collective-permute-start.10 = (bf16[400,128]{1,0:T(8,128)(2,1)S(1)}, bf16[400,128]{1,0:T(8,128)(2,1)S(1)}, u32[]{:S(2)}, u32[]{:S(2)}) collective-permute-start(bf16[400,128]{1,0:T(8,128)(2,1)S(1)} %get-tuple-element.40), channel_id=1, source_target_pairs={{0,8},{4,12},{8,0},{12,4},{16,24},{20,28},{24,16},{28,20},{1,9},{5... | collective-permute-start | bytes 307208 | tf_op jit(solution)/shard_map/ppermute | solution.py:428
  45.8 6.0 %collective-permute-start.11 = (bf16[400,128]{1,0:T(8,128)(2,1)S(1)}, bf16[400,128]{1,0:T(8,128)(2,1)S(1)}, u32[]{:S(2)}, u32[]{:S(2)}) collective-permute-start(bf16[400,128]{1,0:T(8,128)(2,1)S(1)} %get-tuple-element.41), channel_id=1, source_target_pairs={{0,4},{4,0},{8,12},{12,8},{16,20},{20,16},{24,28},{28,24},{1,5},{5... | collective-permute-start | bytes 307208 | tf_op jit(solution)/shard_map/ppermute | solution.py:428
  48.7 5.2 %collective-permute-start.14 = (bf16[400,128]{1,0:T(8,128)(2,1)S(1)}, bf16[400,128]{1,0:T(8,128)(2,1)S(1)}, u32[]{:S(2)}, u32[]{:S(2)}) collective-permute-start(bf16[400,128]{1,0:T(8,128)(2,1)S(1)} %get-tuple-element.43), channel_id=1, source_target_pairs={{0,8},{4,12},{8,0},{12,4},{16,24},{20,28},{24,16},{28,20},{1,9},{5... | collective-permute-start | bytes 307208 | tf_op jit(solution)/shard_map/ppermute | solution.py:428
  48.8 5.1 %collective-permute-start.15 = (bf16[400,128]{1,0:T(8,128)(2,1)S(1)}, bf16[400,128]{1,0:T(8,128)(2,1)S(1)}, u32[]{:S(2)}, u32[]{:S(2)}) collective-permute-start(bf16[400,128]{1,0:T(8,128)(2,1)S(1)} %get-tuple-element.44), channel_id=1, source_target_pairs={{0,4},{4,0},{8,12},{12,8},{16,20},{20,16},{24,28},{28,24},{1,5},{5... | collective-permute-start | bytes 307208 | tf_op jit(solution)/shard_map/ppermute | solution.py:428

commit v7 on v6

--- a/solution.py
+++ b/solution.py
@@ -11,8 +11,7 @@
 ITERS = 2
 ROWS = 16
 PARTS = 3
-EARLY = 20_000_000_000
-CLOSE = 1_000_000_000
+TERMS_COST = 20_000_000_000
 
 F32 = jnp.float32
 BF16 = jnp.bfloat16
@@ -245,15 +244,11 @@
     return coupling, singles
 
 
-def terms_kernel(
-    capacity, orbitals, has_before, has_every, places, index, coefficients, intersections, *refs
-):
-    out = refs[-1]
-    refs = list(refs[:-1])
-    before = refs.pop(0) if has_before else None
+def terms_kernel(capacity, orbitals, has_every, places, index, coefficients, intersections, *refs):
+    refs, out = list(refs[:-1]), refs[-1]
     every = refs.pop(0) if has_every else None
     coupling, singles = gather_terms(
-        capacity, orbitals, index, coefficients, intersections, every, places, refs, before
+        capacity, orbitals, index, coefficients, intersections, every, places, refs, None
     )
     width = intersections.shape[2]
     for s, part in enumerate(coupling):
@@ -425,18 +420,16 @@
         )(send_index, gathered)
 
     def exchange(block, axis, flip):
-        return lax.ppermute(block, axis, [(p, p ^ flip) for p in range(pair_count * orb_count if isinstance(axis, tuple) else lax.axis_size(axis))])
-
-    def terms(before, every, places, blocks, flops):
-        extra = [x for x in (before, every) if x is not None]
+        return lax.ppermute(block, axis, [(p, p ^ flip) for p in range(lax.axis_size(axis))])
+
+    def terms(every, places, blocks):
+        extra = [] if every is None else [every]
         return pl.pallas_call(
-            functools.partial(
-                terms_kernel, capacity, orbitals, before is not None, every is not None, places
-            ),
+            functools.partial(terms_kernel, capacity, orbitals, every is not None, places),
             out_shape=terms_shape,
             in_specs=[tables, tables] + [VMEM] * (1 + len(extra) + len(blocks)),
             out_specs=VMEM,
-            cost_estimate=cost(flops),
+            cost_estimate=cost(TERMS_COST),
             compiler_params=params,
             name="terms",
         )(index, coefficients, intersections, *extra, *blocks)
@@ -444,14 +437,14 @@
     state = amplitudes
     for step in range(ITERS):
         last = step == ITERS - 1
-        partial, places, late = None, [], []
+        places, late = [], []
         if direct:
             mirror = exchange(payload, "pairs", half)
             flips = [0, *range(half - 1, 0, -1)]
             cores = [[o, o + 1] for o in range(0, orb_count, 2)]
             held = lax.all_gather(payload, "orb", axis=0, tiled=False)
             across = pair_count - 1
-            order = [0, across, *flips[1:]]
+            order = [0, half - 1, across, *range(half - 2, 0, -1)]
             sent = select(0, order, held)
             arrived = [sent[0]] + [exchange(part, "pairs", flip) for flip, part in zip(order[1:], sent[1:])]
             mirror = join(mirror, after=sent[:1])
@@ -459,14 +452,14 @@
             held = lax.all_gather(held, "orb", axis=0, axis_index_groups=cores)
             close = [flip for flip in flips if flip + half != across]
             sent = select(capacity, close, held)
-            partial = terms(None, None, [*order, half], arrived + [sent[0]], EARLY)
+            partial = terms(None, [*order, half], arrived + [sent[0]])
             places = [half + flip for flip in close[1:]]
             late = [exchange(part, "pairs", flip) for flip, part in zip(close[1:], sent[1:])]
         else:
             gathered = lax.all_gather(payload, "orb", axis=0, tiled=False)
             outgoing = select_all(gathered)
             every = lax.all_to_all(outgoing, "pairs", split_axis=0, concat_axis=0, tiled=True)
-            partial = terms(None, every, [], [], CLOSE)
+            partial = terms(every, [], [])
         second = jax.ShapeDtypeStruct(amplitudes.shape, F32) if last else payload_shape
         state, payload = pl.pallas_call(
             functools.partial(update_kernel, last, capacity, orbitals, places),

time: 55.5 us -> 55.1 us (level)
  waiting for transfers between devices: 5.35 us -> 4.07 us
  starting transfers between devices: 22.8 us -> 23.6 us
    ppermute x16, waiting for transfers between devices: 5.35 us -> 4.07 us  [exchange(): lax.ppermute(block, axis, [(p, p ^ flip) for p in range(lax.axis_size(axi...]
    ppermute x16, starting transfers between devices: 22.8 us -> 23.6 us  [exchange(): lax.ppermute(block, axis, [(p, p ^ flip) for p in range(lax.axis_size(axi...]
  transfers between devices with their start and end apart: 16 -> 16, of which waited for: 8 -> 7; matrix products, arithmetic and copies ran while one was open for 0% -> 0% of each run, Pallas kernels for 7% -> 7%
where the time goes in v7:
time: 55.1 us; the launch traced here: 54.9 us
  starting transfers between devices  23.6 us (43%)
  blocking collectives  18.6 us (34%)
  Pallas kernels  7.75 us (14%)
  waiting for transfers between devices  4.07 us (7%)
  between operations  0.81 us (1%)
    ppermute x16, starting transfers between devices, exchange(): lax.ppermute(block, axis, [(p, p ^ flip) for p in range(lax.axis_size(axi...  23.6 us
    all_gather x2, blocking collectives, body(): held = lax.all_gather(payload, 'orb', axis=0, tiled=False)  14.2 us
    all_gather x2, blocking collectives, body(): held = lax.all_gather(held, 'orb', axis=0, axis_index_groups=cores)  4.39 us
    ppermute x16, waiting for transfers between devices, exchange(): lax.ppermute(block, axis, [(p, p ^ flip) for p in range(lax.axis_size(axi...  4.07 us
    pallas_call x2, Pallas kernels, terms(): pl.pallas_call(functools.partial(terms_kernel, capacity, orbitals, every...  3.18 us
    pallas_call x2, Pallas kernels, body(): pl.pallas_call(functools.partial(update_kernel, last, capacity, orbitals,...  2.27 us
    pallas_call x1, Pallas kernels, body(): pl.pallas_call(functools.partial(setup_kernel, capacity, orbitals, near,...  1.57 us
  transfers between devices with their start and end apart: 16, of which 7 were waited for; matrix products, arithmetic and copies ran while one was open for 0% of the time, Pallas kernels for 7%

profile of v7, /device:TPU:0, one launch (start us, length us, event | category | flops | bytes accessed | tf_op | source)
XLA Modules:
  0.0 54.9 jit_solution(1769333720958269027)
XLA Ops:
  0.6 1.6 %setup.1 = (bf16[528,128]{1,0:T(8,128)(2,1)S(1)}, s32[8,128]{1,0:T(8,128)S(1)}, s32[4,128]{1,0:T(4,128)S(1)}, f32[4,128]{1,0:T(4,128)S(1)}) custom-call(s32[2,4]{1,0:T(2,128)} %bitcast.11, f32[4,128,128]{2,1,0:T(8,128)} %refs_2_.1, f32[4,128]{1,0:T(4,128)} %refs_5_.3, s32[16,128]{1,0:T(8,128)} %bitcast.14, s32[1,128]{1,0:T(1,128)} %bitcast.15, ...), custom_call_target="tpu_custom_call" | custom-call | tf_op jit(solution)/shard_map/setup/pallas_call | solution.py:337
  2.2 4.1 %collective-permute-start.4 = (bf16[528,128]{1,0:T(8,128)(2,1)S(1)}, bf16[528,128]{1,0:T(8,128)(2,1)S(1)}, u32[]{:S(2)}, u32[]{:S(2)}) collective-permute-start(bf16[528,128]{1,0:T(8,128)(2,1)S(1)} %get-tuple-element.27), channel_id=1, source_target_pairs={{0,16},{4,20},{8,24},{12,28},{16,0},{20,4},{24,8},{28,12},{1,17},{... | collective-permute-start | bytes 405512 | tf_op jit(solution)/shard_map/ppermute | solution.py:423
  6.3 7.2 %all-gather = bf16[2112,128]{1,0:T(8,128)(2,1)S(1)} all-gather(bf16[528,128]{1,0:T(8,128)(2,1)S(1)} %get-tuple-element.27), channel_id=2, replica_groups=mesh['pairs'=8,'orb'=4] {'orb'}, dimensions={0}, use_global_device_ids=true | all-gather | bytes 675840 | tf_op jit(solution)/shard_map/all_gather | solution.py:445
  13.8 0.9 %collective-permute-start.5 = (bf16[528,128]{1,0:T(8,128)(2,1)S(1)}, bf16[528,128]{1,0:T(8,128)(2,1)S(1)}, u32[]{:S(2)}, u32[]{:S(2)}) collective-permute-start(bf16[528,128]{1,0:T(8,128)(2,1)S(1)} %join.4.refs_0_), channel_id=1, source_target_pairs={{0,2},{1,3},{2,0},{3,1},{4,6},{5,7},{6,4},{7,5},{8,10},{9,11},{10,... | collective-permute-start | bytes 405512 | tf_op jit(solution)/shard_map/ppermute | solution.py:423
  14.7 2.5 %collective-permute-start = (bf16[400,128]{1,0:T(8,128)(2,1)S(1)}, bf16[400,128]{1,0:T(8,128)(2,1)S(1)}, u32[]{:S(2)}, u32[]{:S(2)}) collective-permute-start(bf16[400,128]{1,0:T(8,128)(2,1)S(1)} %get-tuple-element.29), channel_id=1, source_target_pairs={{0,12},{4,8},{8,4},{12,0},{16,28},{20,24},{24,20},{28,16},{1,13},{... | collective-permute-start | bytes 307208 | tf_op jit(solution)/shard_map/ppermute | solution.py:423
  17.2 1.7 %collective-permute-start.1 = (bf16[400,128]{1,0:T(8,128)(2,1)S(1)}, bf16[400,128]{1,0:T(8,128)(2,1)S(1)}, u32[]{:S(2)}, u32[]{:S(2)}) collective-permute-start(bf16[400,128]{1,0:T(8,128)(2,1)S(1)} %get-tuple-element.30), channel_id=1, source_target_pairs={{0,28},{4,24},{8,20},{12,16},{16,12},{20,8},{24,4},{28,0},{1,29},{... | collective-permute-start | bytes 307208 | tf_op jit(solution)/shard_map/ppermute | solution.py:423
  18.9 1.1 %collective-permute-start.2 = (bf16[400,128]{1,0:T(8,128)(2,1)S(1)}, bf16[400,128]{1,0:T(8,128)(2,1)S(1)}, u32[]{:S(2)}, u32[]{:S(2)}) collective-permute-start(bf16[400,128]{1,0:T(8,128)(2,1)S(1)} %get-tuple-element.31), channel_id=1, source_target_pairs={{0,8},{4,12},{8,0},{12,4},{16,24},{20,28},{24,16},{28,20},{1,9},{5... | collective-permute-start | bytes 307208 | tf_op jit(solution)/shard_map/ppermute | solution.py:423
  19.9 1.5 %collective-permute-start.3 = (bf16[400,128]{1,0:T(8,128)(2,1)S(1)}, bf16[400,128]{1,0:T(8,128)(2,1)S(1)}, u32[]{:S(2)}, u32[]{:S(2)}) collective-permute-start(bf16[400,128]{1,0:T(8,128)(2,1)S(1)} %get-tuple-element.32), channel_id=1, source_target_pairs={{0,4},{4,0},{8,12},{12,8},{16,20},{20,16},{24,28},{28,24},{1,5},{5... | collective-permute-start | bytes 307208 | tf_op jit(solution)/shard_map/ppermute | solution.py:423
  21.5 2.2 %all-gather.1 = bf16[4,528,128]{2,1,0:T(8,128)(2,1)S(1)} all-gather(bf16[2,528,128]{2,1,0:T(8,128)(2,1)S(1)} %join.5), channel_id=3, replica_groups={{0,1},{2,3},{4,5},{6,7},{8,9},{10,11},{12,13},{14,15},{16,17},{18,19},{..., dimensions={0}, use_global_device_ids=true | all-gather | bytes 811008 | tf_op jit(solution)/shard_map/all_gather | solution.py:452
  23.9 1.4 %collective-permute-start.7 = (bf16[400,128]{1,0:T(8,128)(2,1)S(1)}, bf16[400,128]{1,0:T(8,128)(2,1)S(1)}, u32[]{:S(2)}, u32[]{:S(2)}) collective-permute-start(bf16[400,128]{1,0:T(8,128)(2,1)S(1)} %get-tuple-element.35), channel_id=1, source_target_pairs={{0,4},{4,0},{8,12},{12,8},{16,20},{20,16},{24,28},{28,24},{1,5},{5... | collective-permute-start | bytes 307208 | tf_op jit(solution)/shard_map/ppermute | solution.py:423
  25.9 1.6 %terms.2.before = f32[520,128]{1,0:T(8,128)S(1)} custom-call(s32[4,128]{1,0:T(4,128)S(1)} %get-tuple-element.24.index, f32[4,128]{1,0:T(4,128)S(1)} %get-tuple-element.25.coefficients, bf16[4,16,128,128]{3,2,1,0:T(8,128)(2,1)S(1)} %copy-done, bf16[400,128]{1,0:T(8,128)(2,1)S(1)} %get-tuple-element.28.refs_1_.refs_2_.refs_0_, ...), custom_call_target="tpu_custom_call" | custom-call | flops 20000000000 | tf_op jit(solution)/shard_map/terms/pallas_call | solution.py:427
  27.5 1.4 %collective-permute-done.6.refs_0_ = bf16[400,128]{1,0:T(8,128)(2,1)S(1)} collective-permute-done((bf16[400,128]{1,0:T(8,128)(2,1)S(1)}, bf16[400,128]{1,0:T(8,128)(2,1)S(1)}, u32[]{:S(2)}, u32[]{:S(2)}) %collective-permute-start.6) | collective-permute-done | bytes 102432 | tf_op jit(solution)/shard_map/ppermute | solution.py:423
  28.9 0.8 %update.2 = (f32[4,128,128]{2,1,0:T(8,128)S(1)}, bf16[528,128]{1,0:T(8,128)(2,1)S(1)}) custom-call(s32[4,128]{1,0:T(4,128)S(1)} %get-tuple-element.24.index, f32[4,128]{1,0:T(4,128)S(1)} %get-tuple-element.25.coefficients, s32[2,4]{1,0:T(2,128)S(1)} %bitcast.12, bf16[4,16,128,128]{3,2,1,0:T(8,128)(2,1)S(1)} %copy-done, f32[520,128]{1,0:T(8,128)S(1)} %terms.2.before, ...), custom_call_target="tpu_custom_call" | custom-call | tf_op jit(solution)/shard_map/update/pallas_call | solution.py:464
  29.8 1.7 %collective-permute-start.12 = (bf16[528,128]{1,0:T(8,128)(2,1)S(1)}, bf16[528,128]{1,0:T(8,128)(2,1)S(1)}, u32[]{:S(2)}, u32[]{:S(2)}) collective-permute-start(bf16[528,128]{1,0:T(8,128)(2,1)S(1)} %get-tuple-element.36), channel_id=1, source_target_pairs={{0,16},{4,20},{8,24},{12,28},{16,0},{20,4},{24,8},{28,12},{1,17},{... | collective-permute-start | bytes 405512 | tf_op jit(solution)/shard_map/ppermute | solution.py:423
  31.4 7.0 %all-gather.2 = bf16[2112,128]{1,0:T(8,128)(2,1)S(1)} all-gather(bf16[528,128]{1,0:T(8,128)(2,1)S(1)} %get-tuple-element.36), channel_id=4, replica_groups=mesh['pairs'=8,'orb'=4] {'orb'}, dimensions={0}, use_global_device_ids=true | all-gather | bytes 675840 | tf_op jit(solution)/shard_map/all_gather | solution.py:445
  38.6 0.9 %collective-permute-start.13 = (bf16[528,128]{1,0:T(8,128)(2,1)S(1)}, bf16[528,128]{1,0:T(8,128)(2,1)S(1)}, u32[]{:S(2)}, u32[]{:S(2)}) collective-permute-start(bf16[528,128]{1,0:T(8,128)(2,1)S(1)} %join.6.refs_0_), channel_id=1, source_target_pairs={{0,2},{1,3},{2,0},{3,1},{4,6},{5,7},{6,4},{7,5},{8,10},{9,11},{10,... | collective-permute-start | bytes 405512 | tf_op jit(solution)/shard_map/ppermute | solution.py:423
  39.5 1.6 %collective-permute-start.8 = (bf16[400,128]{1,0:T(8,128)(2,1)S(1)}, bf16[400,128]{1,0:T(8,128)(2,1)S(1)}, u32[]{:S(2)}, u32[]{:S(2)}) collective-permute-start(bf16[400,128]{1,0:T(8,128)(2,1)S(1)} %get-tuple-element.38), channel_id=1, source_target_pairs={{0,12},{4,8},{8,4},{12,0},{16,28},{20,24},{24,20},{28,16},{1,13},{... | collective-permute-start | bytes 307208 | tf_op jit(solution)/shard_map/ppermute | solution.py:423
  41.1 2.1 %collective-permute-start.9 = (bf16[400,128]{1,0:T(8,128)(2,1)S(1)}, bf16[400,128]{1,0:T(8,128)(2,1)S(1)}, u32[]{:S(2)}, u32[]{:S(2)}) collective-permute-start(bf16[400,128]{1,0:T(8,128)(2,1)S(1)} %get-tuple-element.39), channel_id=1, source_target_pairs={{0,28},{4,24},{8,20},{12,16},{16,12},{20,8},{24,4},{28,0},{1,29},{... | collective-permute-start | bytes 307208 | tf_op jit(solution)/shard_map/ppermute | solution.py:423
  44.7 2.2 %all-gather.3 = bf16[4,528,128]{2,1,0:T(8,128)(2,1)S(1)} all-gather(bf16[2,528,128]{2,1,0:T(8,128)(2,1)S(1)} %join.7), channel_id=5, replica_groups={{0,1},{2,3},{4,5},{6,7},{8,9},{10,11},{12,13},{14,15},{16,17},{18,19},{..., dimensions={0}, use_global_device_ids=true | all-gather | bytes 811008 | tf_op jit(solution)/shard_map/all_gather | solution.py:452
  47.0 1.7 %collective-permute-start.14 = (bf16[400,128]{1,0:T(8,128)(2,1)S(1)}, bf16[400,128]{1,0:T(8,128)(2,1)S(1)}, u32[]{:S(2)}, u32[]{:S(2)}) collective-permute-start(bf16[400,128]{1,0:T(8,128)(2,1)S(1)} %get-tuple-element.43), channel_id=1, source_target_pairs={{0,8},{4,12},{8,0},{12,4},{16,24},{20,28},{24,16},{28,20},{1,9},{5... | collective-permute-start | bytes 307208 | tf_op jit(solution)/shard_map/ppermute | solution.py:423
  48.8 0.9 %collective-permute-start.15 = (bf16[400,128]{1,0:T(8,128)(2,1)S(1)}, bf16[400,128]{1,0:T(8,128)(2,1)S(1)}, u32[]{:S(2)}, u32[]{:S(2)}) collective-permute-start(bf16[400,128]{1,0:T(8,128)(2,1)S(1)} %get-tuple-element.44), channel_id=1, source_target_pairs={{0,4},{4,0},{8,12},{12,8},{16,20},{20,16},{24,28},{28,24},{1,5},{5... | collective-permute-start | bytes 307208 | tf_op jit(solution)/shard_map/ppermute | solution.py:423
  50.2 1.6 %terms.3.before = f32[520,128]{1,0:T(8,128)S(1)} custom-call(s32[4,128]{1,0:T(4,128)S(1)} %get-tuple-element.24.index, f32[4,128]{1,0:T(4,128)S(1)} %get-tuple-element.25.coefficients, bf16[4,16,128,128]{3,2,1,0:T(8,128)(2,1)S(1)} %copy-done, bf16[400,128]{1,0:T(8,128)(2,1)S(1)} %get-tuple-element.37.refs_1_.refs_2_.refs_0_, ...), custom_call_target="tpu_custom_call" | custom-call | flops 20000000000 | tf_op jit(solution)/shard_map/terms/pallas_call | solution.py:427
  52.0 1.4 %collective-permute-done.15.refs_1_ = bf16[400,128]{1,0:T(8,128)(2,1)S(1)} collective-permute-done((bf16[400,128]{1,0:T(8,128)(2,1)S(1)}, bf16[400,128]{1,0:T(8,128)(2,1)S(1)}, u32[]{:S(2)}, u32[]{:S(2)}) %collective-permute-start.15) | collective-permute-done | bytes 102432 | tf_op jit(solution)/shard_map/ppermute | solution.py:423
  53.4 1.4 %update.3 = (f32[4,128,128]{2,1,0:T(8,128)}, f32[4,128,128]{2,1,0:T(8,128)}) custom-call(s32[4,128]{1,0:T(4,128)S(1)} %get-tuple-element.24.index, f32[4,128]{1,0:T(4,128)S(1)} %get-tuple-element.25.coefficients, s32[2,4]{1,0:T(2,128)S(1)} %bitcast.13, bf16[4,16,128,128]{3,2,1,0:T(8,128)(2,1)S(1)} %copy-done, f32[520,128]{1,0:T(8,128)S(1)} %terms.3.before, ...), custom_call_target="tpu_custom_call" | custom-call | tf_op jit(solution)/shard_map/update/pallas_call | solution.py:464
  (37 shorter events, 3.6 us)
Async XLA Ops:
  0.6 25.2 %copy-start = (bf16[4,16,128,128]{3,2,1,0:T(8,128)(2,1)S(1)}, bf16[4,16,128,128]{3,2,1,0:T(8,128)(2,1)}, u32[]{:S(2)}) copy-start(bf16[4,16,128,128]{3,2,1,0:T(8,128)(2,1)} %intersections.7) | copy-start | bytes 6291460
  2.2 11.5 %collective-permute-start.4 = (bf16[528,128]{1,0:T(8,128)(2,1)S(1)}, bf16[528,128]{1,0:T(8,128)(2,1)S(1)}, u32[]{:S(2)}, u32[]{:S(2)}) collective-permute-start(bf16[528,128]{1,0:T(8,128)(2,1)S(1)} %get-tuple-element.27), channel_id=1, source_target_pairs={{0,16},{4,20},{8,24},{12,28},{16,0},{20,4},{24,8},{28,12},{1,17},{... | collective-permute-start | bytes 405512 | tf_op jit(solution)/shard_map/ppermute | solution.py:423
  13.8 7.7 %collective-permute-start.5 = (bf16[528,128]{1,0:T(8,128)(2,1)S(1)}, bf16[528,128]{1,0:T(8,128)(2,1)S(1)}, u32[]{:S(2)}, u32[]{:S(2)}) collective-permute-start(bf16[528,128]{1,0:T(8,128)(2,1)S(1)} %join.4.refs_0_), channel_id=1, source_target_pairs={{0,2},{1,3},{2,0},{3,1},{4,6},{5,7},{6,4},{7,5},{8,10},{9,11},{10,... | collective-permute-start | bytes 405512 | tf_op jit(solution)/shard_map/ppermute | solution.py:423
  14.7 9.2 %collective-permute-start = (bf16[400,128]{1,0:T(8,128)(2,1)S(1)}, bf16[400,128]{1,0:T(8,128)(2,1)S(1)}, u32[]{:S(2)}, u32[]{:S(2)}) collective-permute-start(bf16[400,128]{1,0:T(8,128)(2,1)S(1)} %get-tuple-element.29), channel_id=1, source_target_pairs={{0,12},{4,8},{8,4},{12,0},{16,28},{20,24},{24,20},{28,16},{1,13},{... | collective-permute-start | bytes 307208 | tf_op jit(solution)/shard_map/ppermute | solution.py:423
  17.2 8.4 %collective-permute-start.1 = (bf16[400,128]{1,0:T(8,128)(2,1)S(1)}, bf16[400,128]{1,0:T(8,128)(2,1)S(1)}, u32[]{:S(2)}, u32[]{:S(2)}) collective-permute-start(bf16[400,128]{1,0:T(8,128)(2,1)S(1)} %get-tuple-element.30), channel_id=1, source_target_pairs={{0,28},{4,24},{8,20},{12,16},{16,12},{20,8},{24,4},{28,0},{1,29},{... | collective-permute-start | bytes 307208 | tf_op jit(solution)/shard_map/ppermute | solution.py:423
  18.9 6.8 %collective-permute-start.2 = (bf16[400,128]{1,0:T(8,128)(2,1)S(1)}, bf16[400,128]{1,0:T(8,128)(2,1)S(1)}, u32[]{:S(2)}, u32[]{:S(2)}) collective-permute-start(bf16[400,128]{1,0:T(8,128)(2,1)S(1)} %get-tuple-element.31), channel_id=1, source_target_pairs={{0,8},{4,12},{8,0},{12,4},{16,24},{20,28},{24,16},{28,20},{1,9},{5... | collective-permute-start | bytes 307208 | tf_op jit(solution)/shard_map/ppermute | solution.py:423
  19.9 5.9 %collective-permute-start.3 = (bf16[400,128]{1,0:T(8,128)(2,1)S(1)}, bf16[400,128]{1,0:T(8,128)(2,1)S(1)}, u32[]{:S(2)}, u32[]{:S(2)}) collective-permute-start(bf16[400,128]{1,0:T(8,128)(2,1)S(1)} %get-tuple-element.32), channel_id=1, source_target_pairs={{0,4},{4,0},{8,12},{12,8},{16,20},{20,16},{24,28},{28,24},{1,5},{5... | collective-permute-start | bytes 307208 | tf_op jit(solution)/shard_map/ppermute | solution.py:423
  23.8 5.0 %collective-permute-start.6 = (bf16[400,128]{1,0:T(8,128)(2,1)S(1)}, bf16[400,128]{1,0:T(8,128)(2,1)S(1)}, u32[]{:S(2)}, u32[]{:S(2)}) collective-permute-start(bf16[400,128]{1,0:T(8,128)(2,1)S(1)} %get-tuple-element.34), channel_id=1, source_target_pairs={{0,8},{4,12},{8,0},{12,4},{16,24},{20,28},{24,16},{28,20},{1,9},{5... | collective-permute-start | bytes 307208 | tf_op jit(solution)/shard_map/ppermute | solution.py:423
  23.9 5.0 %collective-permute-start.7 = (bf16[400,128]{1,0:T(8,128)(2,1)S(1)}, bf16[400,128]{1,0:T(8,128)(2,1)S(1)}, u32[]{:S(2)}, u32[]{:S(2)}) collective-permute-start(bf16[400,128]{1,0:T(8,128)(2,1)S(1)} %get-tuple-element.35), channel_id=1, source_target_pairs={{0,4},{4,0},{8,12},{12,8},{16,20},{20,16},{24,28},{28,24},{1,5},{5... | collective-permute-start | bytes 307208 | tf_op jit(solution)/shard_map/ppermute | solution.py:423
  25.8 3.1 %copy-start.1 = (f32[4,128,128]{2,1,0:T(8,128)S(1)}, f32[4,128,128]{2,1,0:T(8,128)}, u32[]{:S(2)}) copy-start(f32[4,128,128]{2,1,0:T(8,128)} %refs_2_.1) | copy-start | bytes 786436
  25.8 3.1 %copy-start.2 = (bf16[4,128,128]{2,1,0:T(8,128)(2,1)S(1)}, bf16[4,128,128]{2,1,0:T(8,128)(2,1)}, u32[]{:S(2)}) copy-start(bf16[4,128,128]{2,1,0:T(8,128)(2,1)} %refs_3_.3) | copy-start | bytes 393220
  25.8 3.1 %copy-start.3 = (f32[4,128]{1,0:T(4,128)S(1)}, f32[4,128]{1,0:T(4,128)}, u32[]{:S(2)}) copy-start(f32[4,128]{1,0:T(4,128)} %refs_5_.3) | copy-start | bytes 6148
  25.8 3.1 %copy-start.4 = (s32[4,2]{0,1:T(2,128)S(1)}, s32[4,2]{0,1:T(2,128)}, u32[]{:S(2)}) copy-start(s32[4,2]{0,1:T(2,128)} %param.15) | copy-start | bytes 100
  25.8 3.1 %copy-start.5 = (f32[4,128]{1,0:T(4,128)S(1)}, f32[4,128]{1,0:T(4,128)}, u32[]{:S(2)}) copy-start(f32[4,128]{1,0:T(4,128)} %refs_4_.3) | copy-start | bytes 6148
  29.8 8.8 %collective-permute-start.12 = (bf16[528,128]{1,0:T(8,128)(2,1)S(1)}, bf16[528,128]{1,0:T(8,128)(2,1)S(1)}, u32[]{:S(2)}, u32[]{:S(2)}) collective-permute-start(bf16[528,128]{1,0:T(8,128)(2,1)S(1)} %get-tuple-element.36), channel_id=1, source_target_pairs={{0,16},{4,20},{8,24},{12,28},{16,0},{20,4},{24,8},{28,12},{1,17},{... | collective-permute-start | bytes 405512 | tf_op jit(solution)/shard_map/ppermute | solution.py:423
  38.6 6.0 %collective-permute-start.13 = (bf16[528,128]{1,0:T(8,128)(2,1)S(1)}, bf16[528,128]{1,0:T(8,128)(2,1)S(1)}, u32[]{:S(2)}, u32[]{:S(2)}) collective-permute-start(bf16[528,128]{1,0:T(8,128)(2,1)S(1)} %join.6.refs_0_), channel_id=1, source_target_pairs={{0,2},{1,3},{2,0},{3,1},{4,6},{5,7},{6,4},{7,5},{8,10},{9,11},{10,... | collective-permute-start | bytes 405512 | tf_op jit(solution)/shard_map/ppermute | solution.py:423
  39.5 9.3 %collective-permute-start.8 = (bf16[400,128]{1,0:T(8,128)(2,1)S(1)}, bf16[400,128]{1,0:T(8,128)(2,1)S(1)}, u32[]{:S(2)}, u32[]{:S(2)}) collective-permute-start(bf16[400,128]{1,0:T(8,128)(2,1)S(1)} %get-tuple-element.38), channel_id=1, source_target_pairs={{0,12},{4,8},{8,4},{12,0},{16,28},{20,24},{24,20},{28,16},{1,13},{... | collective-permute-start | bytes 307208 | tf_op jit(solution)/shard_map/ppermute | solution.py:423
  41.1 8.6 %collective-permute-start.9 = (bf16[400,128]{1,0:T(8,128)(2,1)S(1)}, bf16[400,128]{1,0:T(8,128)(2,1)S(1)}, u32[]{:S(2)}, u32[]{:S(2)}) collective-permute-start(bf16[400,128]{1,0:T(8,128)(2,1)S(1)} %get-tuple-element.39), channel_id=1, source_target_pairs={{0,28},{4,24},{8,20},{12,16},{16,12},{20,8},{24,4},{28,0},{1,29},{... | collective-permute-start | bytes 307208 | tf_op jit(solution)/shard_map/ppermute | solution.py:423
  43.2 6.5 %collective-permute-start.10 = (bf16[400,128]{1,0:T(8,128)(2,1)S(1)}, bf16[400,128]{1,0:T(8,128)(2,1)S(1)}, u32[]{:S(2)}, u32[]{:S(2)}) collective-permute-start(bf16[400,128]{1,0:T(8,128)(2,1)S(1)} %get-tuple-element.40), channel_id=1, source_target_pairs={{0,8},{4,12},{8,0},{12,4},{16,24},{20,28},{24,16},{28,20},{1,9},{5... | collective-permute-start | bytes 307208 | tf_op jit(solution)/shard_map/ppermute | solution.py:423
  44.0 6.2 %collective-permute-start.11 = (bf16[400,128]{1,0:T(8,128)(2,1)S(1)}, bf16[400,128]{1,0:T(8,128)(2,1)S(1)}, u32[]{:S(2)}, u32[]{:S(2)}) collective-permute-start(bf16[400,128]{1,0:T(8,128)(2,1)S(1)} %get-tuple-element.41), channel_id=1, source_target_pairs={{0,4},{4,0},{8,12},{12,8},{16,20},{20,16},{24,28},{28,24},{1,5},{5... | collective-permute-start | bytes 307208 | tf_op jit(solution)/shard_map/ppermute | solution.py:423
  47.0 5.0 %collective-permute-start.14 = (bf16[400,128]{1,0:T(8,128)(2,1)S(1)}, bf16[400,128]{1,0:T(8,128)(2,1)S(1)}, u32[]{:S(2)}, u32[]{:S(2)}) collective-permute-start(bf16[400,128]{1,0:T(8,128)(2,1)S(1)} %get-tuple-element.43), channel_id=1, source_target_pairs={{0,8},{4,12},{8,0},{12,4},{16,24},{20,28},{24,16},{28,20},{1,9},{5... | collective-permute-start | bytes 307208 | tf_op jit(solution)/shard_map/ppermute | solution.py:423
  48.8 4.7 %collective-permute-start.15 = (bf16[400,128]{1,0:T(8,128)(2,1)S(1)}, bf16[400,128]{1,0:T(8,128)(2,1)S(1)}, u32[]{:S(2)}, u32[]{:S(2)}) collective-permute-start(bf16[400,128]{1,0:T(8,128)(2,1)S(1)} %get-tuple-element.44), channel_id=1, source_target_pairs={{0,4},{4,0},{8,12},{12,8},{16,20},{20,16},{24,28},{28,24},{1,5},{5... | collective-permute-start | bytes 307208 | tf_op jit(solution)/shard_map/ppermute | solution.py:423

commit v8 on v7

--- a/solution.py
+++ b/solution.py
@@ -244,8 +244,46 @@
     return coupling, singles
 
 
-def terms_kernel(capacity, orbitals, has_every, places, index, coefficients, intersections, *refs):
-    refs, out = list(refs[:-1]), refs[-1]
+def add_ready(capacity, orbitals, wide, rows, blocks, coupling, singles):
+    per_device, width = wide.shape[0], wide.shape[1]
+    slots = [(ref, c * width) for ref in blocks for c in range(capacity)]
+    scaled = [[] for _ in range(per_device)]
+    empty = jnp.zeros((width, width), BF16)
+    for p in range(0, len(slots), 2):
+        near = [ref[pl.ds(row, width), :] for ref, row in slots[p : p + 2]]
+        lanes = pl.ds(p * width, len(near) * width)
+        if len(near) == 2:
+            near = jnp.concatenate(
+                [jnp.concatenate([near[0], empty], axis=1), jnp.concatenate([empty, near[1]], axis=1)], axis=0
+            )
+        else:
+            near = near[0]
+        mixing = jnp.concatenate([wide[s, :, lanes] for s in range(per_device)], axis=0)
+        lifted = jnp.dot(mixing, near, preferred_element_type=F32)
+        for s in range(per_device):
+            block = lifted[s * width : (s + 1) * width]
+            scaled[s].append((rows[pl.ds(s, 1), lanes] * block).astype(BF16))
+    for s in range(per_device):
+        coupling[s] = coupling[s] + lax.dot_general(
+            jnp.concatenate(scaled[s], axis=1), wide[s], (((1,), (1,)), ((), ())), preferred_element_type=F32
+        )
+    for ref in blocks:
+        tail = ref.shape[0] - capacity * width
+        singles = singles + join_parts(ref[pl.ds(capacity * width, tail), :], orbitals)
+    return singles
+
+
+def terms_kernel(capacity, orbitals, has_every, places, later, index, coefficients, intersections, *refs):
+    refs = list(refs)
+    if later:
+        rows, wide = refs.pop(), refs.pop()
+        per_device, width = intersections.shape[0], intersections.shape[2]
+        for j, lane in enumerate([place * capacity + c for place in later for c in range(capacity)]):
+            lanes = pl.ds(j * width, width)
+            for s in range(per_device):
+                wide[s, :, lanes] = intersections[s, index[s, lane]]
+                rows[pl.ds(s, 1), lanes] = jnp.full((1, width), coefficients[s, lane], F32)
+    out = refs.pop()
     every = refs.pop(0) if has_every else None
     coupling, singles = gather_terms(
         capacity, orbitals, index, coefficients, intersections, every, places, refs, None
@@ -257,19 +295,22 @@
 
 
 def update_kernel(
-    last, capacity, orbitals, places,
-    index, coefficients, ends, intersections, before, *refs,
+    last, capacity, orbitals, count,
+    ends, before, *refs,
 ):
-    blocks = refs[: len(places)]
-    state, integrals, energies, projector, out_a, out_b = refs[len(places) : len(places) + 6]
+    if count:
+        wide, rows, refs = refs[0], refs[1], refs[2:]
+    blocks = refs[:count]
+    state, integrals, energies, projector, out_a, out_b = refs[count : count + 6]
     final = out_a, out_b
     if last:
         out_a, out_b, sems = refs[-3:]
     copies = []
     per_device, width = state.shape[0], state.shape[1]
-    coupling, singles = gather_terms(
-        capacity, orbitals, index, coefficients, intersections, None, places, blocks, before
-    )
+    coupling = [before[pl.ds(s * width, width), :] for s in range(per_device)]
+    singles = before[pl.ds(per_device * width, orbitals), :]
+    if count:
+        singles = add_ready(capacity, orbitals, wide, rows, blocks, coupling, singles)
     eye = eye_mask(width)
     total = jnp.zeros((orbitals, width), F32)
     counts_a = end_counts(orbitals, per_device, lambda s: ends[0, s])
@@ -422,13 +463,16 @@
     def exchange(block, axis, flip):
         return lax.ppermute(block, axis, [(p, p ^ flip) for p in range(lax.axis_size(axis))])
 
-    def terms(every, places, blocks):
+    def terms(every, places, blocks, later):
+        span = len(later) * capacity * width
+        ready = [jax.ShapeDtypeStruct((per_device, width, span), BF16), jax.ShapeDtypeStruct((per_device, span), F32)]
+        shapes = [terms_shape, *(ready if later else [])]
         extra = [] if every is None else [every]
         return pl.pallas_call(
-            functools.partial(terms_kernel, capacity, orbitals, every is not None, places),
-            out_shape=terms_shape,
+            functools.partial(terms_kernel, capacity, orbitals, every is not None, places, later),
+            out_shape=shapes,
             in_specs=[tables, tables] + [VMEM] * (1 + len(extra) + len(blocks)),
-            out_specs=VMEM,
+            out_specs=[VMEM] * len(shapes),
             cost_estimate=cost(TERMS_COST),
             compiler_params=params,
             name="terms",
@@ -437,7 +481,7 @@
     state = amplitudes
     for step in range(ITERS):
         last = step == ITERS - 1
-        places, late = [], []
+        late = []
         if direct:
             mirror = exchange(payload, "pairs", half)
             flips = [0, *range(half - 1, 0, -1)]
@@ -452,19 +496,19 @@
             held = lax.all_gather(held, "orb", axis=0, axis_index_groups=cores)
             close = [flip for flip in flips if flip + half != across]
             sent = select(capacity, close, held)
-            partial = terms(None, [*order, half], arrived + [sent[0]])
-            places = [half + flip for flip in close[1:]]
+            later = [half + flip for flip in close[1:]]
+            partial = terms(None, [*order, half], arrived + [sent[0]], later)
             late = [exchange(part, "pairs", flip) for flip, part in zip(close[1:], sent[1:])]
         else:
             gathered = lax.all_gather(payload, "orb", axis=0, tiled=False)
             outgoing = select_all(gathered)
             every = lax.all_to_all(outgoing, "pairs", split_axis=0, concat_axis=0, tiled=True)
-            partial = terms(every, [], [])
+            partial = terms(every, [], [], [])
         second = jax.ShapeDtypeStruct(amplitudes.shape, F32) if last else payload_shape
         state, payload = pl.pallas_call(
-            functools.partial(update_kernel, last, capacity, orbitals, places),
+            functools.partial(update_kernel, last, capacity, orbitals, len(late)),
             out_shape=(jax.ShapeDtypeStruct(amplitudes.shape, F32), second),
-            in_specs=[VMEM] * (9 + len(late)),
+            in_specs=[VMEM] * (5 + len(partial) + len(late)),
             out_specs=(HBM, HBM) if last else (VMEM, VMEM),
             scratch_shapes=[
                 pltpu.VMEM(amplitudes.shape, F32),
@@ -476,7 +520,7 @@
             compiler_params=params,
             name="update",
         )(
-            index, coefficients, ends, intersections, partial, *late, state, integrals, energies, projector,
+            ends, *partial, *late, state, integrals, energies, projector,
         )
     return state, payload
 

time: 55.1 us -> 54.9 us (level)
  transfers between devices with their start and end apart: 16 -> 16, of which waited for: 7 -> 7; matrix products, arithmetic and copies ran while one was open for 0% -> 0% of each run, Pallas kernels for 7% -> 8%
where the time goes in v8:
time: 54.9 us; the launch traced here: 54.8 us
  starting transfers between devices  23.6 us (43%)
  blocking collectives  18.6 us (34%)
  Pallas kernels  7.98 us (15%)
  waiting for transfers between devices  3.72 us (7%)
  between operations  0.81 us (1%)
    ppermute x16, starting transfers between devices, exchange(): lax.ppermute(block, axis, [(p, p ^ flip) for p in range(lax.axis_size(axi...  23.6 us
    all_gather x2, blocking collectives, body(): held = lax.all_gather(payload, 'orb', axis=0, tiled=False)  14.2 us
    all_gather x2, blocking collectives, body(): held = lax.all_gather(held, 'orb', axis=0, axis_index_groups=cores)  4.39 us
    ppermute x16, waiting for transfers between devices, exchange(): lax.ppermute(block, axis, [(p, p ^ flip) for p in range(lax.axis_size(axi...  3.72 us
    pallas_call x2, Pallas kernels, terms(): pl.pallas_call(functools.partial(terms_kernel, capacity, orbitals, every...  3.53 us
    pallas_call x2, Pallas kernels, body(): pl.pallas_call(functools.partial(update_kernel, last, capacity, orbitals,...  2.15 us
    pallas_call x1, Pallas kernels, body(): pl.pallas_call(functools.partial(setup_kernel, capacity, orbitals, near,...  1.57 us
  transfers between devices with their start and end apart: 16, of which 7 were waited for; matrix products, arithmetic and copies ran while one was open for 0% of the time, Pallas kernels for 8%

profile of v8, /device:TPU:0, one launch (start us, length us, event | category | flops | bytes accessed | tf_op | source)
XLA Modules:
  0.0 54.8 jit_solution(14348764718453275191)
XLA Ops:
  0.6 1.6 %setup.1 = (bf16[528,128]{1,0:T(8,128)(2,1)S(1)}, s32[8,128]{1,0:T(8,128)S(1)}, s32[4,128]{1,0:T(4,128)S(1)}, f32[4,128]{1,0:T(4,128)S(1)}) custom-call(s32[2,4]{1,0:T(2,128)} %bitcast.11, f32[4,128,128]{2,1,0:T(8,128)} %refs_4_.1, f32[4,128]{1,0:T(4,128)} %refs_7_.3, s32[16,128]{1,0:T(8,128)} %bitcast.14, s32[1,128]{1,0:T(1,128)} %bitcast.15, ...), custom_call_target="tpu_custom_call" | custom-call | tf_op jit(solution)/shard_map/setup/pallas_call | solution.py:378
  2.2 4.1 %collective-permute-start.4 = (bf16[528,128]{1,0:T(8,128)(2,1)S(1)}, bf16[528,128]{1,0:T(8,128)(2,1)S(1)}, u32[]{:S(2)}, u32[]{:S(2)}) collective-permute-start(bf16[528,128]{1,0:T(8,128)(2,1)S(1)} %get-tuple-element.33), channel_id=1, source_target_pairs={{0,16},{4,20},{8,24},{12,28},{16,0},{20,4},{24,8},{28,12},{1,17},{... | collective-permute-start | bytes 405512 | tf_op jit(solution)/shard_map/ppermute | solution.py:464
  6.3 7.2 %all-gather = bf16[2112,128]{1,0:T(8,128)(2,1)S(1)} all-gather(bf16[528,128]{1,0:T(8,128)(2,1)S(1)} %get-tuple-element.33), channel_id=2, replica_groups=mesh['pairs'=8,'orb'=4] {'orb'}, dimensions={0}, use_global_device_ids=true | all-gather | bytes 675840 | tf_op jit(solution)/shard_map/all_gather | solution.py:489
  13.8 0.9 %collective-permute-start.5 = (bf16[528,128]{1,0:T(8,128)(2,1)S(1)}, bf16[528,128]{1,0:T(8,128)(2,1)S(1)}, u32[]{:S(2)}, u32[]{:S(2)}) collective-permute-start(bf16[528,128]{1,0:T(8,128)(2,1)S(1)} %join.4.refs_0_), channel_id=1, source_target_pairs={{0,2},{1,3},{2,0},{3,1},{4,6},{5,7},{6,4},{7,5},{8,10},{9,11},{10,... | collective-permute-start | bytes 405512 | tf_op jit(solution)/shard_map/ppermute | solution.py:464
  14.7 2.5 %collective-permute-start = (bf16[400,128]{1,0:T(8,128)(2,1)S(1)}, bf16[400,128]{1,0:T(8,128)(2,1)S(1)}, u32[]{:S(2)}, u32[]{:S(2)}) collective-permute-start(bf16[400,128]{1,0:T(8,128)(2,1)S(1)} %get-tuple-element.35), channel_id=1, source_target_pairs={{0,12},{4,8},{8,4},{12,0},{16,28},{20,24},{24,20},{28,16},{1,13},{... | collective-permute-start | bytes 307208 | tf_op jit(solution)/shard_map/ppermute | solution.py:464
  17.2 1.7 %collective-permute-start.1 = (bf16[400,128]{1,0:T(8,128)(2,1)S(1)}, bf16[400,128]{1,0:T(8,128)(2,1)S(1)}, u32[]{:S(2)}, u32[]{:S(2)}) collective-permute-start(bf16[400,128]{1,0:T(8,128)(2,1)S(1)} %get-tuple-element.36), channel_id=1, source_target_pairs={{0,28},{4,24},{8,20},{12,16},{16,12},{20,8},{24,4},{28,0},{1,29},{... | collective-permute-start | bytes 307208 | tf_op jit(solution)/shard_map/ppermute | solution.py:464
  18.9 1.1 %collective-permute-start.2 = (bf16[400,128]{1,0:T(8,128)(2,1)S(1)}, bf16[400,128]{1,0:T(8,128)(2,1)S(1)}, u32[]{:S(2)}, u32[]{:S(2)}) collective-permute-start(bf16[400,128]{1,0:T(8,128)(2,1)S(1)} %get-tuple-element.37), channel_id=1, source_target_pairs={{0,8},{4,12},{8,0},{12,4},{16,24},{20,28},{24,16},{28,20},{1,9},{5... | collective-permute-start | bytes 307208 | tf_op jit(solution)/shard_map/ppermute | solution.py:464
  19.9 1.5 %collective-permute-start.3 = (bf16[400,128]{1,0:T(8,128)(2,1)S(1)}, bf16[400,128]{1,0:T(8,128)(2,1)S(1)}, u32[]{:S(2)}, u32[]{:S(2)}) collective-permute-start(bf16[400,128]{1,0:T(8,128)(2,1)S(1)} %get-tuple-element.38), channel_id=1, source_target_pairs={{0,4},{4,0},{8,12},{12,8},{16,20},{20,16},{24,28},{28,24},{1,5},{5... | collective-permute-start | bytes 307208 | tf_op jit(solution)/shard_map/ppermute | solution.py:464
  21.5 2.2 %all-gather.1 = bf16[4,528,128]{2,1,0:T(8,128)(2,1)S(1)} all-gather(bf16[2,528,128]{2,1,0:T(8,128)(2,1)S(1)} %join.5), channel_id=3, replica_groups={{0,1},{2,3},{4,5},{6,7},{8,9},{10,11},{12,13},{14,15},{16,17},{18,19},{..., dimensions={0}, use_global_device_ids=true | all-gather | bytes 811008 | tf_op jit(solution)/shard_map/all_gather | solution.py:496
  23.9 1.4 %collective-permute-start.7 = (bf16[400,128]{1,0:T(8,128)(2,1)S(1)}, bf16[400,128]{1,0:T(8,128)(2,1)S(1)}, u32[]{:S(2)}, u32[]{:S(2)}) collective-permute-start(bf16[400,128]{1,0:T(8,128)(2,1)S(1)} %get-tuple-element.44), channel_id=1, source_target_pairs={{0,4},{4,0},{8,12},{12,8},{16,20},{20,16},{24,28},{28,24},{1,5},{5... | collective-permute-start | bytes 307208 | tf_op jit(solution)/shard_map/ppermute | solution.py:464
  25.9 1.8 %terms.2 = (f32[520,128]{1,0:T(8,128)S(1)}, bf16[4,128,768]{2,1,0:T(8,128)(2,1)S(1)}, f32[4,768]{1,0:T(4,128)S(1)}) custom-call(s32[4,128]{1,0:T(4,128)S(1)} %get-tuple-element.30.index, f32[4,128]{1,0:T(4,128)S(1)} %get-tuple-element.31.coefficients, bf16[4,16,128,128]{3,2,1,0:T(8,128)(2,1)S(1)} %copy-done.5, ...), custom_call_target="tpu_custom_call" | custom-call | flops 20000000000 | tf_op jit(solution)/shard_map/terms/pallas_call | solution.py:471
  27.6 1.2 %collective-permute-done.6.refs_2_ = bf16[400,128]{1,0:T(8,128)(2,1)S(1)} collective-permute-done((bf16[400,128]{1,0:T(8,128)(2,1)S(1)}, bf16[400,128]{1,0:T(8,128)(2,1)S(1)}, u32[]{:S(2)}, u32[]{:S(2)}) %collective-permute-start.6) | collective-permute-done | bytes 102432 | tf_op jit(solution)/shard_map/ppermute | solution.py:464
  29.7 1.7 %collective-permute-start.12 = (bf16[528,128]{1,0:T(8,128)(2,1)S(1)}, bf16[528,128]{1,0:T(8,128)(2,1)S(1)}, u32[]{:S(2)}, u32[]{:S(2)}) collective-permute-start(bf16[528,128]{1,0:T(8,128)(2,1)S(1)} %get-tuple-element.45), channel_id=1, source_target_pairs={{0,16},{4,20},{8,24},{12,28},{16,0},{20,4},{24,8},{28,12},{1,17},{... | collective-permute-start | bytes 405512 | tf_op jit(solution)/shard_map/ppermute | solution.py:464
  31.4 7.0 %all-gather.2 = bf16[2112,128]{1,0:T(8,128)(2,1)S(1)} all-gather(bf16[528,128]{1,0:T(8,128)(2,1)S(1)} %get-tuple-element.45), channel_id=4, replica_groups=mesh['pairs'=8,'orb'=4] {'orb'}, dimensions={0}, use_global_device_ids=true | all-gather | bytes 675840 | tf_op jit(solution)/shard_map/all_gather | solution.py:489
  38.6 0.9 %collective-permute-start.13 = (bf16[528,128]{1,0:T(8,128)(2,1)S(1)}, bf16[528,128]{1,0:T(8,128)(2,1)S(1)}, u32[]{:S(2)}, u32[]{:S(2)}) collective-permute-start(bf16[528,128]{1,0:T(8,128)(2,1)S(1)} %join.6.refs_0_), channel_id=1, source_target_pairs={{0,2},{1,3},{2,0},{3,1},{4,6},{5,7},{6,4},{7,5},{8,10},{9,11},{10,... | collective-permute-start | bytes 405512 | tf_op jit(solution)/shard_map/ppermute | solution.py:464
  39.5 1.6 %collective-permute-start.8 = (bf16[400,128]{1,0:T(8,128)(2,1)S(1)}, bf16[400,128]{1,0:T(8,128)(2,1)S(1)}, u32[]{:S(2)}, u32[]{:S(2)}) collective-permute-start(bf16[400,128]{1,0:T(8,128)(2,1)S(1)} %get-tuple-element.47), channel_id=1, source_target_pairs={{0,12},{4,8},{8,4},{12,0},{16,28},{20,24},{24,20},{28,16},{1,13},{... | collective-permute-start | bytes 307208 | tf_op jit(solution)/shard_map/ppermute | solution.py:464
  41.1 2.1 %collective-permute-start.9 = (bf16[400,128]{1,0:T(8,128)(2,1)S(1)}, bf16[400,128]{1,0:T(8,128)(2,1)S(1)}, u32[]{:S(2)}, u32[]{:S(2)}) collective-permute-start(bf16[400,128]{1,0:T(8,128)(2,1)S(1)} %get-tuple-element.48), channel_id=1, source_target_pairs={{0,28},{4,24},{8,20},{12,16},{16,12},{20,8},{24,4},{28,0},{1,29},{... | collective-permute-start | bytes 307208 | tf_op jit(solution)/shard_map/ppermute | solution.py:464
  43.1 0.8 %collective-permute-start.10 = (bf16[400,128]{1,0:T(8,128)(2,1)S(1)}, bf16[400,128]{1,0:T(8,128)(2,1)S(1)}, u32[]{:S(2)}, u32[]{:S(2)}) collective-permute-start(bf16[400,128]{1,0:T(8,128)(2,1)S(1)} %get-tuple-element.49), channel_id=1, source_target_pairs={{0,8},{4,12},{8,0},{12,4},{16,24},{20,28},{24,16},{28,20},{1,9},{5... | collective-permute-start | bytes 307208 | tf_op jit(solution)/shard_map/ppermute | solution.py:464
  44.6 2.2 %all-gather.3 = bf16[4,528,128]{2,1,0:T(8,128)(2,1)S(1)} all-gather(bf16[2,528,128]{2,1,0:T(8,128)(2,1)S(1)} %join.7), channel_id=5, replica_groups={{0,1},{2,3},{4,5},{6,7},{8,9},{10,11},{12,13},{14,15},{16,17},{18,19},{..., dimensions={0}, use_global_device_ids=true | all-gather | bytes 811008 | tf_op jit(solution)/shard_map/all_gather | solution.py:496
  47.0 1.7 %collective-permute-start.14 = (bf16[400,128]{1,0:T(8,128)(2,1)S(1)}, bf16[400,128]{1,0:T(8,128)(2,1)S(1)}, u32[]{:S(2)}, u32[]{:S(2)}) collective-permute-start(bf16[400,128]{1,0:T(8,128)(2,1)S(1)} %get-tuple-element.55), channel_id=1, source_target_pairs={{0,8},{4,12},{8,0},{12,4},{16,24},{20,28},{24,16},{28,20},{1,9},{5... | collective-permute-start | bytes 307208 | tf_op jit(solution)/shard_map/ppermute | solution.py:464
  48.7 0.9 %collective-permute-start.15 = (bf16[400,128]{1,0:T(8,128)(2,1)S(1)}, bf16[400,128]{1,0:T(8,128)(2,1)S(1)}, u32[]{:S(2)}, u32[]{:S(2)}) collective-permute-start(bf16[400,128]{1,0:T(8,128)(2,1)S(1)} %get-tuple-element.56), channel_id=1, source_target_pairs={{0,4},{4,0},{8,12},{12,8},{16,20},{20,16},{24,28},{28,24},{1,5},{5... | collective-permute-start | bytes 307208 | tf_op jit(solution)/shard_map/ppermute | solution.py:464
  50.1 1.8 %terms.3 = (f32[520,128]{1,0:T(8,128)S(1)}, bf16[4,128,768]{2,1,0:T(8,128)(2,1)S(1)}, f32[4,768]{1,0:T(4,128)S(1)}) custom-call(s32[4,128]{1,0:T(4,128)S(1)} %get-tuple-element.30.index, f32[4,128]{1,0:T(4,128)S(1)} %get-tuple-element.31.coefficients, bf16[4,16,128,128]{3,2,1,0:T(8,128)(2,1)S(1)} %copy-done.5, ...), custom_call_target="tpu_custom_call" | custom-call | flops 20000000000 | tf_op jit(solution)/shard_map/terms/pallas_call | solution.py:471
  52.0 1.4 %collective-permute-done.15.refs_3_ = bf16[400,128]{1,0:T(8,128)(2,1)S(1)} collective-permute-done((bf16[400,128]{1,0:T(8,128)(2,1)S(1)}, bf16[400,128]{1,0:T(8,128)(2,1)S(1)}, u32[]{:S(2)}, u32[]{:S(2)}) %collective-permute-start.15) | collective-permute-done | bytes 102432 | tf_op jit(solution)/shard_map/ppermute | solution.py:464
  53.4 1.4 %update.3 = (f32[4,128,128]{2,1,0:T(8,128)}, f32[4,128,128]{2,1,0:T(8,128)}) custom-call(s32[2,4]{1,0:T(2,128)S(1)} %bitcast.13, f32[520,128]{1,0:T(8,128)S(1)} %get-tuple-element.52.before, bf16[4,128,768]{2,1,0:T(8,128)(2,1)S(1)} %get-tuple-element.53.refs_0_, f32[4,768]{1,0:T(4,128)S(1)} %get-tuple-element.54.refs_1_, ...), custom_call_target="tpu_custom_call" | custom-call | tf_op jit(solution)/shard_map/update/pallas_call | solution.py:508
  (37 shorter events, 3.4 us)
Async XLA Ops:
  0.6 25.2 %copy-start.5 = (bf16[4,16,128,128]{3,2,1,0:T(8,128)(2,1)S(1)}, bf16[4,16,128,128]{3,2,1,0:T(8,128)(2,1)}, u32[]{:S(2)}) copy-start(bf16[4,16,128,128]{3,2,1,0:T(8,128)(2,1)} %intersections.3) | copy-start | bytes 6291460
  2.2 11.5 %collective-permute-start.4 = (bf16[528,128]{1,0:T(8,128)(2,1)S(1)}, bf16[528,128]{1,0:T(8,128)(2,1)S(1)}, u32[]{:S(2)}, u32[]{:S(2)}) collective-permute-start(bf16[528,128]{1,0:T(8,128)(2,1)S(1)} %get-tuple-element.33), channel_id=1, source_target_pairs={{0,16},{4,20},{8,24},{12,28},{16,0},{20,4},{24,8},{28,12},{1,17},{... | collective-permute-start | bytes 405512 | tf_op jit(solution)/shard_map/ppermute | solution.py:464
  13.8 7.7 %collective-permute-start.5 = (bf16[528,128]{1,0:T(8,128)(2,1)S(1)}, bf16[528,128]{1,0:T(8,128)(2,1)S(1)}, u32[]{:S(2)}, u32[]{:S(2)}) collective-permute-start(bf16[528,128]{1,0:T(8,128)(2,1)S(1)} %join.4.refs_0_), channel_id=1, source_target_pairs={{0,2},{1,3},{2,0},{3,1},{4,6},{5,7},{6,4},{7,5},{8,10},{9,11},{10,... | collective-permute-start | bytes 405512 | tf_op jit(solution)/shard_map/ppermute | solution.py:464
  14.7 9.2 %collective-permute-start = (bf16[400,128]{1,0:T(8,128)(2,1)S(1)}, bf16[400,128]{1,0:T(8,128)(2,1)S(1)}, u32[]{:S(2)}, u32[]{:S(2)}) collective-permute-start(bf16[400,128]{1,0:T(8,128)(2,1)S(1)} %get-tuple-element.35), channel_id=1, source_target_pairs={{0,12},{4,8},{8,4},{12,0},{16,28},{20,24},{24,20},{28,16},{1,13},{... | collective-permute-start | bytes 307208 | tf_op jit(solution)/shard_map/ppermute | solution.py:464
  17.2 8.4 %collective-permute-start.1 = (bf16[400,128]{1,0:T(8,128)(2,1)S(1)}, bf16[400,128]{1,0:T(8,128)(2,1)S(1)}, u32[]{:S(2)}, u32[]{:S(2)}) collective-permute-start(bf16[400,128]{1,0:T(8,128)(2,1)S(1)} %get-tuple-element.36), channel_id=1, source_target_pairs={{0,28},{4,24},{8,20},{12,16},{16,12},{20,8},{24,4},{28,0},{1,29},{... | collective-permute-start | bytes 307208 | tf_op jit(solution)/shard_map/ppermute | solution.py:464
  18.9 6.8 %collective-permute-start.2 = (bf16[400,128]{1,0:T(8,128)(2,1)S(1)}, bf16[400,128]{1,0:T(8,128)(2,1)S(1)}, u32[]{:S(2)}, u32[]{:S(2)}) collective-permute-start(bf16[400,128]{1,0:T(8,128)(2,1)S(1)} %get-tuple-element.37), channel_id=1, source_target_pairs={{0,8},{4,12},{8,0},{12,4},{16,24},{20,28},{24,16},{28,20},{1,9},{5... | collective-permute-start | bytes 307208 | tf_op jit(solution)/shard_map/ppermute | solution.py:464
  19.9 5.9 %collective-permute-start.3 = (bf16[400,128]{1,0:T(8,128)(2,1)S(1)}, bf16[400,128]{1,0:T(8,128)(2,1)S(1)}, u32[]{:S(2)}, u32[]{:S(2)}) collective-permute-start(bf16[400,128]{1,0:T(8,128)(2,1)S(1)} %get-tuple-element.38), channel_id=1, source_target_pairs={{0,4},{4,0},{8,12},{12,8},{16,20},{20,16},{24,28},{28,24},{1,5},{5... | collective-permute-start | bytes 307208 | tf_op jit(solution)/shard_map/ppermute | solution.py:464
  23.8 5.0 %collective-permute-start.6 = (bf16[400,128]{1,0:T(8,128)(2,1)S(1)}, bf16[400,128]{1,0:T(8,128)(2,1)S(1)}, u32[]{:S(2)}, u32[]{:S(2)}) collective-permute-start(bf16[400,128]{1,0:T(8,128)(2,1)S(1)} %get-tuple-element.43), channel_id=1, source_target_pairs={{0,8},{4,12},{8,0},{12,4},{16,24},{20,28},{24,16},{28,20},{1,9},{5... | collective-permute-start | bytes 307208 | tf_op jit(solution)/shard_map/ppermute | solution.py:464
  23.9 5.0 %collective-permute-start.7 = (bf16[400,128]{1,0:T(8,128)(2,1)S(1)}, bf16[400,128]{1,0:T(8,128)(2,1)S(1)}, u32[]{:S(2)}, u32[]{:S(2)}) collective-permute-start(bf16[400,128]{1,0:T(8,128)(2,1)S(1)} %get-tuple-element.44), channel_id=1, source_target_pairs={{0,4},{4,0},{8,12},{12,8},{16,20},{20,16},{24,28},{28,24},{1,5},{5... | collective-permute-start | bytes 307208 | tf_op jit(solution)/shard_map/ppermute | solution.py:464
  25.8 3.1 %copy-start = (f32[4,128,128]{2,1,0:T(8,128)S(1)}, f32[4,128,128]{2,1,0:T(8,128)}, u32[]{:S(2)}) copy-start(f32[4,128,128]{2,1,0:T(8,128)} %refs_4_.1) | copy-start | bytes 786436
  25.8 3.1 %copy-start.1 = (bf16[4,128,128]{2,1,0:T(8,128)(2,1)S(1)}, bf16[4,128,128]{2,1,0:T(8,128)(2,1)}, u32[]{:S(2)}) copy-start(bf16[4,128,128]{2,1,0:T(8,128)(2,1)} %refs_5_.3) | copy-start | bytes 393220
  25.8 3.1 %copy-start.2 = (f32[4,128]{1,0:T(4,128)S(1)}, f32[4,128]{1,0:T(4,128)}, u32[]{:S(2)}) copy-start(f32[4,128]{1,0:T(4,128)} %refs_7_.3) | copy-start | bytes 6148
  25.8 3.1 %copy-start.3 = (s32[4,2]{0,1:T(2,128)S(1)}, s32[4,2]{0,1:T(2,128)}, u32[]{:S(2)}) copy-start(s32[4,2]{0,1:T(2,128)} %param.15) | copy-start | bytes 100
  25.8 3.1 %copy-start.4 = (f32[4,128]{1,0:T(4,128)S(1)}, f32[4,128]{1,0:T(4,128)}, u32[]{:S(2)}) copy-start(f32[4,128]{1,0:T(4,128)} %refs_6_.3) | copy-start | bytes 6148
  29.7 8.8 %collective-permute-start.12 = (bf16[528,128]{1,0:T(8,128)(2,1)S(1)}, bf16[528,128]{1,0:T(8,128)(2,1)S(1)}, u32[]{:S(2)}, u32[]{:S(2)}) collective-permute-start(bf16[528,128]{1,0:T(8,128)(2,1)S(1)} %get-tuple-element.45), channel_id=1, source_target_pairs={{0,16},{4,20},{8,24},{12,28},{16,0},{20,4},{24,8},{28,12},{1,17},{... | collective-permute-start | bytes 405512 | tf_op jit(solution)/shard_map/ppermute | solution.py:464
  38.6 6.0 %collective-permute-start.13 = (bf16[528,128]{1,0:T(8,128)(2,1)S(1)}, bf16[528,128]{1,0:T(8,128)(2,1)S(1)}, u32[]{:S(2)}, u32[]{:S(2)}) collective-permute-start(bf16[528,128]{1,0:T(8,128)(2,1)S(1)} %join.6.refs_0_), channel_id=1, source_target_pairs={{0,2},{1,3},{2,0},{3,1},{4,6},{5,7},{6,4},{7,5},{8,10},{9,11},{10,... | collective-permute-start | bytes 405512 | tf_op jit(solution)/shard_map/ppermute | solution.py:464
  39.5 9.3 %collective-permute-start.8 = (bf16[400,128]{1,0:T(8,128)(2,1)S(1)}, bf16[400,128]{1,0:T(8,128)(2,1)S(1)}, u32[]{:S(2)}, u32[]{:S(2)}) collective-permute-start(bf16[400,128]{1,0:T(8,128)(2,1)S(1)} %get-tuple-element.47), channel_id=1, source_target_pairs={{0,12},{4,8},{8,4},{12,0},{16,28},{20,24},{24,20},{28,16},{1,13},{... | collective-permute-start | bytes 307208 | tf_op jit(solution)/shard_map/ppermute | solution.py:464
  41.1 8.6 %collective-permute-start.9 = (bf16[400,128]{1,0:T(8,128)(2,1)S(1)}, bf16[400,128]{1,0:T(8,128)(2,1)S(1)}, u32[]{:S(2)}, u32[]{:S(2)}) collective-permute-start(bf16[400,128]{1,0:T(8,128)(2,1)S(1)} %get-tuple-element.48), channel_id=1, source_target_pairs={{0,28},{4,24},{8,20},{12,16},{16,12},{20,8},{24,4},{28,0},{1,29},{... | collective-permute-start | bytes 307208 | tf_op jit(solution)/shard_map/ppermute | solution.py:464
  43.1 6.5 %collective-permute-start.10 = (bf16[400,128]{1,0:T(8,128)(2,1)S(1)}, bf16[400,128]{1,0:T(8,128)(2,1)S(1)}, u32[]{:S(2)}, u32[]{:S(2)}) collective-permute-start(bf16[400,128]{1,0:T(8,128)(2,1)S(1)} %get-tuple-element.49), channel_id=1, source_target_pairs={{0,8},{4,12},{8,0},{12,4},{16,24},{20,28},{24,16},{28,20},{1,9},{5... | collective-permute-start | bytes 307208 | tf_op jit(solution)/shard_map/ppermute | solution.py:464
  43.9 6.2 %collective-permute-start.11 = (bf16[400,128]{1,0:T(8,128)(2,1)S(1)}, bf16[400,128]{1,0:T(8,128)(2,1)S(1)}, u32[]{:S(2)}, u32[]{:S(2)}) collective-permute-start(bf16[400,128]{1,0:T(8,128)(2,1)S(1)} %get-tuple-element.50), channel_id=1, source_target_pairs={{0,4},{4,0},{8,12},{12,8},{16,20},{20,16},{24,28},{28,24},{1,5},{5... | collective-permute-start | bytes 307208 | tf_op jit(solution)/shard_map/ppermute | solution.py:464
  47.0 5.0 %collective-permute-start.14 = (bf16[400,128]{1,0:T(8,128)(2,1)S(1)}, bf16[400,128]{1,0:T(8,128)(2,1)S(1)}, u32[]{:S(2)}, u32[]{:S(2)}) collective-permute-start(bf16[400,128]{1,0:T(8,128)(2,1)S(1)} %get-tuple-element.55), channel_id=1, source_target_pairs={{0,8},{4,12},{8,0},{12,4},{16,24},{20,28},{24,16},{28,20},{1,9},{5... | collective-permute-start | bytes 307208 | tf_op jit(solution)/shard_map/ppermute | solution.py:464
  48.7 4.7 %collective-permute-start.15 = (bf16[400,128]{1,0:T(8,128)(2,1)S(1)}, bf16[400,128]{1,0:T(8,128)(2,1)S(1)}, u32[]{:S(2)}, u32[]{:S(2)}) collective-permute-start(bf16[400,128]{1,0:T(8,128)(2,1)S(1)} %get-tuple-element.56), channel_id=1, source_target_pairs={{0,4},{4,0},{8,12},{12,8},{16,20},{20,16},{24,28},{28,24},{1,5},{5... | collective-permute-start | bytes 307208 | tf_op jit(solution)/shard_map/ppermute | solution.py:464

commit v9 on v8

--- a/solution.py
+++ b/solution.py
@@ -488,7 +488,7 @@
             cores = [[o, o + 1] for o in range(0, orb_count, 2)]
             held = lax.all_gather(payload, "orb", axis=0, tiled=False)
             across = pair_count - 1
-            order = [0, half - 1, across, *range(half - 2, 0, -1)]
+            order = [0, half - 1, across, *range(1, half - 1)]
             sent = select(0, order, held)
             arrived = [sent[0]] + [exchange(part, "pairs", flip) for flip, part in zip(order[1:], sent[1:])]
             mirror = join(mirror, after=sent[:1])

time: 54.9 us -> 54.9 us (level)
  transfers between devices with their start and end apart: 16 -> 16, of which waited for: 7 -> 5; matrix products, arithmetic and copies ran while one was open for 0% -> 0% of each run, Pallas kernels for 8% -> 8%
where the time goes in v9:
time: 54.9 us; the launch traced here: 54.8 us
  starting transfers between devices  23.6 us (43%)
  blocking collectives  18.6 us (34%)
  Pallas kernels  7.98 us (15%)
  waiting for transfers between devices  3.7 us (7%)
  between operations  0.83 us (2%)
    ppermute x16, starting transfers between devices, exchange(): lax.ppermute(block, axis, [(p, p ^ flip) for p in range(lax.axis_size(axi...  23.6 us
    all_gather x2, blocking collectives, body(): held = lax.all_gather(payload, 'orb', axis=0, tiled=False)  14.2 us
    all_gather x2, blocking collectives, body(): held = lax.all_gather(held, 'orb', axis=0, axis_index_groups=cores)  4.39 us
    ppermute x16, waiting for transfers between devices, exchange(): lax.ppermute(block, axis, [(p, p ^ flip) for p in range(lax.axis_size(axi...  3.7 us
    pallas_call x2, Pallas kernels, terms(): pl.pallas_call(functools.partial(terms_kernel, capacity, orbitals, every...  3.53 us
    pallas_call x2, Pallas kernels, body(): pl.pallas_call(functools.partial(update_kernel, last, capacity, orbitals,...  2.15 us
    pallas_call x1, Pallas kernels, body(): pl.pallas_call(functools.partial(setup_kernel, capacity, orbitals, near,...  1.57 us
  transfers between devices with their start and end apart: 16, of which 5 were waited for; matrix products, arithmetic and copies ran while one was open for 0% of the time, Pallas kernels for 8%

profile of v9, /device:TPU:0, one launch (start us, length us, event | category | flops | bytes accessed | tf_op | source)
XLA Modules:
  0.0 54.8 jit_solution(12494772145846657708)
XLA Ops:
  0.6 1.6 %setup.1 = (bf16[528,128]{1,0:T(8,128)(2,1)S(1)}, s32[8,128]{1,0:T(8,128)S(1)}, s32[4,128]{1,0:T(4,128)S(1)}, f32[4,128]{1,0:T(4,128)S(1)}) custom-call(s32[2,4]{1,0:T(2,128)} %bitcast.11, f32[4,128,128]{2,1,0:T(8,128)} %refs_4_.1, f32[4,128]{1,0:T(4,128)} %refs_7_.3, s32[16,128]{1,0:T(8,128)} %bitcast.14, s32[1,128]{1,0:T(1,128)} %bitcast.15, ...), custom_call_target="tpu_custom_call" | custom-call | tf_op jit(solution)/shard_map/setup/pallas_call | solution.py:378
  2.2 4.1 %collective-permute-start.4 = (bf16[528,128]{1,0:T(8,128)(2,1)S(1)}, bf16[528,128]{1,0:T(8,128)(2,1)S(1)}, u32[]{:S(2)}, u32[]{:S(2)}) collective-permute-start(bf16[528,128]{1,0:T(8,128)(2,1)S(1)} %get-tuple-element.33), channel_id=1, source_target_pairs={{0,16},{4,20},{8,24},{12,28},{16,0},{20,4},{24,8},{28,12},{1,17},{... | collective-permute-start | bytes 405512 | tf_op jit(solution)/shard_map/ppermute | solution.py:464
  6.3 7.2 %all-gather = bf16[2112,128]{1,0:T(8,128)(2,1)S(1)} all-gather(bf16[528,128]{1,0:T(8,128)(2,1)S(1)} %get-tuple-element.33), channel_id=2, replica_groups=mesh['pairs'=8,'orb'=4] {'orb'}, dimensions={0}, use_global_device_ids=true | all-gather | bytes 675840 | tf_op jit(solution)/shard_map/all_gather | solution.py:489
  13.8 0.9 %collective-permute-start.5 = (bf16[528,128]{1,0:T(8,128)(2,1)S(1)}, bf16[528,128]{1,0:T(8,128)(2,1)S(1)}, u32[]{:S(2)}, u32[]{:S(2)}) collective-permute-start(bf16[528,128]{1,0:T(8,128)(2,1)S(1)} %join.4.refs_0_), channel_id=1, source_target_pairs={{0,2},{1,3},{2,0},{3,1},{4,6},{5,7},{6,4},{7,5},{8,10},{9,11},{10,... | collective-permute-start | bytes 405512 | tf_op jit(solution)/shard_map/ppermute | solution.py:464
  14.7 2.5 %collective-permute-start = (bf16[400,128]{1,0:T(8,128)(2,1)S(1)}, bf16[400,128]{1,0:T(8,128)(2,1)S(1)}, u32[]{:S(2)}, u32[]{:S(2)}) collective-permute-start(bf16[400,128]{1,0:T(8,128)(2,1)S(1)} %get-tuple-element.35), channel_id=1, source_target_pairs={{0,12},{4,8},{8,4},{12,0},{16,28},{20,24},{24,20},{28,16},{1,13},{... | collective-permute-start | bytes 307208 | tf_op jit(solution)/shard_map/ppermute | solution.py:464
  17.2 1.7 %collective-permute-start.1 = (bf16[400,128]{1,0:T(8,128)(2,1)S(1)}, bf16[400,128]{1,0:T(8,128)(2,1)S(1)}, u32[]{:S(2)}, u32[]{:S(2)}) collective-permute-start(bf16[400,128]{1,0:T(8,128)(2,1)S(1)} %get-tuple-element.36), channel_id=1, source_target_pairs={{0,28},{4,24},{8,20},{12,16},{16,12},{20,8},{24,4},{28,0},{1,29},{... | collective-permute-start | bytes 307208 | tf_op jit(solution)/shard_map/ppermute | solution.py:464
  19.4 2.1 %collective-permute-start.3 = (bf16[400,128]{1,0:T(8,128)(2,1)S(1)}, bf16[400,128]{1,0:T(8,128)(2,1)S(1)}, u32[]{:S(2)}, u32[]{:S(2)}) collective-permute-start(bf16[400,128]{1,0:T(8,128)(2,1)S(1)} %get-tuple-element.38), channel_id=1, source_target_pairs={{0,8},{4,12},{8,0},{12,4},{16,24},{20,28},{24,16},{28,20},{1,9},{5... | collective-permute-start | bytes 307208 | tf_op jit(solution)/shard_map/ppermute | solution.py:464
  21.5 2.2 %all-gather.1 = bf16[4,528,128]{2,1,0:T(8,128)(2,1)S(1)} all-gather(bf16[2,528,128]{2,1,0:T(8,128)(2,1)S(1)} %join.5), channel_id=3, replica_groups={{0,1},{2,3},{4,5},{6,7},{8,9},{10,11},{12,13},{14,15},{16,17},{18,19},{..., dimensions={0}, use_global_device_ids=true | all-gather | bytes 811008 | tf_op jit(solution)/shard_map/all_gather | solution.py:496
  23.9 1.4 %collective-permute-start.7 = (bf16[400,128]{1,0:T(8,128)(2,1)S(1)}, bf16[400,128]{1,0:T(8,128)(2,1)S(1)}, u32[]{:S(2)}, u32[]{:S(2)}) collective-permute-start(bf16[400,128]{1,0:T(8,128)(2,1)S(1)} %get-tuple-element.44), channel_id=1, source_target_pairs={{0,4},{4,0},{8,12},{12,8},{16,20},{20,16},{24,28},{28,24},{1,5},{5... | collective-permute-start | bytes 307208 | tf_op jit(solution)/shard_map/ppermute | solution.py:464
  25.7 1.8 %terms.2 = (f32[520,128]{1,0:T(8,128)S(1)}, bf16[4,128,768]{2,1,0:T(8,128)(2,1)S(1)}, f32[4,768]{1,0:T(4,128)S(1)}) custom-call(s32[4,128]{1,0:T(4,128)S(1)} %get-tuple-element.30.index, f32[4,128]{1,0:T(4,128)S(1)} %get-tuple-element.31.coefficients, bf16[4,16,128,128]{3,2,1,0:T(8,128)(2,1)S(1)} %copy-done.5, ...), custom_call_target="tpu_custom_call" | custom-call | flops 20000000000 | tf_op jit(solution)/shard_map/terms/pallas_call | solution.py:471
  27.5 1.3 %collective-permute-done.6.refs_2_ = bf16[400,128]{1,0:T(8,128)(2,1)S(1)} collective-permute-done((bf16[400,128]{1,0:T(8,128)(2,1)S(1)}, bf16[400,128]{1,0:T(8,128)(2,1)S(1)}, u32[]{:S(2)}, u32[]{:S(2)}) %collective-permute-start.6) | collective-permute-done | bytes 102432 | tf_op jit(solution)/shard_map/ppermute | solution.py:464
  28.9 0.8 %update.2 = (f32[4,128,128]{2,1,0:T(8,128)S(1)}, bf16[528,128]{1,0:T(8,128)(2,1)S(1)}) custom-call(s32[2,4]{1,0:T(2,128)S(1)} %bitcast.12, f32[520,128]{1,0:T(8,128)S(1)} %get-tuple-element.40.before, bf16[4,128,768]{2,1,0:T(8,128)(2,1)S(1)} %get-tuple-element.41.refs_0_, f32[4,768]{1,0:T(4,128)S(1)} %get-tuple-element.42.refs_1_, ...), custom_call_target="tpu_custom_call" | custom-call | tf_op jit(solution)/shard_map/update/pallas_call | solution.py:508
  29.7 1.7 %collective-permute-start.12 = (bf16[528,128]{1,0:T(8,128)(2,1)S(1)}, bf16[528,128]{1,0:T(8,128)(2,1)S(1)}, u32[]{:S(2)}, u32[]{:S(2)}) collective-permute-start(bf16[528,128]{1,0:T(8,128)(2,1)S(1)} %get-tuple-element.45), channel_id=1, source_target_pairs={{0,16},{4,20},{8,24},{12,28},{16,0},{20,4},{24,8},{28,12},{1,17},{... | collective-permute-start | bytes 405512 | tf_op jit(solution)/shard_map/ppermute | solution.py:464
  31.4 7.0 %all-gather.2 = bf16[2112,128]{1,0:T(8,128)(2,1)S(1)} all-gather(bf16[528,128]{1,0:T(8,128)(2,1)S(1)} %get-tuple-element.45), channel_id=4, replica_groups=mesh['pairs'=8,'orb'=4] {'orb'}, dimensions={0}, use_global_device_ids=true | all-gather | bytes 675840 | tf_op jit(solution)/shard_map/all_gather | solution.py:489
  38.6 0.9 %collective-permute-start.13 = (bf16[528,128]{1,0:T(8,128)(2,1)S(1)}, bf16[528,128]{1,0:T(8,128)(2,1)S(1)}, u32[]{:S(2)}, u32[]{:S(2)}) collective-permute-start(bf16[528,128]{1,0:T(8,128)(2,1)S(1)} %join.6.refs_0_), channel_id=1, source_target_pairs={{0,2},{1,3},{2,0},{3,1},{4,6},{5,7},{6,4},{7,5},{8,10},{9,11},{10,... | collective-permute-start | bytes 405512 | tf_op jit(solution)/shard_map/ppermute | solution.py:464
  39.5 1.6 %collective-permute-start.8 = (bf16[400,128]{1,0:T(8,128)(2,1)S(1)}, bf16[400,128]{1,0:T(8,128)(2,1)S(1)}, u32[]{:S(2)}, u32[]{:S(2)}) collective-permute-start(bf16[400,128]{1,0:T(8,128)(2,1)S(1)} %get-tuple-element.47), channel_id=1, source_target_pairs={{0,12},{4,8},{8,4},{12,0},{16,28},{20,24},{24,20},{28,16},{1,13},{... | collective-permute-start | bytes 307208 | tf_op jit(solution)/shard_map/ppermute | solution.py:464
  41.1 2.1 %collective-permute-start.9 = (bf16[400,128]{1,0:T(8,128)(2,1)S(1)}, bf16[400,128]{1,0:T(8,128)(2,1)S(1)}, u32[]{:S(2)}, u32[]{:S(2)}) collective-permute-start(bf16[400,128]{1,0:T(8,128)(2,1)S(1)} %get-tuple-element.48), channel_id=1, source_target_pairs={{0,28},{4,24},{8,20},{12,16},{16,12},{20,8},{24,4},{28,0},{1,29},{... | collective-permute-start | bytes 307208 | tf_op jit(solution)/shard_map/ppermute | solution.py:464
  43.1 1.1 %collective-permute-start.10 = (bf16[400,128]{1,0:T(8,128)(2,1)S(1)}, bf16[400,128]{1,0:T(8,128)(2,1)S(1)}, u32[]{:S(2)}, u32[]{:S(2)}) collective-permute-start(bf16[400,128]{1,0:T(8,128)(2,1)S(1)} %get-tuple-element.49), channel_id=1, source_target_pairs={{0,4},{4,0},{8,12},{12,8},{16,20},{20,16},{24,28},{28,24},{1,5},{5... | collective-permute-start | bytes 307208 | tf_op jit(solution)/shard_map/ppermute | solution.py:464
  44.6 2.2 %all-gather.3 = bf16[4,528,128]{2,1,0:T(8,128)(2,1)S(1)} all-gather(bf16[2,528,128]{2,1,0:T(8,128)(2,1)S(1)} %join.7), channel_id=5, replica_groups={{0,1},{2,3},{4,5},{6,7},{8,9},{10,11},{12,13},{14,15},{16,17},{18,19},{..., dimensions={0}, use_global_device_ids=true | all-gather | bytes 811008 | tf_op jit(solution)/shard_map/all_gather | solution.py:496
  47.0 1.7 %collective-permute-start.14 = (bf16[400,128]{1,0:T(8,128)(2,1)S(1)}, bf16[400,128]{1,0:T(8,128)(2,1)S(1)}, u32[]{:S(2)}, u32[]{:S(2)}) collective-permute-start(bf16[400,128]{1,0:T(8,128)(2,1)S(1)} %get-tuple-element.55), channel_id=1, source_target_pairs={{0,8},{4,12},{8,0},{12,4},{16,24},{20,28},{24,16},{28,20},{1,9},{5... | collective-permute-start | bytes 307208 | tf_op jit(solution)/shard_map/ppermute | solution.py:464
  48.7 0.9 %collective-permute-start.15 = (bf16[400,128]{1,0:T(8,128)(2,1)S(1)}, bf16[400,128]{1,0:T(8,128)(2,1)S(1)}, u32[]{:S(2)}, u32[]{:S(2)}) collective-permute-start(bf16[400,128]{1,0:T(8,128)(2,1)S(1)} %get-tuple-element.56), channel_id=1, source_target_pairs={{0,4},{4,0},{8,12},{12,8},{16,20},{20,16},{24,28},{28,24},{1,5},{5... | collective-permute-start | bytes 307208 | tf_op jit(solution)/shard_map/ppermute | solution.py:464
  49.6 1.3 %collective-permute-done.11.refs_4_ = bf16[400,128]{1,0:T(8,128)(2,1)S(1)} collective-permute-done((bf16[400,128]{1,0:T(8,128)(2,1)S(1)}, bf16[400,128]{1,0:T(8,128)(2,1)S(1)}, u32[]{:S(2)}, u32[]{:S(2)}) %collective-permute-start.11) | collective-permute-done | bytes 102432 | tf_op jit(solution)/shard_map/ppermute | solution.py:464
  51.0 1.8 %terms.3 = (f32[520,128]{1,0:T(8,128)S(1)}, bf16[4,128,768]{2,1,0:T(8,128)(2,1)S(1)}, f32[4,768]{1,0:T(4,128)S(1)}) custom-call(s32[4,128]{1,0:T(4,128)S(1)} %get-tuple-element.30.index, f32[4,128]{1,0:T(4,128)S(1)} %get-tuple-element.31.coefficients, bf16[4,16,128,128]{3,2,1,0:T(8,128)(2,1)S(1)} %copy-done.5, ...), custom_call_target="tpu_custom_call" | custom-call | flops 20000000000 | tf_op jit(solution)/shard_map/terms/pallas_call | solution.py:471
  53.4 1.4 %update.3 = (f32[4,128,128]{2,1,0:T(8,128)}, f32[4,128,128]{2,1,0:T(8,128)}) custom-call(s32[2,4]{1,0:T(2,128)S(1)} %bitcast.13, f32[520,128]{1,0:T(8,128)S(1)} %get-tuple-element.52.before, bf16[4,128,768]{2,1,0:T(8,128)(2,1)S(1)} %get-tuple-element.53.refs_0_, f32[4,768]{1,0:T(4,128)S(1)} %get-tuple-element.54.refs_1_, ...), custom_call_target="tpu_custom_call" | custom-call | tf_op jit(solution)/shard_map/update/pallas_call | solution.py:508
  (37 shorter events, 2.8 us)
Async XLA Ops:
  0.6 25.1 %copy-start.5 = (bf16[4,16,128,128]{3,2,1,0:T(8,128)(2,1)S(1)}, bf16[4,16,128,128]{3,2,1,0:T(8,128)(2,1)}, u32[]{:S(2)}) copy-start(bf16[4,16,128,128]{3,2,1,0:T(8,128)(2,1)} %intersections.3) | copy-start | bytes 6291460
  2.2 11.5 %collective-permute-start.4 = (bf16[528,128]{1,0:T(8,128)(2,1)S(1)}, bf16[528,128]{1,0:T(8,128)(2,1)S(1)}, u32[]{:S(2)}, u32[]{:S(2)}) collective-permute-start(bf16[528,128]{1,0:T(8,128)(2,1)S(1)} %get-tuple-element.33), channel_id=1, source_target_pairs={{0,16},{4,20},{8,24},{12,28},{16,0},{20,4},{24,8},{28,12},{1,17},{... | collective-permute-start | bytes 405512 | tf_op jit(solution)/shard_map/ppermute | solution.py:464
  13.8 7.7 %collective-permute-start.5 = (bf16[528,128]{1,0:T(8,128)(2,1)S(1)}, bf16[528,128]{1,0:T(8,128)(2,1)S(1)}, u32[]{:S(2)}, u32[]{:S(2)}) collective-permute-start(bf16[528,128]{1,0:T(8,128)(2,1)S(1)} %join.4.refs_0_), channel_id=1, source_target_pairs={{0,2},{1,3},{2,0},{3,1},{4,6},{5,7},{6,4},{7,5},{8,10},{9,11},{10,... | collective-permute-start | bytes 405512 | tf_op jit(solution)/shard_map/ppermute | solution.py:464
  14.7 9.2 %collective-permute-start = (bf16[400,128]{1,0:T(8,128)(2,1)S(1)}, bf16[400,128]{1,0:T(8,128)(2,1)S(1)}, u32[]{:S(2)}, u32[]{:S(2)}) collective-permute-start(bf16[400,128]{1,0:T(8,128)(2,1)S(1)} %get-tuple-element.35), channel_id=1, source_target_pairs={{0,12},{4,8},{8,4},{12,0},{16,28},{20,24},{24,20},{28,16},{1,13},{... | collective-permute-start | bytes 307208 | tf_op jit(solution)/shard_map/ppermute | solution.py:464
  17.2 8.4 %collective-permute-start.1 = (bf16[400,128]{1,0:T(8,128)(2,1)S(1)}, bf16[400,128]{1,0:T(8,128)(2,1)S(1)}, u32[]{:S(2)}, u32[]{:S(2)}) collective-permute-start(bf16[400,128]{1,0:T(8,128)(2,1)S(1)} %get-tuple-element.36), channel_id=1, source_target_pairs={{0,28},{4,24},{8,20},{12,16},{16,12},{20,8},{24,4},{28,0},{1,29},{... | collective-permute-start | bytes 307208 | tf_op jit(solution)/shard_map/ppermute | solution.py:464
  18.9 6.8 %collective-permute-start.2 = (bf16[400,128]{1,0:T(8,128)(2,1)S(1)}, bf16[400,128]{1,0:T(8,128)(2,1)S(1)}, u32[]{:S(2)}, u32[]{:S(2)}) collective-permute-start(bf16[400,128]{1,0:T(8,128)(2,1)S(1)} %get-tuple-element.37), channel_id=1, source_target_pairs={{0,4},{4,0},{8,12},{12,8},{16,20},{20,16},{24,28},{28,24},{1,5},{5... | collective-permute-start | bytes 307208 | tf_op jit(solution)/shard_map/ppermute | solution.py:464
  19.4 6.3 %collective-permute-start.3 = (bf16[400,128]{1,0:T(8,128)(2,1)S(1)}, bf16[400,128]{1,0:T(8,128)(2,1)S(1)}, u32[]{:S(2)}, u32[]{:S(2)}) collective-permute-start(bf16[400,128]{1,0:T(8,128)(2,1)S(1)} %get-tuple-element.38), channel_id=1, source_target_pairs={{0,8},{4,12},{8,0},{12,4},{16,24},{20,28},{24,16},{28,20},{1,9},{5... | collective-permute-start | bytes 307208 | tf_op jit(solution)/shard_map/ppermute | solution.py:464
  23.8 5.0 %collective-permute-start.6 = (bf16[400,128]{1,0:T(8,128)(2,1)S(1)}, bf16[400,128]{1,0:T(8,128)(2,1)S(1)}, u32[]{:S(2)}, u32[]{:S(2)}) collective-permute-start(bf16[400,128]{1,0:T(8,128)(2,1)S(1)} %get-tuple-element.43), channel_id=1, source_target_pairs={{0,8},{4,12},{8,0},{12,4},{16,24},{20,28},{24,16},{28,20},{1,9},{5... | collective-permute-start | bytes 307208 | tf_op jit(solution)/shard_map/ppermute | solution.py:464
  23.9 5.0 %collective-permute-start.7 = (bf16[400,128]{1,0:T(8,128)(2,1)S(1)}, bf16[400,128]{1,0:T(8,128)(2,1)S(1)}, u32[]{:S(2)}, u32[]{:S(2)}) collective-permute-start(bf16[400,128]{1,0:T(8,128)(2,1)S(1)} %get-tuple-element.44), channel_id=1, source_target_pairs={{0,4},{4,0},{8,12},{12,8},{16,20},{20,16},{24,28},{28,24},{1,5},{5... | collective-permute-start | bytes 307208 | tf_op jit(solution)/shard_map/ppermute | solution.py:464
  25.7 3.2 %copy-start = (f32[4,128,128]{2,1,0:T(8,128)S(1)}, f32[4,128,128]{2,1,0:T(8,128)}, u32[]{:S(2)}) copy-start(f32[4,128,128]{2,1,0:T(8,128)} %refs_4_.1) | copy-start | bytes 786436
  25.7 3.2 %copy-start.1 = (bf16[4,128,128]{2,1,0:T(8,128)(2,1)S(1)}, bf16[4,128,128]{2,1,0:T(8,128)(2,1)}, u32[]{:S(2)}) copy-start(bf16[4,128,128]{2,1,0:T(8,128)(2,1)} %refs_5_.3) | copy-start | bytes 393220
  25.7 3.2 %copy-start.2 = (f32[4,128]{1,0:T(4,128)S(1)}, f32[4,128]{1,0:T(4,128)}, u32[]{:S(2)}) copy-start(f32[4,128]{1,0:T(4,128)} %refs_7_.3) | copy-start | bytes 6148
  25.7 3.2 %copy-start.3 = (s32[4,2]{0,1:T(2,128)S(1)}, s32[4,2]{0,1:T(2,128)}, u32[]{:S(2)}) copy-start(s32[4,2]{0,1:T(2,128)} %param.15) | copy-start | bytes 100
  25.7 3.2 %copy-start.4 = (f32[4,128]{1,0:T(4,128)S(1)}, f32[4,128]{1,0:T(4,128)}, u32[]{:S(2)}) copy-start(f32[4,128]{1,0:T(4,128)} %refs_6_.3) | copy-start | bytes 6148
  29.7 8.8 %collective-permute-start.12 = (bf16[528,128]{1,0:T(8,128)(2,1)S(1)}, bf16[528,128]{1,0:T(8,128)(2,1)S(1)}, u32[]{:S(2)}, u32[]{:S(2)}) collective-permute-start(bf16[528,128]{1,0:T(8,128)(2,1)S(1)} %get-tuple-element.45), channel_id=1, source_target_pairs={{0,16},{4,20},{8,24},{12,28},{16,0},{20,4},{24,8},{28,12},{1,17},{... | collective-permute-start | bytes 405512 | tf_op jit(solution)/shard_map/ppermute | solution.py:464
  38.6 6.0 %collective-permute-start.13 = (bf16[528,128]{1,0:T(8,128)(2,1)S(1)}, bf16[528,128]{1,0:T(8,128)(2,1)S(1)}, u32[]{:S(2)}, u32[]{:S(2)}) collective-permute-start(bf16[528,128]{1,0:T(8,128)(2,1)S(1)} %join.6.refs_0_), channel_id=1, source_target_pairs={{0,2},{1,3},{2,0},{3,1},{4,6},{5,7},{6,4},{7,5},{8,10},{9,11},{10,... | collective-permute-start | bytes 405512 | tf_op jit(solution)/shard_map/ppermute | solution.py:464
  39.5 9.3 %collective-permute-start.8 = (bf16[400,128]{1,0:T(8,128)(2,1)S(1)}, bf16[400,128]{1,0:T(8,128)(2,1)S(1)}, u32[]{:S(2)}, u32[]{:S(2)}) collective-permute-start(bf16[400,128]{1,0:T(8,128)(2,1)S(1)} %get-tuple-element.47), channel_id=1, source_target_pairs={{0,12},{4,8},{8,4},{12,0},{16,28},{20,24},{24,20},{28,16},{1,13},{... | collective-permute-start | bytes 307208 | tf_op jit(solution)/shard_map/ppermute | solution.py:464
  41.1 8.6 %collective-permute-start.9 = (bf16[400,128]{1,0:T(8,128)(2,1)S(1)}, bf16[400,128]{1,0:T(8,128)(2,1)S(1)}, u32[]{:S(2)}, u32[]{:S(2)}) collective-permute-start(bf16[400,128]{1,0:T(8,128)(2,1)S(1)} %get-tuple-element.48), channel_id=1, source_target_pairs={{0,28},{4,24},{8,20},{12,16},{16,12},{20,8},{24,4},{28,0},{1,29},{... | collective-permute-start | bytes 307208 | tf_op jit(solution)/shard_map/ppermute | solution.py:464
  43.1 6.5 %collective-permute-start.10 = (bf16[400,128]{1,0:T(8,128)(2,1)S(1)}, bf16[400,128]{1,0:T(8,128)(2,1)S(1)}, u32[]{:S(2)}, u32[]{:S(2)}) collective-permute-start(bf16[400,128]{1,0:T(8,128)(2,1)S(1)} %get-tuple-element.49), channel_id=1, source_target_pairs={{0,4},{4,0},{8,12},{12,8},{16,20},{20,16},{24,28},{28,24},{1,5},{5... | collective-permute-start | bytes 307208 | tf_op jit(solution)/shard_map/ppermute | solution.py:464
  44.3 6.7 %collective-permute-start.11 = (bf16[400,128]{1,0:T(8,128)(2,1)S(1)}, bf16[400,128]{1,0:T(8,128)(2,1)S(1)}, u32[]{:S(2)}, u32[]{:S(2)}) collective-permute-start(bf16[400,128]{1,0:T(8,128)(2,1)S(1)} %get-tuple-element.50), channel_id=1, source_target_pairs={{0,8},{4,12},{8,0},{12,4},{16,24},{20,28},{24,16},{28,20},{1,9},{5... | collective-permute-start | bytes 307208 | tf_op jit(solution)/shard_map/ppermute | solution.py:464
  47.0 5.8 %collective-permute-start.14 = (bf16[400,128]{1,0:T(8,128)(2,1)S(1)}, bf16[400,128]{1,0:T(8,128)(2,1)S(1)}, u32[]{:S(2)}, u32[]{:S(2)}) collective-permute-start(bf16[400,128]{1,0:T(8,128)(2,1)S(1)} %get-tuple-element.55), channel_id=1, source_target_pairs={{0,8},{4,12},{8,0},{12,4},{16,24},{20,28},{24,16},{28,20},{1,9},{5... | collective-permute-start | bytes 307208 | tf_op jit(solution)/shard_map/ppermute | solution.py:464
  48.7 4.7 %collective-permute-start.15 = (bf16[400,128]{1,0:T(8,128)(2,1)S(1)}, bf16[400,128]{1,0:T(8,128)(2,1)S(1)}, u32[]{:S(2)}, u32[]{:S(2)}) collective-permute-start(bf16[400,128]{1,0:T(8,128)(2,1)S(1)} %get-tuple-element.56), channel_id=1, source_target_pairs={{0,4},{4,0},{8,12},{12,8},{16,20},{20,16},{24,28},{28,24},{1,5},{5... | collective-permute-start | bytes 307208 | tf_op jit(solution)/shard_map/ppermute | solution.py:464

commit v10 on v9

--- a/solution.py
+++ b/solution.py
@@ -484,7 +484,7 @@
         late = []
         if direct:
             mirror = exchange(payload, "pairs", half)
-            flips = [0, *range(half - 1, 0, -1)]
+            flips = list(range(half))
             cores = [[o, o + 1] for o in range(0, orb_count, 2)]
             held = lax.all_gather(payload, "orb", axis=0, tiled=False)
             across = pair_count - 1

time: 54.9 us -> 54.8 us (level)
  no operation moved by 1% of the time
where the time goes in v10:
time: 54.8 us; the launch traced here: 54.6 us
  starting transfers between devices  23.6 us (43%)
  blocking collectives  18.6 us (34%)
  Pallas kernels  7.98 us (15%)
  waiting for transfers between devices  3.57 us (7%)
  between operations  0.81 us (1%)
    ppermute x16, starting transfers between devices, exchange(): lax.ppermute(block, axis, [(p, p ^ flip) for p in range(lax.axis_size(axi...  23.6 us
    all_gather x2, blocking collectives, body(): held = lax.all_gather(payload, 'orb', axis=0, tiled=False)  14.2 us
    all_gather x2, blocking collectives, body(): held = lax.all_gather(held, 'orb', axis=0, axis_index_groups=cores)  4.39 us
    ppermute x16, waiting for transfers between devices, exchange(): lax.ppermute(block, axis, [(p, p ^ flip) for p in range(lax.axis_size(axi...  3.57 us
    pallas_call x2, Pallas kernels, terms(): pl.pallas_call(functools.partial(terms_kernel, capacity, orbitals, every...  3.53 us
    pallas_call x2, Pallas kernels, body(): pl.pallas_call(functools.partial(update_kernel, last, capacity, orbitals,...  2.15 us
    pallas_call x1, Pallas kernels, body(): pl.pallas_call(functools.partial(setup_kernel, capacity, orbitals, near,...  1.57 us
  transfers between devices with their start and end apart: 16, of which 5 were waited for; matrix products, arithmetic and copies ran while one was open for 0% of the time, Pallas kernels for 8%

profile of v10, /device:TPU:0, one launch (start us, length us, event | category | flops | bytes accessed | tf_op | source)
XLA Modules:
  0.0 54.6 jit_solution(1738089889191040053)
XLA Ops:
  0.6 1.6 %setup.1 = (bf16[528,128]{1,0:T(8,128)(2,1)S(1)}, s32[8,128]{1,0:T(8,128)S(1)}, s32[4,128]{1,0:T(4,128)S(1)}, f32[4,128]{1,0:T(4,128)S(1)}) custom-call(s32[2,4]{1,0:T(2,128)} %bitcast.11, f32[4,128,128]{2,1,0:T(8,128)} %refs_4_.1, f32[4,128]{1,0:T(4,128)} %refs_7_.3, s32[16,128]{1,0:T(8,128)} %bitcast.14, s32[1,128]{1,0:T(1,128)} %bitcast.15, ...), custom_call_target="tpu_custom_call" | custom-call | tf_op jit(solution)/shard_map/setup/pallas_call | solution.py:378
  2.2 4.1 %collective-permute-start.4 = (bf16[528,128]{1,0:T(8,128)(2,1)S(1)}, bf16[528,128]{1,0:T(8,128)(2,1)S(1)}, u32[]{:S(2)}, u32[]{:S(2)}) collective-permute-start(bf16[528,128]{1,0:T(8,128)(2,1)S(1)} %get-tuple-element.33), channel_id=1, source_target_pairs={{0,16},{4,20},{8,24},{12,28},{16,0},{20,4},{24,8},{28,12},{1,17},{... | collective-permute-start | bytes 405512 | tf_op jit(solution)/shard_map/ppermute | solution.py:464
  6.3 7.2 %all-gather = bf16[2112,128]{1,0:T(8,128)(2,1)S(1)} all-gather(bf16[528,128]{1,0:T(8,128)(2,1)S(1)} %get-tuple-element.33), channel_id=2, replica_groups=mesh['pairs'=8,'orb'=4] {'orb'}, dimensions={0}, use_global_device_ids=true | all-gather | bytes 675840 | tf_op jit(solution)/shard_map/all_gather | solution.py:489
  13.8 0.9 %collective-permute-start.5 = (bf16[528,128]{1,0:T(8,128)(2,1)S(1)}, bf16[528,128]{1,0:T(8,128)(2,1)S(1)}, u32[]{:S(2)}, u32[]{:S(2)}) collective-permute-start(bf16[528,128]{1,0:T(8,128)(2,1)S(1)} %join.4.refs_0_), channel_id=1, source_target_pairs={{0,2},{1,3},{2,0},{3,1},{4,6},{5,7},{6,4},{7,5},{8,10},{9,11},{10,... | collective-permute-start | bytes 405512 | tf_op jit(solution)/shard_map/ppermute | solution.py:464
  14.7 2.5 %collective-permute-start = (bf16[400,128]{1,0:T(8,128)(2,1)S(1)}, bf16[400,128]{1,0:T(8,128)(2,1)S(1)}, u32[]{:S(2)}, u32[]{:S(2)}) collective-permute-start(bf16[400,128]{1,0:T(8,128)(2,1)S(1)} %get-tuple-element.35), channel_id=1, source_target_pairs={{0,12},{4,8},{8,4},{12,0},{16,28},{20,24},{24,20},{28,16},{1,13},{... | collective-permute-start | bytes 307208 | tf_op jit(solution)/shard_map/ppermute | solution.py:464
  17.2 1.7 %collective-permute-start.1 = (bf16[400,128]{1,0:T(8,128)(2,1)S(1)}, bf16[400,128]{1,0:T(8,128)(2,1)S(1)}, u32[]{:S(2)}, u32[]{:S(2)}) collective-permute-start(bf16[400,128]{1,0:T(8,128)(2,1)S(1)} %get-tuple-element.36), channel_id=1, source_target_pairs={{0,28},{4,24},{8,20},{12,16},{16,12},{20,8},{24,4},{28,0},{1,29},{... | collective-permute-start | bytes 307208 | tf_op jit(solution)/shard_map/ppermute | solution.py:464
  19.4 2.1 %collective-permute-start.3 = (bf16[400,128]{1,0:T(8,128)(2,1)S(1)}, bf16[400,128]{1,0:T(8,128)(2,1)S(1)}, u32[]{:S(2)}, u32[]{:S(2)}) collective-permute-start(bf16[400,128]{1,0:T(8,128)(2,1)S(1)} %get-tuple-element.38), channel_id=1, source_target_pairs={{0,8},{4,12},{8,0},{12,4},{16,24},{20,28},{24,16},{28,20},{1,9},{5... | collective-permute-start | bytes 307208 | tf_op jit(solution)/shard_map/ppermute | solution.py:464
  21.5 2.2 %all-gather.1 = bf16[4,528,128]{2,1,0:T(8,128)(2,1)S(1)} all-gather(bf16[2,528,128]{2,1,0:T(8,128)(2,1)S(1)} %join.5), channel_id=3, replica_groups={{0,1},{2,3},{4,5},{6,7},{8,9},{10,11},{12,13},{14,15},{16,17},{18,19},{..., dimensions={0}, use_global_device_ids=true | all-gather | bytes 811008 | tf_op jit(solution)/shard_map/all_gather | solution.py:496
  24.4 1.0 %collective-permute-start.7 = (bf16[400,128]{1,0:T(8,128)(2,1)S(1)}, bf16[400,128]{1,0:T(8,128)(2,1)S(1)}, u32[]{:S(2)}, u32[]{:S(2)}) collective-permute-start(bf16[400,128]{1,0:T(8,128)(2,1)S(1)} %get-tuple-element.44), channel_id=1, source_target_pairs={{0,8},{4,12},{8,0},{12,4},{16,24},{20,28},{24,16},{28,20},{1,9},{5... | collective-permute-start | bytes 307208 | tf_op jit(solution)/shard_map/ppermute | solution.py:464
  25.7 1.8 %terms.2 = (f32[520,128]{1,0:T(8,128)S(1)}, bf16[4,128,768]{2,1,0:T(8,128)(2,1)S(1)}, f32[4,768]{1,0:T(4,128)S(1)}) custom-call(s32[4,128]{1,0:T(4,128)S(1)} %get-tuple-element.30.index, f32[4,128]{1,0:T(4,128)S(1)} %get-tuple-element.31.coefficients, bf16[4,16,128,128]{3,2,1,0:T(8,128)(2,1)S(1)} %copy-done.5, ...), custom_call_target="tpu_custom_call" | custom-call | flops 20000000000 | tf_op jit(solution)/shard_map/terms/pallas_call | solution.py:471
  27.5 1.3 %collective-permute-done.6.refs_2_ = bf16[400,128]{1,0:T(8,128)(2,1)S(1)} collective-permute-done((bf16[400,128]{1,0:T(8,128)(2,1)S(1)}, bf16[400,128]{1,0:T(8,128)(2,1)S(1)}, u32[]{:S(2)}, u32[]{:S(2)}) %collective-permute-start.6) | collective-permute-done | bytes 102432 | tf_op jit(solution)/shard_map/ppermute | solution.py:464
  29.1 0.8 %update.2 = (f32[4,128,128]{2,1,0:T(8,128)S(1)}, bf16[528,128]{1,0:T(8,128)(2,1)S(1)}) custom-call(s32[2,4]{1,0:T(2,128)S(1)} %bitcast.12, f32[520,128]{1,0:T(8,128)S(1)} %get-tuple-element.40.before, bf16[4,128,768]{2,1,0:T(8,128)(2,1)S(1)} %get-tuple-element.41.refs_0_, f32[4,768]{1,0:T(4,128)S(1)} %get-tuple-element.42.refs_1_, ...), custom_call_target="tpu_custom_call" | custom-call | tf_op jit(solution)/shard_map/update/pallas_call | solution.py:508
  29.9 1.7 %collective-permute-start.12 = (bf16[528,128]{1,0:T(8,128)(2,1)S(1)}, bf16[528,128]{1,0:T(8,128)(2,1)S(1)}, u32[]{:S(2)}, u32[]{:S(2)}) collective-permute-start(bf16[528,128]{1,0:T(8,128)(2,1)S(1)} %get-tuple-element.45), channel_id=1, source_target_pairs={{0,16},{4,20},{8,24},{12,28},{16,0},{20,4},{24,8},{28,12},{1,17},{... | collective-permute-start | bytes 405512 | tf_op jit(solution)/shard_map/ppermute | solution.py:464
  31.5 7.0 %all-gather.2 = bf16[2112,128]{1,0:T(8,128)(2,1)S(1)} all-gather(bf16[528,128]{1,0:T(8,128)(2,1)S(1)} %get-tuple-element.45), channel_id=4, replica_groups=mesh['pairs'=8,'orb'=4] {'orb'}, dimensions={0}, use_global_device_ids=true | all-gather | bytes 675840 | tf_op jit(solution)/shard_map/all_gather | solution.py:489
  38.7 0.9 %collective-permute-start.13 = (bf16[528,128]{1,0:T(8,128)(2,1)S(1)}, bf16[528,128]{1,0:T(8,128)(2,1)S(1)}, u32[]{:S(2)}, u32[]{:S(2)}) collective-permute-start(bf16[528,128]{1,0:T(8,128)(2,1)S(1)} %join.6.refs_0_), channel_id=1, source_target_pairs={{0,2},{1,3},{2,0},{3,1},{4,6},{5,7},{6,4},{7,5},{8,10},{9,11},{10,... | collective-permute-start | bytes 405512 | tf_op jit(solution)/shard_map/ppermute | solution.py:464
  39.6 1.2 %collective-permute-start.8 = (bf16[400,128]{1,0:T(8,128)(2,1)S(1)}, bf16[400,128]{1,0:T(8,128)(2,1)S(1)}, u32[]{:S(2)}, u32[]{:S(2)}) collective-permute-start(bf16[400,128]{1,0:T(8,128)(2,1)S(1)} %get-tuple-element.47), channel_id=1, source_target_pairs={{0,12},{4,8},{8,4},{12,0},{16,28},{20,24},{24,20},{28,16},{1,13},{... | collective-permute-start | bytes 307208 | tf_op jit(solution)/shard_map/ppermute | solution.py:464
  40.8 2.5 %collective-permute-start.9 = (bf16[400,128]{1,0:T(8,128)(2,1)S(1)}, bf16[400,128]{1,0:T(8,128)(2,1)S(1)}, u32[]{:S(2)}, u32[]{:S(2)}) collective-permute-start(bf16[400,128]{1,0:T(8,128)(2,1)S(1)} %get-tuple-element.48), channel_id=1, source_target_pairs={{0,28},{4,24},{8,20},{12,16},{16,12},{20,8},{24,4},{28,0},{1,29},{... | collective-permute-start | bytes 307208 | tf_op jit(solution)/shard_map/ppermute | solution.py:464
  43.3 1.5 %collective-permute-start.10 = (bf16[400,128]{1,0:T(8,128)(2,1)S(1)}, bf16[400,128]{1,0:T(8,128)(2,1)S(1)}, u32[]{:S(2)}, u32[]{:S(2)}) collective-permute-start(bf16[400,128]{1,0:T(8,128)(2,1)S(1)} %get-tuple-element.49), channel_id=1, source_target_pairs={{0,4},{4,0},{8,12},{12,8},{16,20},{20,16},{24,28},{28,24},{1,5},{5... | collective-permute-start | bytes 307208 | tf_op jit(solution)/shard_map/ppermute | solution.py:464
  44.8 2.2 %all-gather.3 = bf16[4,528,128]{2,1,0:T(8,128)(2,1)S(1)} all-gather(bf16[2,528,128]{2,1,0:T(8,128)(2,1)S(1)} %join.7), channel_id=5, replica_groups={{0,1},{2,3},{4,5},{6,7},{8,9},{10,11},{12,13},{14,15},{16,17},{18,19},{..., dimensions={0}, use_global_device_ids=true | all-gather | bytes 811008 | tf_op jit(solution)/shard_map/all_gather | solution.py:496
  47.2 1.4 %collective-permute-start.14 = (bf16[400,128]{1,0:T(8,128)(2,1)S(1)}, bf16[400,128]{1,0:T(8,128)(2,1)S(1)}, u32[]{:S(2)}, u32[]{:S(2)}) collective-permute-start(bf16[400,128]{1,0:T(8,128)(2,1)S(1)} %get-tuple-element.55), channel_id=1, source_target_pairs={{0,4},{4,0},{8,12},{12,8},{16,20},{20,16},{24,28},{28,24},{1,5},{5... | collective-permute-start | bytes 307208 | tf_op jit(solution)/shard_map/ppermute | solution.py:464
  48.6 1.2 %collective-permute-start.15 = (bf16[400,128]{1,0:T(8,128)(2,1)S(1)}, bf16[400,128]{1,0:T(8,128)(2,1)S(1)}, u32[]{:S(2)}, u32[]{:S(2)}) collective-permute-start(bf16[400,128]{1,0:T(8,128)(2,1)S(1)} %get-tuple-element.56), channel_id=1, source_target_pairs={{0,8},{4,12},{8,0},{12,4},{16,24},{20,28},{24,16},{28,20},{1,9},{5... | collective-permute-start | bytes 307208 | tf_op jit(solution)/shard_map/ppermute | solution.py:464
  50.4 1.8 %terms.3 = (f32[520,128]{1,0:T(8,128)S(1)}, bf16[4,128,768]{2,1,0:T(8,128)(2,1)S(1)}, f32[4,768]{1,0:T(4,128)S(1)}) custom-call(s32[4,128]{1,0:T(4,128)S(1)} %get-tuple-element.30.index, f32[4,128]{1,0:T(4,128)S(1)} %get-tuple-element.31.coefficients, bf16[4,16,128,128]{3,2,1,0:T(8,128)(2,1)S(1)} %copy-done.5, ...), custom_call_target="tpu_custom_call" | custom-call | flops 20000000000 | tf_op jit(solution)/shard_map/terms/pallas_call | solution.py:471
  52.2 1.1 %collective-permute-done.15.refs_3_ = bf16[400,128]{1,0:T(8,128)(2,1)S(1)} collective-permute-done((bf16[400,128]{1,0:T(8,128)(2,1)S(1)}, bf16[400,128]{1,0:T(8,128)(2,1)S(1)}, u32[]{:S(2)}, u32[]{:S(2)}) %collective-permute-start.15) | collective-permute-done | bytes 102432 | tf_op jit(solution)/shard_map/ppermute | solution.py:464
  53.3 1.4 %update.3 = (f32[4,128,128]{2,1,0:T(8,128)}, f32[4,128,128]{2,1,0:T(8,128)}) custom-call(s32[2,4]{1,0:T(2,128)S(1)} %bitcast.13, f32[520,128]{1,0:T(8,128)S(1)} %get-tuple-element.52.before, bf16[4,128,768]{2,1,0:T(8,128)(2,1)S(1)} %get-tuple-element.53.refs_0_, f32[4,768]{1,0:T(4,128)S(1)} %get-tuple-element.54.refs_1_, ...), custom_call_target="tpu_custom_call" | custom-call | tf_op jit(solution)/shard_map/update/pallas_call | solution.py:508
  (37 shorter events, 3.1 us)
Async XLA Ops:
  0.6 25.1 %copy-start.5 = (bf16[4,16,128,128]{3,2,1,0:T(8,128)(2,1)S(1)}, bf16[4,16,128,128]{3,2,1,0:T(8,128)(2,1)}, u32[]{:S(2)}) copy-start(bf16[4,16,128,128]{3,2,1,0:T(8,128)(2,1)} %intersections.3) | copy-start | bytes 6291460
  2.2 11.5 %collective-permute-start.4 = (bf16[528,128]{1,0:T(8,128)(2,1)S(1)}, bf16[528,128]{1,0:T(8,128)(2,1)S(1)}, u32[]{:S(2)}, u32[]{:S(2)}) collective-permute-start(bf16[528,128]{1,0:T(8,128)(2,1)S(1)} %get-tuple-element.33), channel_id=1, source_target_pairs={{0,16},{4,20},{8,24},{12,28},{16,0},{20,4},{24,8},{28,12},{1,17},{... | collective-permute-start | bytes 405512 | tf_op jit(solution)/shard_map/ppermute | solution.py:464
  13.8 7.7 %collective-permute-start.5 = (bf16[528,128]{1,0:T(8,128)(2,1)S(1)}, bf16[528,128]{1,0:T(8,128)(2,1)S(1)}, u32[]{:S(2)}, u32[]{:S(2)}) collective-permute-start(bf16[528,128]{1,0:T(8,128)(2,1)S(1)} %join.4.refs_0_), channel_id=1, source_target_pairs={{0,2},{1,3},{2,0},{3,1},{4,6},{5,7},{6,4},{7,5},{8,10},{9,11},{10,... | collective-permute-start | bytes 405512 | tf_op jit(solution)/shard_map/ppermute | solution.py:464
  14.7 9.7 %collective-permute-start = (bf16[400,128]{1,0:T(8,128)(2,1)S(1)}, bf16[400,128]{1,0:T(8,128)(2,1)S(1)}, u32[]{:S(2)}, u32[]{:S(2)}) collective-permute-start(bf16[400,128]{1,0:T(8,128)(2,1)S(1)} %get-tuple-element.35), channel_id=1, source_target_pairs={{0,12},{4,8},{8,4},{12,0},{16,28},{20,24},{24,20},{28,16},{1,13},{... | collective-permute-start | bytes 307208 | tf_op jit(solution)/shard_map/ppermute | solution.py:464
  17.2 8.4 %collective-permute-start.1 = (bf16[400,128]{1,0:T(8,128)(2,1)S(1)}, bf16[400,128]{1,0:T(8,128)(2,1)S(1)}, u32[]{:S(2)}, u32[]{:S(2)}) collective-permute-start(bf16[400,128]{1,0:T(8,128)(2,1)S(1)} %get-tuple-element.36), channel_id=1, source_target_pairs={{0,28},{4,24},{8,20},{12,16},{16,12},{20,8},{24,4},{28,0},{1,29},{... | collective-permute-start | bytes 307208 | tf_op jit(solution)/shard_map/ppermute | solution.py:464
  18.9 6.8 %collective-permute-start.2 = (bf16[400,128]{1,0:T(8,128)(2,1)S(1)}, bf16[400,128]{1,0:T(8,128)(2,1)S(1)}, u32[]{:S(2)}, u32[]{:S(2)}) collective-permute-start(bf16[400,128]{1,0:T(8,128)(2,1)S(1)} %get-tuple-element.37), channel_id=1, source_target_pairs={{0,4},{4,0},{8,12},{12,8},{16,20},{20,16},{24,28},{28,24},{1,5},{5... | collective-permute-start | bytes 307208 | tf_op jit(solution)/shard_map/ppermute | solution.py:464
  19.4 6.3 %collective-permute-start.3 = (bf16[400,128]{1,0:T(8,128)(2,1)S(1)}, bf16[400,128]{1,0:T(8,128)(2,1)S(1)}, u32[]{:S(2)}, u32[]{:S(2)}) collective-permute-start(bf16[400,128]{1,0:T(8,128)(2,1)S(1)} %get-tuple-element.38), channel_id=1, source_target_pairs={{0,8},{4,12},{8,0},{12,4},{16,24},{20,28},{24,16},{28,20},{1,9},{5... | collective-permute-start | bytes 307208 | tf_op jit(solution)/shard_map/ppermute | solution.py:464
  23.8 5.0 %collective-permute-start.6 = (bf16[400,128]{1,0:T(8,128)(2,1)S(1)}, bf16[400,128]{1,0:T(8,128)(2,1)S(1)}, u32[]{:S(2)}, u32[]{:S(2)}) collective-permute-start(bf16[400,128]{1,0:T(8,128)(2,1)S(1)} %get-tuple-element.43), channel_id=1, source_target_pairs={{0,4},{4,0},{8,12},{12,8},{16,20},{20,16},{24,28},{28,24},{1,5},{5... | collective-permute-start | bytes 307208 | tf_op jit(solution)/shard_map/ppermute | solution.py:464
  24.4 4.7 %collective-permute-start.7 = (bf16[400,128]{1,0:T(8,128)(2,1)S(1)}, bf16[400,128]{1,0:T(8,128)(2,1)S(1)}, u32[]{:S(2)}, u32[]{:S(2)}) collective-permute-start(bf16[400,128]{1,0:T(8,128)(2,1)S(1)} %get-tuple-element.44), channel_id=1, source_target_pairs={{0,8},{4,12},{8,0},{12,4},{16,24},{20,28},{24,16},{28,20},{1,9},{5... | collective-permute-start | bytes 307208 | tf_op jit(solution)/shard_map/ppermute | solution.py:464
  25.7 3.4 %copy-start = (f32[4,128,128]{2,1,0:T(8,128)S(1)}, f32[4,128,128]{2,1,0:T(8,128)}, u32[]{:S(2)}) copy-start(f32[4,128,128]{2,1,0:T(8,128)} %refs_4_.1) | copy-start | bytes 786436
  25.7 3.4 %copy-start.1 = (bf16[4,128,128]{2,1,0:T(8,128)(2,1)S(1)}, bf16[4,128,128]{2,1,0:T(8,128)(2,1)}, u32[]{:S(2)}) copy-start(bf16[4,128,128]{2,1,0:T(8,128)(2,1)} %refs_5_.3) | copy-start | bytes 393220
  25.7 3.4 %copy-start.2 = (f32[4,128]{1,0:T(4,128)S(1)}, f32[4,128]{1,0:T(4,128)}, u32[]{:S(2)}) copy-start(f32[4,128]{1,0:T(4,128)} %refs_7_.3) | copy-start | bytes 6148
  25.7 3.4 %copy-start.3 = (s32[4,2]{0,1:T(2,128)S(1)}, s32[4,2]{0,1:T(2,128)}, u32[]{:S(2)}) copy-start(s32[4,2]{0,1:T(2,128)} %param.15) | copy-start | bytes 100
  25.7 3.4 %copy-start.4 = (f32[4,128]{1,0:T(4,128)S(1)}, f32[4,128]{1,0:T(4,128)}, u32[]{:S(2)}) copy-start(f32[4,128]{1,0:T(4,128)} %refs_6_.3) | copy-start | bytes 6148
  29.9 8.8 %collective-permute-start.12 = (bf16[528,128]{1,0:T(8,128)(2,1)S(1)}, bf16[528,128]{1,0:T(8,128)(2,1)S(1)}, u32[]{:S(2)}, u32[]{:S(2)}) collective-permute-start(bf16[528,128]{1,0:T(8,128)(2,1)S(1)} %get-tuple-element.45), channel_id=1, source_target_pairs={{0,16},{4,20},{8,24},{12,28},{16,0},{20,4},{24,8},{28,12},{1,17},{... | collective-permute-start | bytes 405512 | tf_op jit(solution)/shard_map/ppermute | solution.py:464
  38.7 6.1 %collective-permute-start.13 = (bf16[528,128]{1,0:T(8,128)(2,1)S(1)}, bf16[528,128]{1,0:T(8,128)(2,1)S(1)}, u32[]{:S(2)}, u32[]{:S(2)}) collective-permute-start(bf16[528,128]{1,0:T(8,128)(2,1)S(1)} %join.6.refs_0_), channel_id=1, source_target_pairs={{0,2},{1,3},{2,0},{3,1},{4,6},{5,7},{6,4},{7,5},{8,10},{9,11},{10,... | collective-permute-start | bytes 405512 | tf_op jit(solution)/shard_map/ppermute | solution.py:464
  39.6 9.0 %collective-permute-start.8 = (bf16[400,128]{1,0:T(8,128)(2,1)S(1)}, bf16[400,128]{1,0:T(8,128)(2,1)S(1)}, u32[]{:S(2)}, u32[]{:S(2)}) collective-permute-start(bf16[400,128]{1,0:T(8,128)(2,1)S(1)} %get-tuple-element.47), channel_id=1, source_target_pairs={{0,12},{4,8},{8,4},{12,0},{16,28},{20,24},{24,20},{28,16},{1,13},{... | collective-permute-start | bytes 307208 | tf_op jit(solution)/shard_map/ppermute | solution.py:464
  40.8 9.0 %collective-permute-start.9 = (bf16[400,128]{1,0:T(8,128)(2,1)S(1)}, bf16[400,128]{1,0:T(8,128)(2,1)S(1)}, u32[]{:S(2)}, u32[]{:S(2)}) collective-permute-start(bf16[400,128]{1,0:T(8,128)(2,1)S(1)} %get-tuple-element.48), channel_id=1, source_target_pairs={{0,28},{4,24},{8,20},{12,16},{16,12},{20,8},{24,4},{28,0},{1,29},{... | collective-permute-start | bytes 307208 | tf_op jit(solution)/shard_map/ppermute | solution.py:464
  43.3 6.5 %collective-permute-start.10 = (bf16[400,128]{1,0:T(8,128)(2,1)S(1)}, bf16[400,128]{1,0:T(8,128)(2,1)S(1)}, u32[]{:S(2)}, u32[]{:S(2)}) collective-permute-start(bf16[400,128]{1,0:T(8,128)(2,1)S(1)} %get-tuple-element.49), channel_id=1, source_target_pairs={{0,4},{4,0},{8,12},{12,8},{16,20},{20,16},{24,28},{28,24},{1,5},{5... | collective-permute-start | bytes 307208 | tf_op jit(solution)/shard_map/ppermute | solution.py:464
  44.8 5.6 %collective-permute-start.11 = (bf16[400,128]{1,0:T(8,128)(2,1)S(1)}, bf16[400,128]{1,0:T(8,128)(2,1)S(1)}, u32[]{:S(2)}, u32[]{:S(2)}) collective-permute-start(bf16[400,128]{1,0:T(8,128)(2,1)S(1)} %get-tuple-element.50), channel_id=1, source_target_pairs={{0,8},{4,12},{8,0},{12,4},{16,24},{20,28},{24,16},{28,20},{1,9},{5... | collective-permute-start | bytes 307208 | tf_op jit(solution)/shard_map/ppermute | solution.py:464
  47.2 5.0 %collective-permute-start.14 = (bf16[400,128]{1,0:T(8,128)(2,1)S(1)}, bf16[400,128]{1,0:T(8,128)(2,1)S(1)}, u32[]{:S(2)}, u32[]{:S(2)}) collective-permute-start(bf16[400,128]{1,0:T(8,128)(2,1)S(1)} %get-tuple-element.55), channel_id=1, source_target_pairs={{0,4},{4,0},{8,12},{12,8},{16,20},{20,16},{24,28},{28,24},{1,5},{5... | collective-permute-start | bytes 307208 | tf_op jit(solution)/shard_map/ppermute | solution.py:464
  48.6 4.7 %collective-permute-start.15 = (bf16[400,128]{1,0:T(8,128)(2,1)S(1)}, bf16[400,128]{1,0:T(8,128)(2,1)S(1)}, u32[]{:S(2)}, u32[]{:S(2)}) collective-permute-start(bf16[400,128]{1,0:T(8,128)(2,1)S(1)} %get-tuple-element.56), channel_id=1, source_target_pairs={{0,8},{4,12},{8,0},{12,4},{16,24},{20,28},{24,16},{28,20},{1,9},{5... | collective-permute-start | bytes 307208 | tf_op jit(solution)/shard_map/ppermute | solution.py:464
